TPU v7x, 32 devices: a whole 2x2x4 slice. The times are simulated.
32 devices in a mesh: group: 2 (over x), tile: 16 (over z, y, core).
Axes of the slice: x: 2, y: 2, z: 4, core: 2. Of those that a mesh axis runs over, the one named last changes fastest.
Arguments:
- object_field: float32 [4, 2, 2048, 2048], P('group', None, 'tile'), parts along dimension 0, may hold values from -6 to 6
- probe: float32 [2, 256, 256], replicated, may hold values from -6 to 6
- measured: bfloat16 [64, 256, 256], P(('group', 'tile')), parts along dimension 0, may hold values from 0.099609375 to 3
- frame_table: int32 [64, 3], P(('group', 'tile')), parts along dimension 0, may hold values from 0 to 1792, as said below
- frame_count: int32 [32], P(('group', 'tile')), parts along dimension 0, may hold values from 0 to 2, as said below
Outputs:
- updated_object: float32 [4, 2, 2048, 2048], P('group', None, 'tile'), parts along dimension 0
- phase_map: float32 [4, 2048, 2048], P('group', 'tile'), parts along dimension 0
There are 2 independent parts, one for each index of `group`. A program takes and returns all parts, laid end to end along the dimension named above; an argument that names none is the same for every part. Nothing has to cross between parts.
Inputs may be any that keep to these rules, and one draw needn't show every extreme that they name: `frame_table`: per slot: the row offset is below 128, and the frame's rows d * 128 + offset to that plus 256 - 1 and columns lie inside the projection; the angle is below 2. Only the first frame_count[d] slots of device d are live. `frame_count`: exactly 2 on some device in every draw; zero on every device d with d * 128 > 1792.
All inputs are finite; a program needn't handle non-finite values.
Results may differ from a plain program's by a relative error of at most 0.0009.
Values may be sent and summed in bfloat16 or wider, within the bound.
No kernel may reach another device: no remote copies, remote signals or barrier semaphores. Data moves between devices by JAX's collectives and lax.ppermute only.
A program may use at most 192 MiB of HBM per device.

v0:
```python
import math

import jax
import jax.numpy as jnp
from jax import lax
from jax.sharding import PartitionSpec as P

magnitude_floor = 0.5
soften_term = 0.5
screen_term = 0.0001
epsilon_term = 1e-06
exact_mode = lax.Precision.HIGHEST


def passed_along(x, axis, by):
    size = lax.axis_size(axis)
    pairs = [(i, i + by) for i in range(size) if 0 <= i + by < size]
    return lax.ppermute(x, axis, pairs)


def padded_2(cells, sides, width):
    for axis, dim in sides:
        count = lax.axis_size(axis)
        ends = count - 1
        head = lax.slice_in_dim(cells, 0, width, axis=dim)
        tail = lax.slice_in_dim(cells, cells.shape[dim] - width, cells.shape[dim], axis=dim)
        cells = jnp.concatenate(
            [
                lax.ppermute(tail, axis, [(i, (i + 1) % count) for i in range(ends)]),
                cells,
                lax.ppermute(head, axis, [((i + 1) % count, i) for i in range(ends)]),
            ],
            axis=dim,
        )
    return cells


def fourier_tables(frame_side):
    indices = jnp.arange(frame_side, dtype=jnp.int32)
    products = indices[:, None] * indices[None, :] % frame_side
    phases = products.astype(jnp.float32) * (-2.0 * math.pi / frame_side)
    norm_scale = 1.0 / math.sqrt(frame_side)
    return (
        (jnp.cos(phases) * norm_scale).astype(jnp.bfloat16),
        (jnp.sin(phases) * norm_scale).astype(jnp.bfloat16),
    )


def complex_left(table_re, table_im, operand):
    side = table_re.shape[0]
    stacked = jnp.concatenate([table_re, table_im], 0)
    joined = jnp.concatenate([operand[0], operand[1]], 1)
    products = jnp.dot(stacked, joined, preferred_element_type=jnp.float32)
    return jnp.stack(
        [
            products[:side, :side] - products[side:, side:],
            products[:side, side:] + products[side:, :side],
        ]
    )


def complex_right(operand, table_re, table_im):
    side = table_re.shape[0]
    stacked = jnp.concatenate([operand[0], operand[1]], 0)
    joined = jnp.concatenate([table_re, table_im], 1)
    products = jnp.dot(stacked, joined, preferred_element_type=jnp.float32)
    return jnp.stack(
        [
            products[:side, :side] - products[side:, side:],
            products[:side, side:] + products[side:, :side],
        ]
    )


def correct_frame(exit_field, magnitude, fourier):
    cos_part, sin_part = fourier
    half_spectrum = complex_left(cos_part, sin_part, exit_field).astype(jnp.bfloat16)
    spectrum = complex_right(half_spectrum, cos_part, sin_part)
    amplitude = jnp.sqrt(spectrum[0] * spectrum[0] + spectrum[1] * spectrum[1])
    factor = magnitude.astype(jnp.float32) / jnp.maximum(amplitude, magnitude_floor) - 1.0
    change = (spectrum * factor[None]).astype(jnp.bfloat16)
    half_back = complex_left(cos_part, -sin_part, change).astype(jnp.bfloat16)
    return complex_right(half_back, cos_part, -sin_part)


def exit_wave(probe, patch):
    object_part = patch.astype(jnp.float32)
    real_part = probe[0] * object_part[0] - probe[1] * object_part[1]
    imag_part = probe[0] * object_part[1] + probe[1] * object_part[0]
    return jnp.stack([real_part, imag_part]).astype(jnp.bfloat16)


def object_step(probe, correction, probe_peak):
    real_part = (probe[0] * correction[0] + probe[1] * correction[1]) / probe_peak
    imag_part = (probe[0] * correction[1] - probe[1] * correction[0]) / probe_peak
    return jnp.stack([real_part, imag_part])


def phase_bond(first_cell, second_cell):
    cross_term = first_cell[:, 0] * second_cell[:, 1] - first_cell[:, 1] * second_cell[:, 0]
    power_sum = (
        first_cell[:, 0] ** 2
        + first_cell[:, 1] ** 2
        + second_cell[:, 0] ** 2
        + second_cell[:, 1] ** 2
        + soften_term
    )
    return 2.0 * cross_term / power_sum


def cosine_rows(first_freq, block_rows, grid_side):
    freqs = first_freq + jnp.arange(block_rows, dtype=jnp.int32)
    pixels = jnp.arange(grid_side, dtype=jnp.int32)
    phases = (2 * pixels[None, :] + 1) * freqs[:, None] % (4 * grid_side)
    norm_scale = jnp.where(freqs == 0, math.sqrt(1.0 / grid_side), math.sqrt(2.0 / grid_side))
    return norm_scale[:, None] * jnp.cos(phases.astype(jnp.float32) * (math.pi / grid_side / 2.0))


def eigen_values(freqs, grid_side):
    return 2.0 - 2.0 * jnp.cos(freqs.astype(jnp.float32) * (math.pi / grid_side))


def body(object_field, probe, measured, frame_table, frame_count):
    angles, _, strip_rows, grid_side = object_field.shape
    frame_side = probe.shape[1]
    reach_count = frame_side // strip_rows
    live_count = frame_count[0]
    fourier = fourier_tables(frame_side)
    probe_peak = jnp.max(probe[0] * probe[0] + probe[1] * probe[1]) + epsilon_term
    anchor = jnp.zeros((), jnp.int32)
    own_strip = object_field.astype(jnp.bfloat16)
    growth = []
    window = own_strip
    covered = 1
    while covered < reach_count + 1:
        adding = min(covered, reach_count + 1 - covered)
        arrived = passed_along(window[:, :, : adding * strip_rows], "tile", -covered)
        window = jnp.concatenate([window, arrived], 2)
        growth.append((covered, adding))
        covered = covered + adding

    def extract(record):
        row_offset, column, angle_id = record
        patch = lax.dynamic_slice(
            window, (angle_id, anchor, row_offset, column), (1, 2, frame_side, frame_side)
        )[0]
        return exit_wave(probe, patch)

    patches = lax.map(extract, (frame_table[:, 0], frame_table[:, 1], frame_table[:, 2]))
    corrections = jax.vmap(
        lambda exit_field, magnitude: correct_frame(exit_field, magnitude, fourier)
    )(patches, measured)

    def deposit(slot_index, deposits):
        record = frame_table[slot_index]
        correction = lax.dynamic_index_in_dim(corrections, slot_index, 0, keepdims=False)
        update = object_step(probe, correction, probe_peak)
        corner = (record[2], anchor, record[0], record[1])
        current = lax.dynamic_slice(deposits, corner, (1, 2, frame_side, frame_side))
        return lax.dynamic_update_slice(deposits, current + update[None], corner)

    deposits = lax.fori_loop(0, live_count, deposit, jnp.zeros(window.shape, jnp.float32))
    for covered, adding in reversed(growth):
        piece = deposits[:, :, covered * strip_rows : (covered + adding) * strip_rows]
        arrived = passed_along(piece.astype(jnp.bfloat16), "tile", covered).astype(piece.dtype)
        deposits = jnp.concatenate(
            [
                deposits[:, :, : adding * strip_rows] + arrived,
                deposits[:, :, adding * strip_rows : covered * strip_rows],
            ],
            2,
        )
    updated_object = object_field + deposits
    extended = padded_2(updated_object, (("tile", 2),), 1)
    padded = jnp.pad(extended, ((0, 0), (0, 0), (0, 0), (1, 1)))
    row_grad = phase_bond(padded[:, :, :-1, 1:-1], padded[:, :, 1:, 1:-1])
    col_grad = phase_bond(padded[:, :, 1:-1, :-1], padded[:, :, 1:-1, 1:])
    source = -(row_grad[:, 1:] - row_grad[:, :-1] + col_grad[:, :, 1:] - col_grad[:, :, :-1])
    block_rows = min(512, grid_side)
    column_coeffs = jnp.concatenate(
        [
            jnp.einsum(
                "arn,kn->ark",
                source,
                cosine_rows(first_freq, block_rows, grid_side),
                precision=exact_mode,
            )
            for first_freq in range(0, grid_side, block_rows)
        ],
        2,
    )
    pencil = lax.all_to_all(column_coeffs, "tile", split_axis=2, concat_axis=1, tiled=True)
    width_here = pencil.shape[2]
    col_ids = lax.axis_index("tile") * width_here + jnp.arange(width_here, dtype=jnp.int32)
    col_eigen = eigen_values(col_ids, grid_side)
    solved = jnp.zeros(pencil.shape, jnp.float32)
    for solve_first_freq in range(0, grid_side, block_rows):
        solve_cos_block = cosine_rows(solve_first_freq, block_rows, grid_side)
        partial_value = jnp.einsum("ki,aij->akj", solve_cos_block, pencil, precision=exact_mode)
        row_eigen = eigen_values(
            solve_first_freq + jnp.arange(block_rows, dtype=jnp.int32), grid_side
        )
        partial_value = partial_value / (
            screen_term + row_eigen[None, :, None] + col_eigen[None, None, :]
        )
        solved = solved + jnp.einsum(
            "ki,akj->aij", solve_cos_block, partial_value, precision=exact_mode
        )
    row_solved = lax.all_to_all(solved, "tile", split_axis=1, concat_axis=2, tiled=True)
    phase_map = jnp.zeros(source.shape, jnp.float32)
    for first_freq in range(0, grid_side, block_rows):
        cos_block = cosine_rows(first_freq, block_rows, grid_side)
        phase_map = phase_map + jnp.einsum(
            "ark,kn->arn",
            row_solved[:, :, first_freq : first_freq + block_rows],
            cos_block,
            precision=exact_mode,
        )
    return (updated_object, phase_map)


def solution(mesh):
    return jax.shard_map(
        body,
        mesh=mesh,
        in_specs=(
            P("group", None, "tile", None),
            P(),
            P(("group", "tile"), None, None),
            P(("group", "tile"), None),
            P(("group", "tile")),
        ),
        out_specs=(P("group", None, "tile", None), P("group", "tile", None)),
        check_vma=False,
    )
```

profile of v0, /device:TPU:0, one launch (start us, length us, event | category | flops | bytes accessed | tf_op | source)
XLA Modules:
  0.0 669.9 jit_solution(14193901196056568718)
XLA Ops:
  0.7 2.6 convert_element_type.153
  3.2 1.3 collective-permute-start
  4.5 1.3 collective-permute-start.1
  6.0 0.7 add_reduce_fusion
  7.6 1.0 fusion.271
  8.6 1.1 multiply_convert_fusion
  9.8 67.4 %collective-permute-done.1 = bf16[2,2,128,2048]{3,2,1,0:T(8,128)(2,1)} collective-permute-done((bf16[2,2,128,2048]{3,2,1,0:T(8,128)(2,1)S(1)}, bf16[2,2,128,2048]{3,2,1,0:T(8,128)(2,1)}, u32[]{:S(2)}, u32[]{:S(2)}) %collective-permute-start.1) | collective-permute-done | bytes 2097184 | tf_op jit(solution)/shard_map/ppermute | solution.py:18
  77.2 5.4 pad_maximum_fusion
  82.6 17.7 %while.20 = (s32[]{:T(128)}, bf16[2,2,256,256]{3,2,0,1:T(8,128)(2,1)}, f32[2,256,256]{2,1,0:T(8,128)S(1)}, s32[2]{0:T(128)S(1)}, s32[2]{0:T(128)S(1)}, /*index=5...) while((s32[]{:T(128)}, ...), condition=%wide.region_1.2_spmd, body=%wide.region_0.1_spmd.sunk | while | flops 1179659 | bytes 2622219 | solution.py:149
  82.6 0.6 dynamic_slice.36
  84.9 0.6 dynamic_slice.37
  87.2 0.6 dynamic_slice.35
  89.4 1.2 dynamic-slice_convert_fusion.2
  90.7 0.7 fusion.363
  91.5 0.6 dynamic_slice.36
  93.7 0.6 dynamic_slice.37
  96.0 0.6 dynamic_slice.35
  98.3 1.2 dynamic-slice_convert_fusion.2
  99.6 0.7 fusion.363
  100.3 1.1 slice_bitcast_fusion.7
  104.2 6.1 broadcast_in_dim.39
  110.3 15.3 %while.21 = (s32[]{:T(128)}, f32[2,2,384,2048]{3,2,1,0:T(8,128)}, s32[]{:T(128)}, s32[2,3]{1,0:T(2,128)S(1)}, f32[2,256,256]{2,1,0:T(8,128)S(1)}, /*index=5*/f32...) while((s32[]{:T(128)}, f32[2,2,384,2048]{3,2,1,0:T(8,128)}, ...), condition=%wide.region_4.5_spmd, body=%wide.region_3.4_spmd.sunk | while | flops 786446 | bytes 5243209 | solution.py:162
  111.0 0.6 fusion.364
  117.4 1.4 fusion.365
  118.8 6.2 dynamic_update_slice.11
  125.7 5.6 convert.32
  131.6 5.0 collective-permute-start.2
  136.6 1.4 collective-permute-start.3
  138.1 44.4 %collective-permute-done.2 = bf16[2,2,128,2048]{3,2,1,0:T(8,128)(2,1)S(1)} collective-permute-done((bf16[2,2,128,2048]{3,2,1,0:T(8,128)(2,1)S(1)}, bf16[2,2,128,2048]{3,2,1,0:T(8,128)(2,1)S(1)}, u32[]{:S(2)}, u32[]{:S(2)}) %collective-permute-start.2) | collective-permute-done | bytes 2097184 | tf_op jit(solution)/shard_map/ppermute | solution.py:18
  182.5 3.5 add_add_fusion
  186.0 4.6 constant_dynamic-update-slice_fusion
  190.6 1.1 fusion.343
  191.7 1.3 collective-permute-start.5
  193.0 4.3 collective-permute-start.4
  197.6 2.1 select_maximum_fusion
  199.8 2.1 divide_bitcast_fusion
  201.8 1.8 dynamic-update-slice.1
  203.6 4.2 divide_bitcast_fusion.1
  207.8 0.7 fusion.86
  208.5 19.2 %fusion.38 = f32[2,128,512]{2,1,0:T(8,128)S(1)} fusion(f32[2,128,2048]{2,1,0:T(8,128)S(1)} %fusion.86, s32[2048]{0:T(1024)S(1)} %multiply_add_fusion, f32[512]{0:T(512)S(1)} %fusion.272), kind=kOutput, calls=%fused_computation.74 | convolution fusion | flops 3236954112 | bytes 2631680 | tf_op jit(solution)/shard_map/arn,kn->ark/dot_general | solution.py:182
  227.7 19.6 %fusion.54 = f32[2,128,512]{2,1,0:T(8,128)S(1)} fusion(f32[2,128,2048]{2,1,0:T(8,128)S(1)} %fusion.86, s32[512]{0:T(512)S(1)} %iota_add_fusion.1, f32[512]{0:T(512)S(1)} %compare_select_fusion.1, s32[2048]{0:T(1024)S(1)} %multiply_add_fusion), kind=kOutput, calls=%fused_computation.82 | convolution fusion | flops 3236954112 | bytes 2633728 | tf_op jit(solution)/shard_map/arn,kn->ark/dot_general | solution.py:182
  247.3 19.2 %fusion.62 = f32[2,128,512]{2,1,0:T(8,128)S(1)} fusion(f32[2,128,2048]{2,1,0:T(8,128)S(1)} %fusion.86, s32[512]{0:T(512)S(1)} %iota_add_fusion.2, f32[512]{0:T(512)S(1)} %compare_select_fusion.2, s32[2048]{0:T(1024)S(1)} %multiply_add_fusion), kind=kOutput, calls=%fused_computation.86 | convolution fusion | flops 3236954112 | bytes 2633728 | tf_op jit(solution)/shard_map/arn,kn->ark/dot_general | solution.py:182
  266.5 19.6 %fusion.46 = f32[2,128,512]{2,1,0:T(8,128)S(1)} fusion(f32[2,128,2048]{2,1,0:T(8,128)S(1)} %fusion.86, s32[512]{0:T(512)S(1)} %iota_add_fusion, f32[512]{0:T(512)S(1)} %compare_select_fusion, s32[2048]{0:T(1024)S(1)} %multiply_add_fusion), kind=kOutput, calls=%fused_computation.78 | convolution fusion | flops 3236954112 | bytes 2633728 | tf_op jit(solution)/shard_map/arn,kn->ark/dot_general | solution.py:182
  286.2 2.3 copy.65
  288.6 22.0 %all-to-all-start = ((f32[2,128,2048]{1,0,2:T(2,128)}), f32[2,128,2048]{1,0,2:T(2,128)S(1)}, u32[]{:S(2)}, u32[]{:S(2)}) async-start(f32[2,128,2048]{1,0,2:T(2,128)} %copy.65), calls=%async_computation | async-start | bytes 4194304 | tf_op jit(solution)/shard_map/all_to_all | solution.py:192
  310.9 40.8 %all-to-all-done = f32[2,128,2048]{1,0,2:T(2,128)S(1)} async-done(((f32[2,128,2048]{1,0,2:T(2,128)}), f32[2,128,2048]{1,0,2:T(2,128)S(1)}, u32[]{:S(2)}, u32[]{:S(2)}) %all-to-all-start) | async-done | bytes 2097184 | tf_op jit(solution)/shard_map/all_to_all | solution.py:192
  351.7 1.5 copy.66
  353.2 1.9 copy.67
  355.1 22.5 %fusion.211 = f32[2,512,128]{1,2,0:T(8,128)S(1)} fusion(f32[2,2048,128]{2,1,0:T(8,128)S(1)} %bitcast.238, s32[512]{0:T(512)S(1)} %iota_add_fusion.1, f32[512]{0:T(512)S(1)} %compare_select_fusion.1, s32[2048]{0:T(1024)S(1)} %multiply_add_fusion, f32[512,128]{0,1:T(8,128)S(1)} %get-tuple-element.165), kind=kOutput, calls=%fused_computation.220 | convolution fusion | flops 3237085184 | bytes 2895872 | tf_op jit(solution)/shard_map/ki,aij->akj/dot_general | solution.py:199
  377.6 19.3 %fusion.50 = f32[2,128,2048]{2,1,0:T(8,128)S(1)} fusion(f32[2,512,128]{1,2,0:T(8,128)S(1)} %fusion.211, s32[512]{0:T(512)S(1)} %iota_add_fusion.1, f32[512]{0:T(512)S(1)} %compare_select_fusion.1, s32[2048]{0:T(1024)S(1)} %multiply_add_fusion), kind=kOutput, calls=%fused_computation.80 | convolution fusion | flops 3236954112 | bytes 2633728 | tf_op jit(solution)/shard_map/ki,akj->aij/dot_general | solution.py:206
  396.9 23.2 %fusion.217 = f32[2,512,128]{1,2,0:T(8,128)S(1)} fusion(f32[2,2048,128]{2,1,0:T(8,128)S(1)} %bitcast.239, s32[2048]{0:T(1024)S(1)} %multiply_add_fusion, f32[512]{0:T(512)S(1)} %fusion.272, f32[512,128]{0,1:T(8,128)S(1)} %get-tuple-element.167), kind=kOutput, calls=%fused_computation.222 | convolution fusion | flops 3237085184 | bytes 2893824 | tf_op jit(solution)/shard_map/ki,aij->akj/dot_general | solution.py:199
  420.1 19.3 %fusion.34 = f32[2,128,2048]{2,1,0:T(8,128)S(1)} fusion(f32[2,512,128]{1,2,0:T(8,128)S(1)} %fusion.217, s32[2048]{0:T(1024)S(1)} %multiply_add_fusion, f32[512]{0:T(512)S(1)} %fusion.272), kind=kOutput, calls=%fused_computation.72 | convolution fusion | flops 3236954112 | bytes 2631680 | tf_op jit(solution)/shard_map/ki,akj->aij/dot_general | solution.py:206
  439.4 23.1 %fusion.208 = f32[2,512,128]{1,2,0:T(8,128)S(1)} fusion(f32[2,2048,128]{2,1,0:T(8,128)S(1)} %bitcast.240, s32[512]{0:T(512)S(1)} %iota_add_fusion, f32[512]{0:T(512)S(1)} %compare_select_fusion, s32[2048]{0:T(1024)S(1)} %multiply_add_fusion, f32[512,128]{0,1:T(8,128)S(1)} %get-tuple-element.166), kind=kOutput, calls=%fused_computation.219 | convolution fusion | flops 3237085184 | bytes 2895872 | tf_op jit(solution)/shard_map/ki,aij->akj/dot_general | solution.py:199
  462.5 19.3 %fusion.42 = f32[2,128,2048]{2,1,0:T(8,128)S(1)} fusion(f32[2,512,128]{1,2,0:T(8,128)S(1)} %fusion.208, s32[512]{0:T(512)S(1)} %iota_add_fusion, f32[512]{0:T(512)S(1)} %compare_select_fusion, s32[2048]{0:T(1024)S(1)} %multiply_add_fusion), kind=kOutput, calls=%fused_computation.76 | convolution fusion | flops 3236954112 | bytes 2633728 | tf_op jit(solution)/shard_map/ki,akj->aij/dot_general | solution.py:206
  481.8 23.2 %fusion.214 = f32[2,512,128]{1,2,0:T(8,128)S(1)} fusion(f32[2,2048,128]{2,1,0:T(8,128)S(1)} %bitcast.241, s32[512]{0:T(512)S(1)} %iota_add_fusion.2, f32[512]{0:T(512)S(1)} %compare_select_fusion.2, s32[2048]{0:T(1024)S(1)} %multiply_add_fusion, f32[512,128]{0,1:T(8,128)S(1)} %get-tuple-element.164), kind=kOutput, calls=%fused_computation.221 | convolution fusion | flops 3237085184 | bytes 2895872 | tf_op jit(solution)/shard_map/ki,aij->akj/dot_general | solution.py:199
  505.0 20.8 %fusion.73 = f32[2,2048,128]{1,2,0:T(8,128)} fusion(f32[2,128,2048]{2,1,0:T(8,128)S(1)} %fusion.42, f32[2,128,2048]{2,1,0:T(8,128)S(1)} %fusion.50, f32[2,128,2048]{2,1,0:T(8,128)S(1)} %fusion.34, f32[2,512,128]{1,2,0:T(8,128)S(1)} %fusion.214, s32[512]{0:T(512)S(1)} %iota_add_fusion.2, f32[512]{0:T(512)S(1)} %compare_select_fusion.2, ...), kind=kOutput, calls=%fused_computation.90 | convolution fusion | flops 3238526976 | bytes 8925184 | tf_op jit(solution)/shard_map/ki,akj->aij/dot_general | solution.py:206
  525.8 2.8 copy.72
  528.6 58.3 %all_to_all.36 = f32[2,2048,128]{2,0,1:T(2,128)S(1)} all-to-all(f32[2,2048,128]{2,0,1:T(2,128)S(1)} %copy.72), channel_id=1, replica_groups=mesh['group'=2,'tile'=16] {'tile'}, dimensions={1} | all-to-all | bytes 4194304 | tf_op jit(solution)/shard_map/all_to_all | solution.py:209
  587.0 1.2 copy.91
  588.2 1.6 all_to_all.33
  589.8 20.3 %fusion.48 = f32[2,128,2048]{2,1,0:T(8,128)S(1)} fusion(s32[512]{0:T(512)S(1)} %iota_add_fusion.1, f32[512]{0:T(512)S(1)} %compare_select_fusion.1, s32[2048]{0:T(1024)S(1)} %multiply_add_fusion, f32[2,128,2048]{2,1,0:T(8,128)} %all_to_all.33), kind=kOutput, calls=%fused_computation.79 | convolution fusion | flops 3236954112 | bytes 2633728 | tf_op jit(solution)/shard_map/ark,kn->arn/dot_general | solution.py:213
  610.1 19.5 %fusion.32 = f32[2,128,2048]{2,1,0:T(8,128)S(1)} fusion(s32[2048]{0:T(1024)S(1)} %multiply_add_fusion, f32[512]{0:T(512)S(1)} %fusion.272, f32[2,128,2048]{2,1,0:T(8,128)S(1)} %copy-done.3), kind=kOutput, calls=%fused_computation.71 | convolution fusion | flops 3236954112 | bytes 2631680 | tf_op jit(solution)/shard_map/ark,kn->arn/dot_general | solution.py:213
  629.6 19.1 %fusion.40 = f32[2,128,2048]{2,1,0:T(8,128)S(1)} fusion(s32[512]{0:T(512)S(1)} %iota_add_fusion, f32[512]{0:T(512)S(1)} %compare_select_fusion, s32[2048]{0:T(1024)S(1)} %multiply_add_fusion, f32[2,128,2048]{2,1,0:T(8,128)S(1)} %copy-done.3), kind=kOutput, calls=%fused_computation.75 | convolution fusion | flops 3236954112 | bytes 2633728 | tf_op jit(solution)/shard_map/ark,kn->arn/dot_general | solution.py:213
  648.7 21.0 %fusion.82 = f32[2,128,2048]{2,1,0:T(8,128)} fusion(f32[2,128,2048]{2,1,0:T(8,128)S(1)} %fusion.40, f32[2,128,2048]{2,1,0:T(8,128)S(1)} %fusion.48, f32[2,128,2048]{2,1,0:T(8,128)S(1)} %fusion.32, s32[512]{0:T(512)S(1)} %iota_add_fusion.2, f32[512]{0:T(512)S(1)} %compare_select_fusion.2, s32[2048]{0:T(1024)S(1)} %multiply_add_fusion, ...), kind=kOutput, calls=%fused_computation.93 | convolution fusion | flops 3238526976 | bytes 8925184 | tf_op jit(solution)/shard_map/ark,kn->arn/dot_general | solution.py:213
  (49 shorter events, 4.6 us)
Async XLA Ops:
  0.6 5.2 copy-start.4
  0.6 5.4 copy-start
  0.7 6.8 %copy-start.5 = (s32[2,3]{1,0:T(2,128)S(1)}, s32[2,3]{1,0:T(2,128)}, u32[]{:S(2)}) copy-start(s32[2,3]{1,0:T(2,128)} %param.12) | copy-start | bytes 76
  3.2 6.5 collective-permute-start
  4.5 72.6 %collective-permute-start.1 = (bf16[2,2,128,2048]{3,2,1,0:T(8,128)(2,1)S(1)}, bf16[2,2,128,2048]{3,2,1,0:T(8,128)(2,1)}, u32[]{:S(2)}, u32[]{:S(2)}) collective-permute-start(bf16[2,2,128,2048]{3,2,1,0:T(8,128)(2,1)S(1)} %convert_element_type.153), channel_id=1, source_target_pairs={{2,0},{3,1},{4,2},{5,3},{6,4},{7,5},{8,6},{9,7},{10,8},{11,9},{12,... | collective-permute-start | bytes 6291464 | tf_op jit(solution)/shard_map/ppermute | solution.py:18
  131.2 51.3 %copy-start.2 = (f32[2,2,128,2048]{3,2,1,0:T(8,128)S(1)}, f32[2,2,128,2048]{3,2,1,0:T(8,128)}, u32[]{:S(2)}) copy-start(f32[2,2,128,2048]{3,2,1,0:T(8,128)} %param.9) | copy-start | bytes 12582916
  131.6 50.9 %collective-permute-start.2 = (bf16[2,2,128,2048]{3,2,1,0:T(8,128)(2,1)S(1)}, bf16[2,2,128,2048]{3,2,1,0:T(8,128)(2,1)S(1)}, u32[]{:S(2)}, u32[]{:S(2)}) collective-permute-start(bf16[2,2,128,2048]{3,2,1,0:T(8,128)(2,1)S(1)} %get-tuple-element.145), channel_id=1, source_target_pairs={{0,2},{1,3},{2,4},{3,5},{4,6},{5,7},{6,8},{7,9},{8,10},{9,11},{10,... | collective-permute-start | bytes 6291464 | tf_op jit(solution)/shard_map/ppermute | solution.py:18
  136.6 45.9 %collective-permute-start.3 = (bf16[2,2,128,2048]{3,2,1,0:T(8,128)(2,1)S(1)}, bf16[2,2,128,2048]{3,2,1,0:T(8,128)(2,1)S(1)}, u32[]{:S(2)}, u32[]{:S(2)}) collective-permute-start(bf16[2,2,128,2048]{3,2,1,0:T(8,128)(2,1)S(1)} %get-tuple-element.146), channel_id=1, source_target_pairs={{0,1},{1,2},{2,3},{3,4},{4,5},{5,6},{6,7},{7,8},{8,9},{9,10},{10,1... | collective-permute-start | bytes 6291464 | tf_op jit(solution)/shard_map/ppermute | solution.py:18
  186.0 11.6 %copy-start.1 = (f32[2,2,128,2048]{3,2,1,0:T(8,128)}, f32[2,2,128,2048]{3,2,1,0:T(8,128)S(1)}, u32[]{:S(2)}) copy-start(f32[2,2,128,2048]{3,2,1,0:T(8,128)S(1)} %add_add_fusion) | copy-start | bytes 12582916
  191.7 5.6 collective-permute-start.5
  193.0 4.6 collective-permute-start.4
  288.6 63.2 %all-to-all-start = ((f32[2,128,2048]{1,0,2:T(2,128)}), f32[2,128,2048]{1,0,2:T(2,128)S(1)}, u32[]{:S(2)}, u32[]{:S(2)}) async-start(f32[2,128,2048]{1,0,2:T(2,128)} %copy.65), calls=%async_computation | async-start | bytes 4194304 | tf_op jit(solution)/shard_map/all_to_all | solution.py:192
  589.8 20.3 %copy-start.3 = (f32[2,128,2048]{2,1,0:T(8,128)S(1)}, f32[2,128,2048]{2,1,0:T(8,128)}, u32[]{:S(2)}) copy-start(f32[2,128,2048]{2,1,0:T(8,128)} %all_to_all.33) | copy-start | bytes 6291460
where the time goes:
time: 680 us; the launch traced here: 670 us
  matrix products  330 us (49%)
  waiting for transfers between devices  153 us (22%)
  blocking collectives  58.3 us (9%)
  local copies, waits for them, and re-layouts  37.1 us (5%)
  starting transfers between devices  36.6 us (5%)
  other arithmetic  35.8 us (5%)
  loops' own time  17.2 us (3%)
    ppermute x4, waiting for transfers between devices, passed_along(): return lax.ppermute(x, axis, pairs)  112 us
    dot_general x4, matrix products, body(): jnp.einsum('ki,aij->akj', solve_cos_block, pencil, precision=exact_mode)  92 us
    dot_general x4, matrix products, body(): jnp.einsum('ark,kn->arn', row_solved[:, :, first_freq:first_freq + block_...  79.8 us
    dot_general x4, matrix products, body(): jnp.einsum('ki,akj->aij', solve_cos_block, partial_value, precision=exact...  78.7 us
    dot_general x4, matrix products, body(): jnp.einsum('arn,kn->ark', source, cosine_rows(first_freq, block_rows, gri...  77.6 us
    all_to_all x1, blocking collectives, body(): lax.all_to_all(solved, 'tile', split_axis=1, concat_axis=2, tiled=True)  58.3 us
    all_to_all x1, waiting for transfers between devices, body(): lax.all_to_all(column_coeffs, 'tile', split_axis=2, concat_axis=1, tiled=...  40.8 us
    all_to_all x1, starting transfers between devices, body(): lax.all_to_all(column_coeffs, 'tile', split_axis=2, concat_axis=1, tiled=...  22 us
  transfers between devices with their start and end apart: 7, of which 4 were waited for; matrix products, arithmetic and copies ran while one was open for 1% of the time, Pallas kernels for 0%

commit v1 on v0

v1 whole, which is shorter than its diff:
```python
import functools
import math

import jax
import jax.numpy as jnp
import ml_dtypes
import numpy as np
from jax import lax
from jax.experimental import pallas as pl
from jax.experimental.pallas import tpu as pltpu
from jax.sharding import PartitionSpec as P

magnitude_floor = 0.5
soften_term = 0.5
screen_term = 0.0001
epsilon_term = 1e-06
LANES = 128
SEG = 8
PAD = 8
f32 = jnp.float32
bf16 = jnp.bfloat16
VMEM_SPEC = pl.BlockSpec(memory_space=pltpu.VMEM)
SMEM_SPEC = pl.BlockSpec(memory_space=pltpu.SMEM)
ANY_SPEC = pl.BlockSpec(memory_space=pl.ANY)
PARAMS = pltpu.CompilerParams(vmem_limit_bytes=52 * 1024 * 1024)


def split_table(table):
    high = table.astype(ml_dtypes.bfloat16)
    low = (table - high.astype(np.float64)).astype(ml_dtypes.bfloat16)
    return np.stack([high, low])


def fourier_blocks(side):
    index = np.arange(side)
    phase = (index[:, None] * index[None, :] % side) * (-2.0 * math.pi / side)
    cos_part = np.cos(phase) / math.sqrt(side)
    sin_part = np.sin(phase) / math.sqrt(side)
    left = np.block([[cos_part, -sin_part], [sin_part, cos_part]])
    right = np.block([[cos_part, sin_part], [-sin_part, cos_part]])
    return left.astype(ml_dtypes.bfloat16), right.astype(ml_dtypes.bfloat16)


def cosine_halves(grid):
    half = grid // 2
    freqs = np.arange(grid)
    pixels = np.arange(half)
    phase = (2 * pixels[None, :] + 1) * freqs[:, None] % (4 * grid)
    scale = np.where(freqs == 0, math.sqrt(1.0 / grid), math.sqrt(2.0 / grid))
    table = scale[:, None] * np.cos(phase * (math.pi / (2 * grid)))
    return np.stack([table[0::2], table[1::2]])


def decay_tables(grid, strip):
    freqs = np.concatenate([np.arange(0, grid, 2), np.arange(1, grid, 2)])
    mu = screen_term + 4.0 * np.sin(freqs * (math.pi / (2 * grid))) ** 2
    root = 1.0 + mu / 2 - np.sqrt(mu + mu * mu / 4)
    log_root = np.log(root)
    steps = strip // SEG
    devices = grid // strip

    def power(exponents):
        return np.exp(np.maximum(log_root[None, :] * np.asarray(exponents)[:, None], -80.0)) * (
            log_root[None, :] * np.asarray(exponents)[:, None] > -80.0
        )

    scan = np.concatenate([power([1, steps, 2 * steps, 4 * steps]), (root / (1 - root * root))[None]])
    inner = power(np.arange(1, steps + 1))
    segs = power(steps * np.arange(SEG))
    strips = power(strip * np.arange(devices + 1))
    closing = 1.0 / (1.0 - power([2 * grid]))
    as32 = lambda x: x.astype(np.float32)
    return as32(scan), as32(inner), as32(segs), as32(segs[::-1]), as32(strips), as32(closing)


def clip(value, top):
    return jnp.minimum(jnp.maximum(value, 0), top)


def extract_kernel(tab, field, out, raw, sems):
    caps, _, strip, frame = out.shape
    angles, grid = field.shape[0], field.shape[3]
    wide = frame + LANES
    copies = []
    shifts = []
    for slot in range(caps):
        column = clip(tab[3 * slot + 1], grid - frame)
        angle = clip(tab[3 * slot + 2], angles - 1)
        block = jnp.minimum(column // LANES, (grid - wide) // LANES)
        shifts.append(column - block * LANES)
        start = pl.multiple_of(block * LANES, LANES)
        copies.append(
            pltpu.make_async_copy(
                field.at[angle, :, :, pl.ds(start, wide)], raw.at[slot], sems.at[slot]
            )
        )
    for copy in copies:
        copy.start()
    for slot in range(caps):
        copies[slot].wait()
        for part in range(2):
            moved = pltpu.roll(raw[slot, part], lax.rem(wide - shifts[slot], wide), axis=1)
            out[slot, part] = moved[:, :frame].astype(bf16)


def extract(tab, field, caps, frame):
    angles, _, strip, grid = field.shape
    return pl.pallas_call(
        extract_kernel,
        out_shape=jax.ShapeDtypeStruct((caps, 2, strip, frame), bf16),
        in_specs=[SMEM_SPEC, ANY_SPEC],
        out_specs=VMEM_SPEC,
        scratch_shapes=[
            pltpu.VMEM((caps, 2, strip, frame + LANES), f32),
            pltpu.SemaphoreType.DMA((caps,)),
        ],
        compiler_params=PARAMS,
        name="extract",
    )(tab, field)


def frame_kernel(reach, center, tab, probe, measured, left, right, *rest):
    windows = rest[: reach + 1]
    first_piece = rest[reach + 1]
    pieces = rest[reach + 2 : 2 * reach + 3]
    window_buf, update_buf = rest[2 * reach + 3 :]
    caps, frame = measured.shape[0], measured.shape[1]
    strip = windows[0].shape[2]
    blocks = frame // LANES
    count = tab[3 * caps]
    probe_re, probe_im = probe[0], probe[1]
    peak = jnp.max(probe_re * probe_re + probe_im * probe_im) + epsilon_term
    for slot in range(caps):
        update_buf[...] = jnp.zeros_like(update_buf)

        @pl.when(slot < count)
        def _():
            offset = clip(tab[3 * slot], strip - 1)
            for j in range(reach + 1):
                for part in range(2):
                    for k in range(blocks):
                        window_buf[part, k, j * strip : (j + 1) * strip] = windows[j][
                            slot, part, :, k * LANES : (k + 1) * LANES
                        ].astype(f32)
            obj_re, obj_im = (
                jnp.concatenate(
                    [window_buf[part, k, pl.ds(offset, frame), :] for k in range(blocks)], axis=1
                )
                for part in range(2)
            )
            wave = jnp.concatenate(
                [
                    (probe_re * obj_re - probe_im * obj_im).astype(bf16),
                    (probe_re * obj_im + probe_im * obj_re).astype(bf16),
                ],
                axis=0,
            )

            def both(first, second, rows):
                first_half = jnp.dot(first, rows, preferred_element_type=f32).astype(bf16)
                beside = jnp.concatenate([first_half[:frame], first_half[frame:]], axis=1)
                return jnp.dot(beside, second, preferred_element_type=f32)

            spectrum = both(left[...], right[...], wave)
            spec_re, spec_im = spectrum[:, :frame], spectrum[:, frame:]
            power = spec_re * spec_re + spec_im * spec_im
            factor = (
                measured[slot].astype(f32) * lax.rsqrt(jnp.maximum(power, magnitude_floor**2)) - 1.0
            )
            change = jnp.concatenate(
                [(spec_re * factor).astype(bf16), (spec_im * factor).astype(bf16)], axis=0
            )
            correction = both(right[...], left[...], change)
            corr_re, corr_im = correction[:, :frame], correction[:, frame:]
            update = (
                (probe_re * corr_re + probe_im * corr_im) / peak,
                (probe_re * corr_im - probe_im * corr_re) / peak,
            )
            for part in range(2):
                for k in range(blocks):
                    update_buf[part, k, pl.ds(2 * PAD + offset, frame), :] = update[part][
                        :, k * LANES : (k + 1) * LANES
                    ]

        for part in range(2):
            for k in range(blocks):
                lanes = slice(k * LANES, (k + 1) * LANES)
                first_piece[slot, part, :, lanes] = update_buf[part, k, 2 * PAD : 4 * PAD].astype(
                    first_piece.dtype
                )
                for j in range(reach + 1):
                    pieces[j][slot, part, :, lanes] = update_buf[
                        part, k, j * strip + PAD : (j + 1) * strip + 3 * PAD
                    ].astype(pieces[j].dtype)


def run_frames(tab, probe, measured, windows, center):
    reach = len(windows) - 1
    caps, frame = measured.shape[0], measured.shape[1]
    strip = windows[0].shape[2]
    left, right = fourier_blocks(frame)
    rows = (reach + 1) * strip
    piece = lambda j: jax.ShapeDtypeStruct(
        (caps, 2, strip + 2 * PAD, frame), f32 if j == center else bf16
    )
    return pl.pallas_call(
        functools.partial(frame_kernel, reach, center),
        out_shape=[jax.ShapeDtypeStruct((caps, 2, 2 * PAD, frame), bf16)]
        + [piece(j) for j in range(reach + 1)],
        in_specs=[SMEM_SPEC] + [VMEM_SPEC] * (5 + reach),
        out_specs=[VMEM_SPEC] * (reach + 2),
        scratch_shapes=[
            pltpu.VMEM((2, frame // LANES, rows, LANES), f32),
            pltpu.VMEM((2, frame // LANES, rows + 4 * PAD, LANES), f32),
        ],
        compiler_params=PARAMS,
        name="frames",
    )(tab, probe, measured, jnp.asarray(left), jnp.asarray(right), *windows)


def reversed_lanes(values):
    index = LANES - 1 - lax.broadcasted_iota(jnp.int32, values.shape, 1)
    return jnp.take_along_axis(values, index, axis=1)


def split_pair(values):
    high = values.astype(bf16)
    return high, (values - high.astype(f32)).astype(bf16)


def three_pass(rows, count, high, low):
    both = jnp.dot(rows, high, preferred_element_type=f32)
    return both[:count] + both[count:] + jnp.dot(rows[:count], low, preferred_element_type=f32)


def update_kernel(reach, tabs, field, top, bottom, scan, table_hbm, *rest):
    first_piece = rest[0]
    pieces = rest[1 : reach + 2]
    updated, inner, carry_y, carry_z, ends = rest[reach + 2 : reach + 7]
    ext, row_bond, source, rows_in, table, load_sems, store_sems, table_sems = rest[reach + 7 :]
    angles, _, strip, grid = field.shape
    blocks = grid // LANES
    half_blocks = blocks // 2
    half = grid // 2
    steps = strip // SEG
    count = angles * strip
    caps = pieces[0].shape[0]
    frame = pieces[0].shape[3]
    frame_blocks = frame // LANES

    def load(a, b):
        start = b * LANES
        return pltpu.make_async_copy(
            field.at[a, :, :, pl.ds(start, LANES)],
            ext.at[a, :, b, pl.ds(PAD, strip), :],
            load_sems.at[a, b],
        )

    def store(a, b):
        start = b * LANES
        return pltpu.make_async_copy(
            ext.at[a, :, b, pl.ds(PAD, strip), :],
            updated.at[a, :, :, pl.ds(start, LANES)],
            store_sems.at[a, b],
        )

    def load_table(h, k):
        return pltpu.make_async_copy(table_hbm.at[k, h], table.at[k, h], table_sems.at[k, h])

    for a in range(angles):
        for b in range(blocks):
            load(a, b).start()
    for h in range(2):
        for k in range(2):
            load_table(h, k).start()

    for a in range(angles):
        for part in range(2):
            for b in range(blocks):
                lanes = slice(b * LANES, (b + 1) * LANES)
                ext[a, part, b, PAD - 1 : PAD, :] = top[a, part, :, lanes]
                ext[a, part, b, PAD + strip : PAD + strip + 1, :] = bottom[a, part, :, lanes]
            ext[a, part, blocks] = jnp.zeros((strip + 2 * PAD, LANES), f32)
    for a in range(angles):
        for b in range(blocks):
            load(a, b).wait()

    def add_piece(piece, tab_row, slot, first_row, rows):
        @pl.when(slot < tabs[tab_row, 3 * caps])
        def _():
            column = clip(tabs[tab_row, 3 * slot + 1], grid - frame)
            angle = clip(tabs[tab_row, 3 * slot + 2], angles - 1)
            block = jnp.minimum(column // LANES, blocks - frame_blocks - 1)
            shift = column - block * LANES
            for part in range(2):
                values = piece[slot, part, :rows].astype(f32)
                values = jnp.concatenate([values, jnp.zeros((rows, LANES), f32)], axis=1)
                values = pltpu.roll(values, shift, axis=1)
                for k in range(frame_blocks + 1):
                    spot = ext.at[angle, part, block + k, first_row : first_row + rows]
                    spot[...] += values[:, k * LANES : (k + 1) * LANES]

    for slot in range(caps):
        add_piece(first_piece, 0, slot, PAD + strip, PAD)
        for j in range(reach + 1):
            add_piece(pieces[j], j + 1, slot, 0, strip + 2 * PAD)

    for a in range(angles):
        for b in range(blocks):
            store(a, b).start()

    lane = lax.broadcasted_iota(jnp.int32, (strip, LANES), 1)

    def bond(re, im, power, re_to, im_to, power_to):
        whole = power + power_to
        guess = pl.reciprocal(whole, approx=True)
        guess = guess * (2.0 - whole * guess)
        return (re * im_to - im * re_to) * guess

    def reach_right(now, after):
        return pltpu.roll(jnp.where(lane == 0, after, now), LANES - 1, axis=1)

    for a in range(angles):

        def columns(b, before, a=a):
            tall = strip + PAD
            re, im = ext[a, 0, b, 0:tall], ext[a, 1, b, 0:tall]
            re_to, im_to = ext[a, 0, b, 1 : tall + 1], ext[a, 1, b, 1 : tall + 1]
            power = 0.5 * (re * re + im * im) + 0.25 * soften_term
            power_to = 0.5 * (re_to * re_to + im_to * im_to) + 0.25 * soften_term
            row_bond[0:tall] = bond(re, im, power, re_to, im_to, power_to)
            re, im, power = re[PAD:], im[PAD:], power[PAD:]
            re_to = reach_right(re, ext[a, 0, b + 1, PAD:tall])
            im_to = reach_right(im, ext[a, 1, b + 1, PAD:tall])
            power_to = 0.5 * (re_to * re_to + im_to * im_to) + 0.25 * soften_term
            here = bond(re, im, power, re_to, im_to, power_to)
            shifted = pltpu.roll(jnp.where(lane == LANES - 1, before, here), 1, axis=1)
            source[a, b] = (
                row_bond[PAD - 1 : tall - 1] - row_bond[PAD:tall] + shifted - here
            )
            return here

        lax.fori_loop(0, blocks, columns, jnp.zeros((strip, LANES), f32))

    def fold(b, _):
        lanes = pl.ds(pl.multiple_of(b * LANES, LANES), LANES)
        for a in range(angles):
            for t in range(0, steps, 2):
                lower = jnp.concatenate(
                    [source[a, b, pl.ds(t + i, SEG, stride=steps), :] for i in range(2)], 0
                )
                upper = jnp.concatenate(
                    [
                        source[a, blocks - 1 - b, pl.ds(t + i, SEG, stride=steps), :]
                        for i in range(2)
                    ],
                    0,
                )
                upper = reversed_lanes(upper)
                at = a * strip + t * SEG
                for h, values in enumerate((lower + upper, lower - upper)):
                    high, low = split_pair(values)
                    rows_in[h, at : at + 2 * SEG, lanes] = high
                    rows_in[h, count + at : count + at + 2 * SEG, lanes] = low
        return 0

    lax.fori_loop(0, half_blocks, fold, 0)

    wide = min(2 * LANES, half)
    sub = lax.broadcasted_iota(jnp.int32, (SEG, wide), 0)
    for h in range(2):
        for k in range(2):
            load_table(h, k).wait()

        def transform(c, _, h=h):
            lanes = pl.ds(pl.multiple_of(c * wide, wide), wide)
            spots = pl.ds(pl.multiple_of(h * half + c * wide, wide), wide)
            values = three_pass(rows_in[h], count, table[0, h, :, lanes], table[1, h, :, lanes])
            root = jnp.broadcast_to(scan[0:1, spots], (SEG, wide))
            for a in range(angles):
                terms = [
                    values[a * strip + t * SEG : a * strip + (t + 1) * SEG] for t in range(steps)
                ]
                down = [terms[0]]
                for t in range(1, steps):
                    down.append(terms[t] + root * down[-1])
                up = terms[steps - 1]
                inner[a, (steps - 1) * SEG : steps * SEG, spots] = down[steps - 1]
                for t in range(steps - 2, -1, -1):
                    after = root * up
                    inner[a, t * SEG : (t + 1) * SEG, spots] = down[t] + after
                    up = terms[t] + after
                tail_y, tail_z = down[steps - 1], up
                for i, k in enumerate((1, 2, 4)):
                    factor = scan[i + 1 : i + 2, spots]
                    tail_y = tail_y + jnp.where(
                        sub >= k, factor * pltpu.roll(tail_y, k, axis=0), 0.0
                    )
                    tail_z = tail_z + jnp.where(
                        sub < SEG - k, factor * pltpu.roll(tail_z, SEG - k, axis=0), 0.0
                    )
                carry_y[a, :, spots] = jnp.where(sub >= 1, pltpu.roll(tail_y, 1, axis=0), 0.0)
                carry_z[a, :, spots] = jnp.where(
                    sub < SEG - 1, pltpu.roll(tail_z, SEG - 1, axis=0), 0.0
                )
                ends[0, a : a + 1, spots] = tail_z[0:1]
                ends[1, a : a + 1, spots] = tail_y[SEG - 1 : SEG]
            return 0

        lax.fori_loop(0, half // wide, transform, 0)

    for a in range(angles):
        for b in range(blocks):
            store(a, b).wait()


def run_update(tabs, field, top, bottom, scan, table, first_piece, pieces):
    angles, _, strip, grid = field.shape
    reach = len(pieces) - 1
    blocks = grid // LANES
    half = grid // 2
    return pl.pallas_call(
        functools.partial(update_kernel, reach),
        out_shape=[
            jax.ShapeDtypeStruct(field.shape, f32),
            jax.ShapeDtypeStruct((angles, strip, grid), f32),
            jax.ShapeDtypeStruct((angles, SEG, grid), f32),
            jax.ShapeDtypeStruct((angles, SEG, grid), f32),
            jax.ShapeDtypeStruct((2, angles, grid), f32),
        ],
        in_specs=[SMEM_SPEC, ANY_SPEC, VMEM_SPEC, VMEM_SPEC, VMEM_SPEC, ANY_SPEC]
        + [VMEM_SPEC] * (reach + 2),
        out_specs=[ANY_SPEC] + [VMEM_SPEC] * 4,
        scratch_shapes=[
            pltpu.VMEM((angles, 2, blocks + 1, strip + 2 * PAD, LANES), f32),
            pltpu.VMEM((strip + 2 * PAD, LANES), f32),
            pltpu.VMEM((angles, blocks, strip, LANES), f32),
            pltpu.VMEM((2, 2 * angles * strip, half), bf16),
            pltpu.VMEM((2, 2, half, half), bf16),
            pltpu.SemaphoreType.DMA((angles, blocks)),
            pltpu.SemaphoreType.DMA((angles, blocks)),
            pltpu.SemaphoreType.DMA((2, 2)),
        ],
        compiler_params=PARAMS,
        name="update",
    )(tabs, field, top, bottom, scan, table, first_piece, *pieces)


def phase_kernel(inner, carry_y, carry_z, enter, scan, powers, segs, segs_back, table_hbm, out, rest, rows_in, table, sems):
    angles, strip, grid = inner.shape
    half = grid // 2
    steps = strip // SEG
    count = angles * strip
    half_blocks = half // LANES

    def load_table(h, k):
        return pltpu.make_async_copy(table_hbm.at[k, h], table.at[k, h], sems.at[k, h])

    for h in range(2):
        for k in range(2):
            load_table(h, k).start()

    def solve(b, _):
        spots = pl.ds(pl.multiple_of(b * LANES, LANES), LANES)
        scale = scan[4:5, spots]
        for a in range(angles):
            from_y = scale * (carry_y[a, :, spots] + segs[:, spots] * enter[0, a : a + 1, spots])
            from_z = scale * (carry_z[a, :, spots] + segs_back[:, spots] * enter[1, a : a + 1, spots])
            for t in range(steps):
                rest[a, b, pl.ds(t, SEG, stride=steps), :] = (
                    scale * inner[a, t * SEG : (t + 1) * SEG, spots]
                    + powers[t : t + 1, spots] * from_y
                    + powers[steps - 1 - t : steps - t, spots] * from_z
                )
        return 0

    lax.fori_loop(0, 2 * half_blocks, solve, 0)

    def split(b, _):
        lanes = pl.ds(pl.multiple_of(b * LANES, LANES), LANES)
        for h in range(2):
            for a in range(angles):
                high, low = split_pair(rest[a, h * half_blocks + b])
                rows_in[h, a * strip : (a + 1) * strip, lanes] = high
                rows_in[h, count + a * strip : count + (a + 1) * strip, lanes] = low
        return 0

    lax.fori_loop(0, half_blocks, split, 0)
    for h in range(2):
        for k in range(2):
            load_table(h, k).wait()
    wide = min(2 * LANES, half)

    def back(c, _):
        lanes = pl.ds(pl.multiple_of(c * wide, wide), wide)
        even, odd = (
            three_pass(rows_in[h], count, table[0, h, :, lanes], table[1, h, :, lanes])
            for h in range(2)
        )
        mirrored = even - odd
        plain = even + odd
        for a in range(angles):
            out[a, :, lanes] = plain[a * strip : (a + 1) * strip]
            for k in range(wide // LANES):
                spot = pl.ds(
                    pl.multiple_of(grid - (k + 1) * LANES - c * wide, LANES), LANES
                )
                out[a, :, spot] = reversed_lanes(
                    mirrored[a * strip : (a + 1) * strip, k * LANES : (k + 1) * LANES]
                )
        return 0

    lax.fori_loop(0, half // wide, back, 0)


def run_phase(inner, carry_y, carry_z, enter, scan, powers, segs, segs_back, table):
    angles, strip, grid = inner.shape
    half = grid // 2
    return pl.pallas_call(
        phase_kernel,
        out_shape=jax.ShapeDtypeStruct((angles, strip, grid), f32),
        in_specs=[VMEM_SPEC] * 8 + [ANY_SPEC],
        out_specs=VMEM_SPEC,
        scratch_shapes=[
            pltpu.VMEM((angles, grid // LANES, strip, LANES), f32),
            pltpu.VMEM((2, 2 * angles * strip, half), bf16),
            pltpu.VMEM((2, 2, half, half), bf16),
            pltpu.SemaphoreType.DMA((2, 2)),
        ],
        compiler_params=PARAMS,
        name="phase",
    )(inner, carry_y, carry_z, enter, scan, powers, segs, segs_back, table)


def passed_along(x, by):
    size = lax.axis_size("tile")
    pairs = [(i, i + by) for i in range(size) if 0 <= i + by < size]
    return lax.ppermute(x, "tile", pairs)


def entering_values(ends, strips, closing):
    size = lax.axis_size("tile")
    me = lax.axis_index("tile")
    head, tail = ends[0], ends[1]
    enter_y = jnp.zeros_like(head)
    enter_z = jnp.zeros_like(head)
    row = lambda i: lax.dynamic_slice_in_dim(strips, i, 1, 0)
    width = 1
    while width < size:
        other = lax.ppermute(
            jnp.stack([head, tail]), "tile", [(i, i ^ width) for i in range(size)]
        )
        head_to, tail_to = other[0], other[1]
        second = (me & width) != 0
        before = me & (width - 1)
        span = strips[width : width + 1]
        enter_y = enter_y + jnp.where(second, row(before) * tail_to, 0.0)
        enter_z = enter_z + jnp.where(second, 0.0, row(width - 1 - before) * head_to)
        head, tail = (
            jnp.where(second, head_to + span * head, head + span * head_to),
            jnp.where(second, tail + span * tail_to, tail_to + span * tail),
        )
        width *= 2
    whole = strips[size : size + 1]
    enter_y = enter_y + row(me) * (head + whole * tail) * closing
    enter_z = enter_z + row(size - 1 - me) * (tail + whole * head) * closing
    return jnp.stack([enter_y, enter_z])


def body(object_field, probe, measured, frame_table, frame_count):
    angles, _, strip, grid = object_field.shape
    caps, frame = measured.shape[0], measured.shape[1]
    reach = frame // strip
    center = reach // 2
    table = cosine_halves(grid)
    forward_table = jnp.asarray(split_table(np.swapaxes(table, 1, 2)))
    back_table = jnp.asarray(split_table(table))
    scan, powers, segs, segs_back, strips, closing = (
        jnp.asarray(x) for x in decay_tables(grid, strip)
    )

    own_tab = jnp.concatenate([frame_table.reshape(-1), frame_count])
    tabs = {j: own_tab if j == 0 else passed_along(own_tab, j) for j in range(-1, reach + 1)}
    measured_here = passed_along(measured, center)
    bottom = passed_along(object_field[:, :, :1], -1)
    top = passed_along(object_field[:, :, strip - 1 :], 1)
    windows = []
    for j in range(reach + 1):
        window = extract(tabs[j], object_field, caps, frame)
        windows.append(window if j == center else passed_along(window, center - j))
    first_piece, *pieces = run_frames(tabs[center], probe, measured_here, windows, center)
    first_piece = passed_along(first_piece, -1 - center)
    pieces = [
        piece if j == center else passed_along(piece, j - center) for j, piece in enumerate(pieces)
    ]
    all_tabs = jnp.stack([tabs[j] for j in range(-1, reach + 1)])
    updated, inner, carry_y, carry_z, ends = run_update(
        all_tabs, object_field, top, bottom, scan, forward_table, first_piece, pieces
    )
    enter = entering_values(ends, strips, closing)
    phase_map = run_phase(
        inner, carry_y, carry_z, enter, scan, powers, segs, segs_back, back_table
    )
    return (updated, phase_map)


def solution(mesh):
    return jax.shard_map(
        body,
        mesh=mesh,
        in_specs=(
            P("group", None, "tile", None),
            P(),
            P(("group", "tile"), None, None),
            P(("group", "tile"), None),
            P(("group", "tile")),
        ),
        out_specs=(P("group", None, "tile", None), P("group", "tile", None)),
        check_vma=False,
    )
```

time: 680 us -> 95.9 us (0.14); the launches traced: 670 us -> 94.1 us
  matrix products: 330 us -> 0 us
  waiting for transfers between devices: 153 us -> 11.6 us
  blocking collectives: 58.3 us -> 0 us
  Pallas kernels: 0 us -> 37 us
  other arithmetic: 35.8 us -> 0.44 us
  local copies, waits for them, and re-layouts: 37.1 us -> 4.18 us
  loops' own time: 17.2 us -> 0 us
    dot_general x20 -> x0, matrix products: 330 us -> none  [the longest x4 92 us: body(): jnp.einsum('ki,aij->akj', solve_cos_block, pencil, precision=exact_mode)]
    ppermute x6 -> x15, waiting for transfers between devices: 112 us -> 11.6 us  [the longest x4 5.98 us: entering_values(): lax.ppermute(jnp.stack([head, tail]), 'tile', [(i, i ^ width) for i in ra...]
    all_to_all x1 -> x0, blocking collectives: 58.3 us -> none  [body(): lax.all_to_all(solved, 'tile', split_axis=1, concat_axis=2, tiled=True)]
    all_to_all x1 -> x0, waiting for transfers between devices: 40.8 us -> none  [body(): lax.all_to_all(column_coeffs, 'tile', split_axis=2, concat_axis=1, tiled=...]
    pallas_call x0 -> x6, Pallas kernels: none -> 37 us  [the longest x1 17.8 us: run_update(): pl.pallas_call(functools.partial(update_kernel, reach), out_shape=[jax.Sh...]
    ppermute x6 -> x15, starting transfers between devices: 14.5 us -> 39.2 us  [the longest x11 29.9 us: passed_along(): return lax.ppermute(x, 'tile', pairs)]
    all_to_all x1 -> x0, starting transfers between devices: 22 us -> none  [body(): lax.all_to_all(column_coeffs, 'tile', split_axis=2, concat_axis=1, tiled=...]
    another operation x2 -> x0, loops' own time: 17.2 us -> none  [the longest x1 10.2 us: body(): lax.map(extract, (frame_table[:, 0], frame_table[:, 1], frame_table[:, 2]))]
  transfers between devices with their start and end apart: 7 -> 15, of which waited for: 4 -> 5; matrix products, arithmetic and copies ran while one was open for 1% -> 3% of each run, Pallas kernels for 0% -> 9%
where the time goes in v1:
time: 95.9 us; the launch traced here: 94.1 us
  starting transfers between devices  39.2 us (41%)
  Pallas kernels  37 us (39%)
  waiting for transfers between devices  11.6 us (12%)
  local copies, waits for them, and re-layouts  4.18 us (4%)
  between operations  1.67 us (2%)
    ppermute x11, starting transfers between devices, passed_along(): return lax.ppermute(x, 'tile', pairs)  29.9 us
    pallas_call x1, Pallas kernels, run_update(): pl.pallas_call(functools.partial(update_kernel, reach), out_shape=[jax.Sh...  17.8 us
    pallas_call x1, Pallas kernels, run_phase(): pl.pallas_call(phase_kernel, out_shape=jax.ShapeDtypeStruct((angles, stri...  10.8 us
    ppermute x4, starting transfers between devices, entering_values(): lax.ppermute(jnp.stack([head, tail]), 'tile', [(i, i ^ width) for i in ra...  9.29 us
    ppermute x4, waiting for transfers between devices, entering_values(): lax.ppermute(jnp.stack([head, tail]), 'tile', [(i, i ^ width) for i in ra...  5.98 us
    pallas_call x3, Pallas kernels, extract(): pl.pallas_call(extract_kernel, out_shape=jax.ShapeDtypeStruct((caps, 2, s...  5.89 us
    ppermute x11, waiting for transfers between devices, passed_along(): return lax.ppermute(x, 'tile', pairs)  5.65 us
    pallas_call x1, Pallas kernels, run_frames(): pl.pallas_call(functools.partial(frame_kernel, reach, center), out_shape=...  2.5 us
  transfers between devices with their start and end apart: 15, of which 5 were waited for; matrix products, arithmetic and copies ran while one was open for 3% of the time, Pallas kernels for 9%

profile of v1, /device:TPU:0, one launch (start us, length us, event | category | flops | bytes accessed | tf_op | source)
XLA Modules:
  0.0 94.1 jit_solution(7782202149276662500)
XLA Ops:
  0.6 0.0 copy-start.10
  1.3 0.8 reshape.427
  2.1 0.1 pad_add_fusion.1.tab
  2.2 4.9 %collective-permute-start.2 = (s32[7]{0:T(128)S(1)}, s32[7]{0:T(128)S(1)}, u32[]{:S(2)}, u32[]{:S(2)}) collective-permute-start(s32[7]{0:T(128)S(1)} %pad_add_fusion.1.tab), channel_id=1, source_target_pairs={{0,2},{1,3},{2,4},{3,5},{4,6},{5,7},{6,8},{7,9},{8,10},{9,11},{10,... | collective-permute-start | bytes 92 | tf_op jit(solution)/shard_map/ppermute | solution.py:538
  7.0 1.9 %extract.3 = bf16[2,2,128,256]{3,2,1,0:T(8,128)(2,1)S(1)} custom-call(s32[7]{0:T(128)S(1)} %pad_add_fusion.1.tab, f32[2,2,128,2048]{3,2,1,0:T(8,128)} %field.7), custom_call_target="tpu_custom_call" | custom-call | tf_op jit(solution)/shard_map/extract/pallas_call | solution.py:108
  8.9 1.5 %collective-permute-start.6 = (bf16[2,2,128,256]{3,2,1,0:T(8,128)(2,1)S(1)}, bf16[2,2,128,256]{3,2,1,0:T(8,128)(2,1)S(1)}, u32[]{:S(2)}, u32[]{:S(2)}) collective-permute-start(bf16[2,2,128,256]{3,2,1,0:T(8,128)(2,1)S(1)} %extract.3), channel_id=1, source_target_pairs={{0,1},{1,2},{2,3},{3,4},{4,5},{5,6},{6,7},{7,8},{8,9},{9,10},{10,1... | collective-permute-start | bytes 786440 | tf_op jit(solution)/shard_map/ppermute | solution.py:538
  10.4 0.0 copy-done.10
  10.4 4.0 %collective-permute-start.5 = (bf16[2,256,256]{2,1,0:T(8,128)(2,1)S(1)}, bf16[2,256,256]{2,1,0:T(8,128)(2,1)S(1)}, u32[]{:S(2)}, u32[]{:S(2)}) collective-permute-start(bf16[2,256,256]{2,1,0:T(8,128)(2,1)S(1)} %copy-done.10), channel_id=1, source_target_pairs={{0,1},{1,2},{2,3},{3,4},{4,5},{5,6},{6,7},{7,8},{8,9},{9,10},{10,1... | collective-permute-start | bytes 786440 | tf_op jit(solution)/shard_map/ppermute | solution.py:538
  14.4 0.0 collective-permute-done.2.tab
  14.4 2.0 %extract.5 = bf16[2,2,128,256]{3,2,1,0:T(8,128)(2,1)S(1)} custom-call(s32[7]{0:T(128)S(1)} %collective-permute-done.2.tab, f32[2,2,128,2048]{3,2,1,0:T(8,128)} %field.7), custom_call_target="tpu_custom_call" | custom-call | tf_op jit(solution)/shard_map/extract/pallas_call | solution.py:108
  16.4 0.0 copy-start.1
  16.4 1.4 %collective-permute-start.7 = (bf16[2,2,128,256]{3,2,1,0:T(8,128)(2,1)S(1)}, bf16[2,2,128,256]{3,2,1,0:T(8,128)(2,1)S(1)}, u32[]{:S(2)}, u32[]{:S(2)}) collective-permute-start(bf16[2,2,128,256]{3,2,1,0:T(8,128)(2,1)S(1)} %extract.5), channel_id=1, source_target_pairs={{1,0},{2,1},{3,2},{4,3},{5,4},{6,5},{7,6},{8,7},{9,8},{10,9},{11,1... | collective-permute-start | bytes 786440 | tf_op jit(solution)/shard_map/ppermute | solution.py:538
  17.9 3.0 %collective-permute-start.1 = (s32[7]{0:T(128)S(1)}, s32[7]{0:T(128)S(1)}, u32[]{:S(2)}, u32[]{:S(2)}) collective-permute-start(s32[7]{0:T(128)S(1)} %pad_add_fusion.1.tab), channel_id=1, source_target_pairs={{0,1},{1,2},{2,3},{3,4},{4,5},{5,6},{6,7},{7,8},{8,9},{9,10},{10,1... | collective-permute-start | bytes 92 | tf_op jit(solution)/shard_map/ppermute | solution.py:538
  20.9 1.3 %collective-permute-start = (s32[7]{0:T(128)S(1)}, s32[7]{0:T(128)S(1)}, u32[]{:S(2)}, u32[]{:S(2)}) collective-permute-start(s32[7]{0:T(128)S(1)} %pad_add_fusion.1.tab), channel_id=1, source_target_pairs={{1,0},{2,1},{3,2},{4,3},{5,4},{6,5},{7,6},{8,7},{9,8},{10,9},{11,1... | collective-permute-start | bytes 92 | tf_op jit(solution)/shard_map/ppermute | solution.py:538
  22.2 0.0 collective-permute-done.1.tab
  22.2 2.0 %extract.4.rest_1_ = bf16[2,2,128,256]{3,2,1,0:T(8,128)(2,1)S(1)} custom-call(s32[7]{0:T(128)S(1)} %collective-permute-done.1.tab, f32[2,2,128,2048]{3,2,1,0:T(8,128)} %field.7), custom_call_target="tpu_custom_call" | custom-call | tf_op jit(solution)/shard_map/extract/pallas_call | solution.py:108
  24.2 0.0 collective-permute-done.6.rest_0_
  24.3 0.0 collective-permute-done.5.measured
  24.3 0.0 collective-permute-done.7.rest_2_
  24.3 2.5 %frames.1 = (bf16[2,2,16,256]{3,2,1,0:T(8,128)(2,1)S(1)}, bf16[2,2,144,256]{3,2,1,0:T(8,128)(2,1)S(1)}, f32[2,2,144,256]{3,2,1,0:T(8,128)}, bf16[2,2,144,256]{3,2,1,0:T(8,128)(2,1)S(1)}) custom-call(s32[7]{0:T(128)S(1)} %collective-permute-done.1.tab, f32[2,256,256]{2,1,0:T(8,128)} %probe.1, bf16[2,256,256]{2,1,0:T(8,128)(2,1)S(1)} %collective-permute-done.5.measured, ...), custom_call_target="tpu_custom_call" | custom-call | tf_op jit(solution)/shard_map/frames/pallas_call | solution.py:206
  26.8 1.3 %collective-permute-start.9 = (bf16[2,2,144,256]{3,2,1,0:T(8,128)(2,1)S(1)}, bf16[2,2,144,256]{3,2,1,0:T(8,128)(2,1)S(1)}, u32[]{:S(2)}, u32[]{:S(2)}) collective-permute-start(bf16[2,2,144,256]{3,2,1,0:T(8,128)(2,1)S(1)} %get-tuple-element.12), channel_id=1, source_target_pairs={{1,0},{2,1},{3,2},{4,3},{5,4},{6,5},{7,6},{8,7},{9,8},{10,9},{11,1... | collective-permute-start | bytes 884744 | tf_op jit(solution)/shard_map/ppermute | solution.py:538
  28.1 5.8 %collective-permute-start.10 = (bf16[2,2,144,256]{3,2,1,0:T(8,128)(2,1)S(1)}, bf16[2,2,144,256]{3,2,1,0:T(8,128)(2,1)S(1)}, u32[]{:S(2)}, u32[]{:S(2)}) collective-permute-start(bf16[2,2,144,256]{3,2,1,0:T(8,128)(2,1)S(1)} %get-tuple-element.14), channel_id=1, source_target_pairs={{0,1},{1,2},{2,3},{3,4},{4,5},{5,6},{6,7},{7,8},{8,9},{9,10},{10,1... | collective-permute-start | bytes 884744 | tf_op jit(solution)/shard_map/ppermute | solution.py:538
  33.8 1.1 %fusion = (f32[2,2,1,2048]{3,2,1,0:T(1,128)S(1)}, f32[2,2,1,2048]{3,2,1,0:T(1,128)S(1)}) fusion(f32[2,2,128,2048]{3,2,1,0:T(8,128)} %field.7), kind=kLoop, calls=%fused_computation.24 | loop fusion | bytes 131072 | tf_op jit(solution)/shard_map/slice | solution.py:585
  34.9 1.3 %collective-permute-start.4 = (f32[2,2,1,2048]{3,2,1,0:T(1,128)S(1)}, f32[2,2,1,2048]{3,2,1,0:T(1,128)S(1)}, u32[]{:S(2)}, u32[]{:S(2)}) collective-permute-start(f32[2,2,1,2048]{3,2,1,0:T(1,128)S(1)} %get-tuple-element.20), channel_id=1, source_target_pairs={{1,0},{2,1},{3,2},{4,3},{5,4},{6,5},{7,6},{8,7},{9,8},{10,9},{11,1... | collective-permute-start | bytes 98312 | tf_op jit(solution)/shard_map/ppermute | solution.py:538
  36.2 4.3 %collective-permute-start.3 = (f32[2,2,1,2048]{3,2,1,0:T(1,128)S(1)}, f32[2,2,1,2048]{3,2,1,0:T(1,128)S(1)}, u32[]{:S(2)}, u32[]{:S(2)}) collective-permute-start(f32[2,2,1,2048]{3,2,1,0:T(1,128)S(1)} %get-tuple-element.21), channel_id=1, source_target_pairs={{0,1},{1,2},{2,3},{3,4},{4,5},{5,6},{6,7},{7,8},{8,9},{9,10},{10,1... | collective-permute-start | bytes 98312 | tf_op jit(solution)/shard_map/ppermute | solution.py:538
  40.5 0.1 fusion.1
  40.5 0.0 collective-permute-done
  40.5 1.3 %collective-permute-start.8 = (bf16[2,2,16,256]{3,2,1,0:T(8,128)(2,1)S(1)}, bf16[2,2,16,256]{3,2,1,0:T(8,128)(2,1)S(1)}, u32[]{:S(2)}, u32[]{:S(2)}) collective-permute-start(bf16[2,2,16,256]{3,2,1,0:T(8,128)(2,1)S(1)} %get-tuple-element.11), channel_id=1, source_target_pairs={{2,0},{3,1},{4,2},{5,3},{6,4},{7,5},{8,6},{9,7},{10,8},{11,9},{12,... | collective-permute-start | bytes 98312 | tf_op jit(solution)/shard_map/ppermute | solution.py:538
  41.9 0.0 collective-permute-done.4.bottom
  41.9 0.0 collective-permute-done.3.top
  41.9 5.6 %collective-permute-done.8.rest_0_ = bf16[2,2,16,256]{3,2,1,0:T(8,128)(2,1)S(1)} collective-permute-done((bf16[2,2,16,256]{3,2,1,0:T(8,128)(2,1)S(1)}, bf16[2,2,16,256]{3,2,1,0:T(8,128)(2,1)S(1)}, u32[]{:S(2)}, u32[]{:S(2)}) %collective-permute-start.8) | collective-permute-done | bytes 32800 | tf_op jit(solution)/shard_map/ppermute | solution.py:538
  47.5 0.0 collective-permute-done.9.rest_1_
  47.5 0.0 collective-permute-done.10.rest_3_
  47.5 0.0 copy-done.1
  47.5 0.0 copy-start
  47.5 1.1 %copy-done = f32[2,2,144,256]{3,2,1,0:T(8,128)S(1)} copy-done((f32[2,2,144,256]{3,2,1,0:T(8,128)S(1)}, f32[2,2,144,256]{3,2,1,0:T(8,128)}, u32[]{:S(2)}) %copy-start) | copy-done | bytes 589848
  48.6 0.0 copy-start.9
  48.6 0.0 copy-start.8
  48.6 0.0 copy-start.7
  48.6 0.0 copy-start.6
  48.6 0.0 copy-start.2
  48.6 0.0 copy-start.3
  48.6 0.0 copy-start.4
  48.6 17.8 %update.1 = (f32[2,2,128,2048]{3,2,1,0:T(8,128)}, f32[2,128,2048]{2,1,0:T(8,128)}, f32[2,8,2048]{2,1,0:T(8,128)S(1)}, f32[2,8,2048]{2,1,0:T(8,128)S(1)}, f32[2,2,2048]{2,1,0:T(2,128)S(1)}) custom-call(s32[4,7]{1,0:T(4,128)S(1)} %pad_add_fusion.tabs, f32[2,2,128,2048]{3,2,1,0:T(8,128)} %field.7, f32[2,2,1,2048]{3,2,1,0:T(1,128)S(1)} %collective-permute-done.3.top, ...), custom_call_target="tpu_custom_call" | custom-call | tf_op jit(solution)/shard_map/update/pallas_call | solution.py:422
  66.5 2.0 %collective-permute-start.11 = (f32[2,2,2048]{2,1,0:T(2,128)S(1)}, f32[2,2,2048]{2,1,0:T(2,128)S(1)}, u32[]{:S(2)}, u32[]{:S(2)}) collective-permute-start(f32[2,2,2048]{2,1,0:T(2,128)S(1)} %get-tuple-element.19), channel_id=1, source_target_pairs={{0,1},{1,0},{2,3},{3,2},{4,5},{5,4},{6,7},{7,6},{8,9},{9,8},{10,11... | collective-permute-start | bytes 98312 | tf_op jit(solution)/shard_map/ppermute | solution.py:550
  68.5 0.9 collective-permute-done.11
  69.4 0.0 copy-done.9
  69.4 2.9 %collective-permute-start.12 = (f32[2,2,2048]{2,1,0:T(2,128)S(1)}, f32[2,2,2048]{2,1,0:T(2,128)S(1)}, u32[]{:S(2)}, u32[]{:S(2)}) collective-permute-start(f32[2,2,2048]{2,1,0:T(2,128)S(1)} %pad_maximum_fusion), channel_id=1, source_target_pairs={{0,2},{1,3},{2,0},{3,1},{4,6},{5,7},{6,4},{7,5},{8,10},{9,11},{10,... | collective-permute-start | bytes 98312 | tf_op jit(solution)/shard_map/ppermute | solution.py:550
  72.3 1.9 %collective-permute-done.12 = f32[2,2,2048]{2,1,0:T(2,128)S(1)} collective-permute-done((f32[2,2,2048]{2,1,0:T(2,128)S(1)}, f32[2,2,2048]{2,1,0:T(2,128)S(1)}, u32[]{:S(2)}, u32[]{:S(2)}) %collective-permute-start.12) | collective-permute-done | bytes 32800 | tf_op jit(solution)/shard_map/ppermute | solution.py:550
  74.2 0.0 copy-done.8
  74.2 1.7 %collective-permute-start.13 = (f32[2,2,2048]{2,1,0:T(2,128)S(1)}, f32[2,2,2048]{2,1,0:T(2,128)S(1)}, u32[]{:S(2)}, u32[]{:S(2)}) collective-permute-start(f32[2,2,2048]{2,1,0:T(2,128)S(1)} %pad_maximum_fusion.1), channel_id=1, source_target_pairs={{0,4},{1,5},{2,6},{3,7},{4,0},{5,1},{6,2},{7,3},{8,12},{9,13},{10,... | collective-permute-start | bytes 98312 | tf_op jit(solution)/shard_map/ppermute | solution.py:550
  75.9 2.3 %collective-permute-done.13 = f32[2,2,2048]{2,1,0:T(2,128)S(1)} collective-permute-done((f32[2,2,2048]{2,1,0:T(2,128)S(1)}, f32[2,2,2048]{2,1,0:T(2,128)S(1)}, u32[]{:S(2)}, u32[]{:S(2)}) %collective-permute-start.13) | collective-permute-done | bytes 32800 | tf_op jit(solution)/shard_map/ppermute | solution.py:550
  78.2 0.0 copy-done.7
  78.3 2.7 %collective-permute-start.14 = (f32[2,2,2048]{2,1,0:T(2,128)S(1)}, f32[2,2,2048]{2,1,0:T(2,128)S(1)}, u32[]{:S(2)}, u32[]{:S(2)}) collective-permute-start(f32[2,2,2048]{2,1,0:T(2,128)S(1)} %pad_maximum_fusion.2), channel_id=1, source_target_pairs={{0,8},{1,9},{2,10},{3,11},{4,12},{5,13},{6,14},{7,15},{8,0},{9,1},... | collective-permute-start | bytes 98312 | tf_op jit(solution)/shard_map/ppermute | solution.py:550
  81.0 1.2 %constant_dynamic-slice_fusion.7 = (f32[1,2048]{1,0:T(1,128)S(1)}, f32[1,2048]{1,0:T(1,128)S(1)}, f32[1,2048]{1,0:T(1,128)S(1)}, f32[1,2048]{1,0:T(1,128)S(1)}, ...) fusion(f32[17,2048]{1,0:T(8,128)} %constant.58.clone, ...), kind=kLoop, calls=%fused_computation.22 | loop fusion | bytes 131104 | tf_op jit(solution)/shard_map/dynamic_slice | solution.py:547
  82.2 0.9 collective-permute-done.14
  83.2 0.0 copy-done.5
  83.2 0.0 copy-done.6
  83.2 0.1 multiply_add_fusion
  83.2 0.1 multiply_add_fusion.1
  83.3 0.0 copy-done.2
  83.3 0.0 copy-done.3
  83.3 0.0 copy-done.4
  83.3 10.8 %phase.1 = f32[2,128,2048]{2,1,0:T(8,128)} custom-call(f32[2,128,2048]{2,1,0:T(8,128)} %get-tuple-element.16.inner, f32[2,8,2048]{2,1,0:T(8,128)S(1)} %get-tuple-element.17.carry_y, f32[2,8,2048]{2,1,0:T(8,128)S(1)} %get-tuple-element.18.carry_z, f32[2,2,2048]{2,1,0:T(2,128)S(1)} %pad_maximum_fusion.3.enter, f32[5,2048]{1,0:T(8,128)S(1)} %copy-done.1, ...), custom_call_target="tpu_custom_call" | custom-call | tf_op jit(solution)/shard_map/phase/pallas_call | solution.py:519
  (9 shorter events, 0.2 us)
Async XLA Ops:
  0.6 9.8 %copy-start.10 = (bf16[2,256,256]{2,1,0:T(8,128)(2,1)S(1)}, bf16[2,256,256]{2,1,0:T(8,128)(2,1)}, u32[]{:S(2)}) copy-start(bf16[2,256,256]{2,1,0:T(8,128)(2,1)} %param.17) | copy-start | bytes 786436
  2.2 12.2 %collective-permute-start.2 = (s32[7]{0:T(128)S(1)}, s32[7]{0:T(128)S(1)}, u32[]{:S(2)}, u32[]{:S(2)}) collective-permute-start(s32[7]{0:T(128)S(1)} %pad_add_fusion.1.tab), channel_id=1, source_target_pairs={{0,2},{1,3},{2,4},{3,5},{4,6},{5,7},{6,8},{7,9},{8,10},{9,11},{10,... | collective-permute-start | bytes 92 | tf_op jit(solution)/shard_map/ppermute | solution.py:538
  8.9 15.3 %collective-permute-start.6 = (bf16[2,2,128,256]{3,2,1,0:T(8,128)(2,1)S(1)}, bf16[2,2,128,256]{3,2,1,0:T(8,128)(2,1)S(1)}, u32[]{:S(2)}, u32[]{:S(2)}) collective-permute-start(bf16[2,2,128,256]{3,2,1,0:T(8,128)(2,1)S(1)} %extract.3), channel_id=1, source_target_pairs={{0,1},{1,2},{2,3},{3,4},{4,5},{5,6},{6,7},{7,8},{8,9},{9,10},{10,1... | collective-permute-start | bytes 786440 | tf_op jit(solution)/shard_map/ppermute | solution.py:538
  10.4 13.9 %collective-permute-start.5 = (bf16[2,256,256]{2,1,0:T(8,128)(2,1)S(1)}, bf16[2,256,256]{2,1,0:T(8,128)(2,1)S(1)}, u32[]{:S(2)}, u32[]{:S(2)}) collective-permute-start(bf16[2,256,256]{2,1,0:T(8,128)(2,1)S(1)} %copy-done.10), channel_id=1, source_target_pairs={{0,1},{1,2},{2,3},{3,4},{4,5},{5,6},{6,7},{7,8},{8,9},{9,10},{10,1... | collective-permute-start | bytes 786440 | tf_op jit(solution)/shard_map/ppermute | solution.py:538
  16.4 31.1 %copy-start.1 = (f32[5,2048]{1,0:T(8,128)S(1)}, f32[5,2048]{1,0:T(8,128)}, u32[]{:S(2)}) copy-start(f32[5,2048]{1,0:T(8,128)} %constant.54.clone.scan) | copy-start | bytes 122884
  16.4 7.8 %collective-permute-start.7 = (bf16[2,2,128,256]{3,2,1,0:T(8,128)(2,1)S(1)}, bf16[2,2,128,256]{3,2,1,0:T(8,128)(2,1)S(1)}, u32[]{:S(2)}, u32[]{:S(2)}) collective-permute-start(bf16[2,2,128,256]{3,2,1,0:T(8,128)(2,1)S(1)} %extract.5), channel_id=1, source_target_pairs={{1,0},{2,1},{3,2},{4,3},{5,4},{6,5},{7,6},{8,7},{9,8},{10,9},{11,1... | collective-permute-start | bytes 786440 | tf_op jit(solution)/shard_map/ppermute | solution.py:538
  17.9 4.3 %collective-permute-start.1 = (s32[7]{0:T(128)S(1)}, s32[7]{0:T(128)S(1)}, u32[]{:S(2)}, u32[]{:S(2)}) collective-permute-start(s32[7]{0:T(128)S(1)} %pad_add_fusion.1.tab), channel_id=1, source_target_pairs={{0,1},{1,2},{2,3},{3,4},{4,5},{5,6},{6,7},{7,8},{8,9},{9,10},{10,1... | collective-permute-start | bytes 92 | tf_op jit(solution)/shard_map/ppermute | solution.py:538
  20.9 19.6 %collective-permute-start = (s32[7]{0:T(128)S(1)}, s32[7]{0:T(128)S(1)}, u32[]{:S(2)}, u32[]{:S(2)}) collective-permute-start(s32[7]{0:T(128)S(1)} %pad_add_fusion.1.tab), channel_id=1, source_target_pairs={{1,0},{2,1},{3,2},{4,3},{5,4},{6,5},{7,6},{8,7},{9,8},{10,9},{11,1... | collective-permute-start | bytes 92 | tf_op jit(solution)/shard_map/ppermute | solution.py:538
  26.8 20.7 %collective-permute-start.9 = (bf16[2,2,144,256]{3,2,1,0:T(8,128)(2,1)S(1)}, bf16[2,2,144,256]{3,2,1,0:T(8,128)(2,1)S(1)}, u32[]{:S(2)}, u32[]{:S(2)}) collective-permute-start(bf16[2,2,144,256]{3,2,1,0:T(8,128)(2,1)S(1)} %get-tuple-element.12), channel_id=1, source_target_pairs={{1,0},{2,1},{3,2},{4,3},{5,4},{6,5},{7,6},{8,7},{9,8},{10,9},{11,1... | collective-permute-start | bytes 884744 | tf_op jit(solution)/shard_map/ppermute | solution.py:538
  28.1 19.4 %collective-permute-start.10 = (bf16[2,2,144,256]{3,2,1,0:T(8,128)(2,1)S(1)}, bf16[2,2,144,256]{3,2,1,0:T(8,128)(2,1)S(1)}, u32[]{:S(2)}, u32[]{:S(2)}) collective-permute-start(bf16[2,2,144,256]{3,2,1,0:T(8,128)(2,1)S(1)} %get-tuple-element.14), channel_id=1, source_target_pairs={{0,1},{1,2},{2,3},{3,4},{4,5},{5,6},{6,7},{7,8},{8,9},{9,10},{10,1... | collective-permute-start | bytes 884744 | tf_op jit(solution)/shard_map/ppermute | solution.py:538
  34.9 7.0 %collective-permute-start.4 = (f32[2,2,1,2048]{3,2,1,0:T(1,128)S(1)}, f32[2,2,1,2048]{3,2,1,0:T(1,128)S(1)}, u32[]{:S(2)}, u32[]{:S(2)}) collective-permute-start(f32[2,2,1,2048]{3,2,1,0:T(1,128)S(1)} %get-tuple-element.20), channel_id=1, source_target_pairs={{1,0},{2,1},{3,2},{4,3},{5,4},{6,5},{7,6},{8,7},{9,8},{10,9},{11,1... | collective-permute-start | bytes 98312 | tf_op jit(solution)/shard_map/ppermute | solution.py:538
  36.2 5.7 %collective-permute-start.3 = (f32[2,2,1,2048]{3,2,1,0:T(1,128)S(1)}, f32[2,2,1,2048]{3,2,1,0:T(1,128)S(1)}, u32[]{:S(2)}, u32[]{:S(2)}) collective-permute-start(f32[2,2,1,2048]{3,2,1,0:T(1,128)S(1)} %get-tuple-element.21), channel_id=1, source_target_pairs={{0,1},{1,2},{2,3},{3,4},{4,5},{5,6},{6,7},{7,8},{8,9},{9,10},{10,1... | collective-permute-start | bytes 98312 | tf_op jit(solution)/shard_map/ppermute | solution.py:538
  40.5 7.0 %collective-permute-start.8 = (bf16[2,2,16,256]{3,2,1,0:T(8,128)(2,1)S(1)}, bf16[2,2,16,256]{3,2,1,0:T(8,128)(2,1)S(1)}, u32[]{:S(2)}, u32[]{:S(2)}) collective-permute-start(bf16[2,2,16,256]{3,2,1,0:T(8,128)(2,1)S(1)} %get-tuple-element.11), channel_id=1, source_target_pairs={{2,0},{3,1},{4,2},{5,3},{6,4},{7,5},{8,6},{9,7},{10,8},{11,9},{12,... | collective-permute-start | bytes 98312 | tf_op jit(solution)/shard_map/ppermute | solution.py:538
  47.5 1.1 %copy-start = (f32[2,2,144,256]{3,2,1,0:T(8,128)S(1)}, f32[2,2,144,256]{3,2,1,0:T(8,128)}, u32[]{:S(2)}) copy-start(f32[2,2,144,256]{3,2,1,0:T(8,128)} %get-tuple-element.13.rest_2_) | copy-start | bytes 1769476
  48.6 20.8 %copy-start.9 = (f32[2048]{0:T(1024)S(1)}, f32[2048]{0:T(1024)}, u32[]{:S(2)}) copy-start(f32[2048]{0:T(1024)} %constant.68) | copy-start | bytes 24580
  48.6 25.6 %copy-start.8 = (f32[2048]{0:T(1024)S(1)}, f32[2048]{0:T(1024)}, u32[]{:S(2)}) copy-start(f32[2048]{0:T(1024)} %constant.70) | copy-start | bytes 24580
  48.6 29.6 %copy-start.7 = (f32[2048]{0:T(1024)S(1)}, f32[2048]{0:T(1024)}, u32[]{:S(2)}) copy-start(f32[2048]{0:T(1024)} %constant.72) | copy-start | bytes 24580
  48.6 34.6 %copy-start.5 = (f32[2048]{0:T(1024)S(1)}, f32[2048]{0:T(1024)}, u32[]{:S(2)}) copy-start(f32[2048]{0:T(1024)} %constant.76) | copy-start | bytes 24580
  48.6 34.6 %copy-start.6 = (f32[2048]{0:T(1024)S(1)}, f32[2048]{0:T(1024)}, u32[]{:S(2)}) copy-start(f32[2048]{0:T(1024)} %constant.74) | copy-start | bytes 24580
  48.6 34.7 %copy-start.2 = (f32[16,2048]{1,0:T(8,128)S(1)}, f32[16,2048]{1,0:T(8,128)}, u32[]{:S(2)}) copy-start(f32[16,2048]{1,0:T(8,128)} %constant.55.clone.powers) | copy-start | bytes 393220
  48.6 34.7 %copy-start.3 = (f32[8,2048]{1,0:T(8,128)S(1)}, f32[8,2048]{1,0:T(8,128)}, u32[]{:S(2)}) copy-start(f32[8,2048]{1,0:T(8,128)} %constant.57.clone.segs_back) | copy-start | bytes 196612
  48.6 34.7 %copy-start.4 = (f32[8,2048]{1,0:T(8,128)S(1)}, f32[8,2048]{1,0:T(8,128)}, u32[]{:S(2)}) copy-start(f32[8,2048]{1,0:T(8,128)} %constant.56.clone.segs) | copy-start | bytes 196612
  66.5 2.9 %collective-permute-start.11 = (f32[2,2,2048]{2,1,0:T(2,128)S(1)}, f32[2,2,2048]{2,1,0:T(2,128)S(1)}, u32[]{:S(2)}, u32[]{:S(2)}) collective-permute-start(f32[2,2,2048]{2,1,0:T(2,128)S(1)} %get-tuple-element.19), channel_id=1, source_target_pairs={{0,1},{1,0},{2,3},{3,2},{4,5},{5,4},{6,7},{7,6},{8,9},{9,8},{10,11... | collective-permute-start | bytes 98312 | tf_op jit(solution)/shard_map/ppermute | solution.py:550
  69.4 4.8 %collective-permute-start.12 = (f32[2,2,2048]{2,1,0:T(2,128)S(1)}, f32[2,2,2048]{2,1,0:T(2,128)S(1)}, u32[]{:S(2)}, u32[]{:S(2)}) collective-permute-start(f32[2,2,2048]{2,1,0:T(2,128)S(1)} %pad_maximum_fusion), channel_id=1, source_target_pairs={{0,2},{1,3},{2,0},{3,1},{4,6},{5,7},{6,4},{7,5},{8,10},{9,11},{10,... | collective-permute-start | bytes 98312 | tf_op jit(solution)/shard_map/ppermute | solution.py:550
  74.2 4.0 %collective-permute-start.13 = (f32[2,2,2048]{2,1,0:T(2,128)S(1)}, f32[2,2,2048]{2,1,0:T(2,128)S(1)}, u32[]{:S(2)}, u32[]{:S(2)}) collective-permute-start(f32[2,2,2048]{2,1,0:T(2,128)S(1)} %pad_maximum_fusion.1), channel_id=1, source_target_pairs={{0,4},{1,5},{2,6},{3,7},{4,0},{5,1},{6,2},{7,3},{8,12},{9,13},{10,... | collective-permute-start | bytes 98312 | tf_op jit(solution)/shard_map/ppermute | solution.py:550
  78.3 4.9 %collective-permute-start.14 = (f32[2,2,2048]{2,1,0:T(2,128)S(1)}, f32[2,2,2048]{2,1,0:T(2,128)S(1)}, u32[]{:S(2)}, u32[]{:S(2)}) collective-permute-start(f32[2,2,2048]{2,1,0:T(2,128)S(1)} %pad_maximum_fusion.2), channel_id=1, source_target_pairs={{0,8},{1,9},{2,10},{3,11},{4,12},{5,13},{6,14},{7,15},{8,0},{9,1},... | collective-permute-start | bytes 98312 | tf_op jit(solution)/shard_map/ppermute | solution.py:550

commit v2 on v1

--- a/solution.py
+++ b/solution.py
@@ -22,7 +22,17 @@
 VMEM_SPEC = pl.BlockSpec(memory_space=pltpu.VMEM)
 SMEM_SPEC = pl.BlockSpec(memory_space=pltpu.SMEM)
 ANY_SPEC = pl.BlockSpec(memory_space=pl.ANY)
-PARAMS = pltpu.CompilerParams(vmem_limit_bytes=52 * 1024 * 1024)
+PARAMS = pltpu.CompilerParams(vmem_limit_bytes=26 * 1024 * 1024)
+UPDATE_PARAMS = pltpu.CompilerParams(vmem_limit_bytes=44 * 1024 * 1024)
+PHASE_PARAMS = pltpu.CompilerParams(vmem_limit_bytes=46 * 1024 * 1024)
+DIGIT = 64
+CODE_ROWS = 16
+FIELDS = 4
+BATCH = 8
+
+
+def cost(micros):
+    return pl.CostEstimate(flops=0, bytes_accessed=int(micros * 3.0e6), transcendentals=0)
 
 
 def split_table(table):
@@ -64,7 +74,14 @@
             log_root[None, :] * np.asarray(exponents)[:, None] > -80.0
         )
 
-    scan = np.concatenate([power([1, steps, 2 * steps, 4 * steps]), (root / (1 - root * root))[None]])
+    scan = np.concatenate(
+        [
+            power([1, steps, 2 * steps, 4 * steps]),
+            (2 * root / (1 - root * root))[None],
+            (1 / root)[None],
+            power([strip]),
+        ]
+    )
     inner = power(np.arange(1, steps + 1))
     segs = power(steps * np.arange(SEG))
     strips = power(strip * np.arange(devices + 1))
@@ -77,57 +94,147 @@
     return jnp.minimum(jnp.maximum(value, 0), top)
 
 
-def extract_kernel(tab, field, out, raw, sems):
-    caps, _, strip, frame = out.shape
+def window_copies(tab, field, raw, sems):
+    caps, wide = raw.shape[0], raw.shape[3]
+    frame = wide - LANES
     angles, grid = field.shape[0], field.shape[3]
-    wide = frame + LANES
     copies = []
-    shifts = []
     for slot in range(caps):
-        column = clip(tab[3 * slot + 1], grid - frame)
-        angle = clip(tab[3 * slot + 2], angles - 1)
+        column = clip(tab(slot, 1), grid - frame)
+        angle = clip(tab(slot, 2), angles - 1)
         block = jnp.minimum(column // LANES, (grid - wide) // LANES)
-        shifts.append(column - block * LANES)
         start = pl.multiple_of(block * LANES, LANES)
-        copies.append(
-            pltpu.make_async_copy(
-                field.at[angle, :, :, pl.ds(start, wide)], raw.at[slot], sems.at[slot]
-            )
-        )
-    for copy in copies:
+        copy = pltpu.make_async_copy(
+            field.at[angle, :, :, pl.ds(start, wide)], raw.at[slot], sems.at[slot]
+        )
         copy.start()
+        copies.append((copy, lax.rem(wide - (column - block * LANES), wide)))
+    return copies
+
+
+def window_values(copies, raw, slot, part):
+    wide = raw.shape[3]
+    return pltpu.roll(raw[slot, part], copies[slot][1], axis=1)[:, : wide - LANES].astype(bf16)
+
+
+def decoded(package, ints):
+    rows = package.shape[0]
+    digits = package[rows - CODE_ROWS :, :LANES].astype(f32)
+    ints[...] = (digits[0:1] * DIGIT + digits[1:2]).astype(jnp.int32)
+    return lambda slot, i: ints[0, slot * FIELDS + i]
+
+
+def plain(tab):
+    return lambda slot, i: tab[slot, i]
+
+
+def package_rows(caps, strip, frame, angles, grid):
+    windows = caps * 2 * strip
+    halo = angles * 2 * grid // frame
+    return windows, halo
+
+
+def pack_kernel(caps, tab, field, out, raw, last_rows, halo_buf, sems, row_sem):
+    frame = out.shape[1]
+    angles, _, strip, grid = field.shape
+    at_halo, halo_rows = package_rows(caps, strip, frame, angles, grid)
+    copies = window_copies(plain(tab), field, raw, sems)
+    row_copy = pltpu.make_async_copy(
+        field.at[:, :, pl.ds(strip - PAD, PAD), :], last_rows, row_sem.at[0]
+    )
+    row_copy.start()
+    place = lax.broadcasted_iota(jnp.int32, (CODE_ROWS, frame), 1)
+    row = lax.broadcasted_iota(jnp.int32, (CODE_ROWS, frame), 0)
+    high = jnp.zeros((CODE_ROWS, frame), jnp.int32)
+    low = jnp.zeros((CODE_ROWS, frame), jnp.int32)
     for slot in range(caps):
-        copies[slot].wait()
+        for i in range(FIELDS):
+            here = place == slot * FIELDS + i
+            high = jnp.where(here, tab[slot, i] // DIGIT, high)
+            low = jnp.where(here, lax.rem(tab[slot, i], DIGIT), low)
+    code = jnp.where(row == 0, high, jnp.where(row == 1, low, 0))
+    out[out.shape[0] - CODE_ROWS :] = code.astype(f32).astype(bf16)
+    row_copy.wait()
+    per_row = grid // frame
+    for a in range(angles):
         for part in range(2):
-            moved = pltpu.roll(raw[slot, part], lax.rem(wide - shifts[slot], wide), axis=1)
-            out[slot, part] = moved[:, :frame].astype(bf16)
-
-
-def extract(tab, field, caps, frame):
+            for k in range(per_row):
+                i = (a * 2 + part) * per_row + k
+                halo_buf[i : i + 1] = last_rows[a, part, PAD - 1 :, k * frame : (k + 1) * frame]
+    left_over = halo_buf[...]
+    for i in range(3):
+        digit = left_over.astype(bf16)
+        out[at_halo + i * halo_rows : at_halo + (i + 1) * halo_rows] = digit
+        left_over = left_over - digit.astype(f32)
+    for slot in range(caps):
+        copies[slot][0].wait()
+        for part in range(2):
+            at = (slot * 2 + part) * strip
+            out[at : at + strip] = window_values(copies, raw, slot, part)
+
+
+def pack(tab, field, caps, frame):
     angles, _, strip, grid = field.shape
+    at_halo, halo_rows = package_rows(caps, strip, frame, angles, grid)
     return pl.pallas_call(
-        extract_kernel,
-        out_shape=jax.ShapeDtypeStruct((caps, 2, strip, frame), bf16),
+        functools.partial(pack_kernel, caps),
+        out_shape=jax.ShapeDtypeStruct((at_halo + 3 * halo_rows + CODE_ROWS, frame), bf16),
         in_specs=[SMEM_SPEC, ANY_SPEC],
         out_specs=VMEM_SPEC,
         scratch_shapes=[
             pltpu.VMEM((caps, 2, strip, frame + LANES), f32),
+            pltpu.VMEM((angles, 2, PAD, grid), f32),
+            pltpu.VMEM((halo_rows, frame), f32),
+            pltpu.SemaphoreType.DMA((caps,)),
+            pltpu.SemaphoreType.DMA((1,)),
+        ],
+        compiler_params=PARAMS,
+        cost_estimate=cost(6),
+        name="pack",
+    )(tab, field)
+
+
+def extract_kernel(coded, tab, field, *rest):
+    raw, ints, sems = rest[-3:]
+    out = rest[0] if coded else rest[1]
+    read = decoded(tab, ints) if coded else plain(tab)
+    copies = window_copies(read, field, raw, sems)
+    for slot in range(out.shape[0]):
+        copies[slot][0].wait()
+        for part in range(2):
+            out[slot, part] = window_values(copies, raw, slot, part)
+
+
+def extract(tab, coded, field, caps, frame, package=None):
+    angles, _, strip, grid = field.shape
+    window = jax.ShapeDtypeStruct((caps, 2, strip, frame), bf16)
+    through = [] if coded else [package]
+    out = pl.pallas_call(
+        functools.partial(extract_kernel, coded),
+        out_shape=[window] + [jax.ShapeDtypeStruct(x.shape, x.dtype) for x in through],
+        in_specs=[VMEM_SPEC if coded else SMEM_SPEC, ANY_SPEC] + [ANY_SPEC] * len(through),
+        out_specs=[VMEM_SPEC] + [ANY_SPEC] * len(through),
+        input_output_aliases={2: 1} if through else {},
+        scratch_shapes=[
+            pltpu.VMEM((caps, 2, strip, frame + LANES), f32),
+            pltpu.VMEM((1, LANES), jnp.int32),
             pltpu.SemaphoreType.DMA((caps,)),
         ],
         compiler_params=PARAMS,
+        cost_estimate=cost(2),
         name="extract",
-    )(tab, field)
-
-
-def frame_kernel(reach, center, tab, probe, measured, left, right, *rest):
-    windows = rest[: reach + 1]
-    first_piece = rest[reach + 1]
-    pieces = rest[reach + 2 : 2 * reach + 3]
-    window_buf, update_buf = rest[2 * reach + 3 :]
-    caps, frame = measured.shape[0], measured.shape[1]
-    strip = windows[0].shape[2]
+    )(tab, field, *through)
+    return out[0] if coded else out
+
+
+def frame_kernel(reach, package, measured, probe, left, right, *rest):
+    windows = rest[:reach]
+    pieces = rest[reach : 2 * reach + 1]
+    window_buf, update_buf, ints = rest[2 * reach + 1 :]
+    caps, _, strip, frame = windows[0].shape
+    read = decoded(package, ints)
     blocks = frame // LANES
-    count = tab[3 * caps]
+    count = read(0, 3)
     probe_re, probe_im = probe[0], probe[1]
     peak = jnp.max(probe_re * probe_re + probe_im * probe_im) + epsilon_term
     for slot in range(caps):
@@ -135,13 +242,18 @@
 
         @pl.when(slot < count)
         def _():
-            offset = clip(tab[3 * slot], strip - 1)
+            offset = clip(read(slot, 0), strip - 1)
             for j in range(reach + 1):
                 for part in range(2):
                     for k in range(blocks):
-                        window_buf[part, k, j * strip : (j + 1) * strip] = windows[j][
-                            slot, part, :, k * LANES : (k + 1) * LANES
-                        ].astype(f32)
+                        lanes = slice(k * LANES, (k + 1) * LANES)
+                        at = (slot * 2 + part) * strip
+                        values = (
+                            windows[j - 1][slot, part, :, lanes]
+                            if j
+                            else package[at : at + strip, lanes]
+                        )
+                        window_buf[part, k, j * strip : (j + 1) * strip] = values.astype(f32)
             obj_re, obj_im = (
                 jnp.concatenate(
                     [window_buf[part, k, pl.ds(offset, frame), :] for k in range(blocks)], axis=1
@@ -165,7 +277,8 @@
             spec_re, spec_im = spectrum[:, :frame], spectrum[:, frame:]
             power = spec_re * spec_re + spec_im * spec_im
             factor = (
-                measured[slot].astype(f32) * lax.rsqrt(jnp.maximum(power, magnitude_floor**2)) - 1.0
+                measured[slot].astype(f32)
+                * lax.rsqrt(jnp.maximum(power, magnitude_floor**2)) - 1.0
             )
             change = jnp.concatenate(
                 [(spec_re * factor).astype(bf16), (spec_im * factor).astype(bf16)], axis=0
@@ -185,37 +298,34 @@
         for part in range(2):
             for k in range(blocks):
                 lanes = slice(k * LANES, (k + 1) * LANES)
-                first_piece[slot, part, :, lanes] = update_buf[part, k, 2 * PAD : 4 * PAD].astype(
-                    first_piece.dtype
-                )
                 for j in range(reach + 1):
                     pieces[j][slot, part, :, lanes] = update_buf[
                         part, k, j * strip + PAD : (j + 1) * strip + 3 * PAD
                     ].astype(pieces[j].dtype)
 
 
-def run_frames(tab, probe, measured, windows, center):
-    reach = len(windows) - 1
-    caps, frame = measured.shape[0], measured.shape[1]
-    strip = windows[0].shape[2]
+def run_frames(package, measured, probe, windows, center):
+    reach = len(windows)
+    caps, _, strip, frame = windows[0].shape
     left, right = fourier_blocks(frame)
     rows = (reach + 1) * strip
     piece = lambda j: jax.ShapeDtypeStruct(
         (caps, 2, strip + 2 * PAD, frame), f32 if j == center else bf16
     )
     return pl.pallas_call(
-        functools.partial(frame_kernel, reach, center),
-        out_shape=[jax.ShapeDtypeStruct((caps, 2, 2 * PAD, frame), bf16)]
-        + [piece(j) for j in range(reach + 1)],
-        in_specs=[SMEM_SPEC] + [VMEM_SPEC] * (5 + reach),
-        out_specs=[VMEM_SPEC] * (reach + 2),
+        functools.partial(frame_kernel, reach),
+        out_shape=[piece(j) for j in range(reach + 1)],
+        in_specs=[VMEM_SPEC] * (5 + reach),
+        out_specs=[VMEM_SPEC] * (reach + 1),
         scratch_shapes=[
             pltpu.VMEM((2, frame // LANES, rows, LANES), f32),
             pltpu.VMEM((2, frame // LANES, rows + 4 * PAD, LANES), f32),
+            pltpu.VMEM((1, LANES), jnp.int32),
         ],
         compiler_params=PARAMS,
+        cost_estimate=cost(5),
         name="frames",
-    )(tab, probe, measured, jnp.asarray(left), jnp.asarray(right), *windows)
+    )(package, measured, probe, jnp.asarray(left), jnp.asarray(right), *windows)
 
 
 def reversed_lanes(values):
@@ -233,17 +343,19 @@
     return both[:count] + both[count:] + jnp.dot(rows[:count], low, preferred_element_type=f32)
 
 
-def update_kernel(reach, tabs, field, top, bottom, scan, table_hbm, *rest):
-    first_piece = rest[0]
-    pieces = rest[1 : reach + 2]
-    updated, inner, carry_y, carry_z, ends = rest[reach + 2 : reach + 7]
-    ext, row_bond, source, rows_in, table, load_sems, store_sems, table_sems = rest[reach + 7 :]
+def update_kernel(reach, center, *refs):
+    tabs = refs[:reach]
+    field, package, halo, scan, segs, tables, *rest = refs[reach:]
+    tabs = tabs[:center] + (None,) + tabs[center:]
+    pieces = rest[: reach + 1]
+    updated, inner, carry_y, carry_z, ends = rest[reach + 1 : reach + 6]
+    ext, col_bond, source, edge, rows_in, ints, table, load_sems, store_sems, table_sems = rest[reach + 6 :]
     angles, _, strip, grid = field.shape
     blocks = grid // LANES
     half_blocks = blocks // 2
     half = grid // 2
     steps = strip // SEG
-    count = angles * strip
+    count = angles * strip + 2 * PAD
     caps = pieces[0].shape[0]
     frame = pieces[0].shape[3]
     frame_blocks = frame // LANES
@@ -265,7 +377,9 @@
         )
 
     def load_table(h, k):
-        return pltpu.make_async_copy(table_hbm.at[k, h], table.at[k, h], table_sems.at[k, h])
+        return pltpu.make_async_copy(
+            tables.at[0, k, h], table.at[k, h], table_sems.at[k, h]
+        )
 
     for a in range(angles):
         for b in range(blocks):
@@ -274,73 +388,104 @@
         for k in range(2):
             load_table(h, k).start()
 
+    halo_rows = halo.shape[0] // 3
+    top = sum(halo[i * halo_rows : (i + 1) * halo_rows].astype(f32) for i in range(3))
+    per_row = grid // frame
+    read = decoded(package, ints)
     for a in range(angles):
         for part in range(2):
             for b in range(blocks):
-                lanes = slice(b * LANES, (b + 1) * LANES)
-                ext[a, part, b, PAD - 1 : PAD, :] = top[a, part, :, lanes]
-                ext[a, part, b, PAD + strip : PAD + strip + 1, :] = bottom[a, part, :, lanes]
+                row = (a * 2 + part) * per_row + b // frame_blocks
+                lanes = slice(b % frame_blocks * LANES, (b % frame_blocks + 1) * LANES)
+                ext[a, part, b, PAD - 1 : PAD, :] = top[row : row + 1, lanes]
             ext[a, part, blocks] = jnp.zeros((strip + 2 * PAD, LANES), f32)
     for a in range(angles):
         for b in range(blocks):
             load(a, b).wait()
 
-    def add_piece(piece, tab_row, slot, first_row, rows):
-        @pl.when(slot < tabs[tab_row, 3 * caps])
+    rows = strip + 2 * PAD
+
+    def add_piece(piece, tab, slot):
+        @pl.when(slot < tab(0, 3))
         def _():
-            column = clip(tabs[tab_row, 3 * slot + 1], grid - frame)
-            angle = clip(tabs[tab_row, 3 * slot + 2], angles - 1)
+            column = clip(tab(slot, 1), grid - frame)
+            angle = clip(tab(slot, 2), angles - 1)
             block = jnp.minimum(column // LANES, blocks - frame_blocks - 1)
             shift = column - block * LANES
             for part in range(2):
-                values = piece[slot, part, :rows].astype(f32)
+                values = piece[slot, part].astype(f32)
                 values = jnp.concatenate([values, jnp.zeros((rows, LANES), f32)], axis=1)
                 values = pltpu.roll(values, shift, axis=1)
                 for k in range(frame_blocks + 1):
-                    spot = ext.at[angle, part, block + k, first_row : first_row + rows]
+                    spot = ext.at[angle, part, block + k]
                     spot[...] += values[:, k * LANES : (k + 1) * LANES]
 
     for slot in range(caps):
-        add_piece(first_piece, 0, slot, PAD + strip, PAD)
         for j in range(reach + 1):
-            add_piece(pieces[j], j + 1, slot, 0, strip + 2 * PAD)
+            add_piece(pieces[j], read if j == center else plain(tabs[j]), slot)
 
     for a in range(angles):
         for b in range(blocks):
             store(a, b).start()
 
-    lane = lax.broadcasted_iota(jnp.int32, (strip, LANES), 1)
-
-    def bond(re, im, power, re_to, im_to, power_to):
-        whole = power + power_to
-        guess = pl.reciprocal(whole, approx=True)
-        guess = guess * (2.0 - whole * guess)
-        return (re * im_to - im * re_to) * guess
-
-    def reach_right(now, after):
-        return pltpu.roll(jnp.where(lane == 0, after, now), LANES - 1, axis=1)
+    lane = lax.broadcasted_iota(jnp.int32, (SEG, LANES), 1)
+    sub = lax.broadcasted_iota(jnp.int32, (SEG, LANES), 0)
+
+    def power_of(re, im):
+        return re * re + (im * im + 0.5 * soften_term)
+
+    def bond(re, im, power, re_to, im_to):
+        return (re * im_to - im * re_to) * pl.reciprocal(
+            power + power_of(re_to, im_to), approx=True
+        )
 
     for a in range(angles):
-
-        def columns(b, before, a=a):
-            tall = strip + PAD
-            re, im = ext[a, 0, b, 0:tall], ext[a, 1, b, 0:tall]
-            re_to, im_to = ext[a, 0, b, 1 : tall + 1], ext[a, 1, b, 1 : tall + 1]
-            power = 0.5 * (re * re + im * im) + 0.25 * soften_term
-            power_to = 0.5 * (re_to * re_to + im_to * im_to) + 0.25 * soften_term
-            row_bond[0:tall] = bond(re, im, power, re_to, im_to, power_to)
-            re, im, power = re[PAD:], im[PAD:], power[PAD:]
-            re_to = reach_right(re, ext[a, 0, b + 1, PAD:tall])
-            im_to = reach_right(im, ext[a, 1, b + 1, PAD:tall])
-            power_to = 0.5 * (re_to * re_to + im_to * im_to) + 0.25 * soften_term
-            here = bond(re, im, power, re_to, im_to, power_to)
-            shifted = pltpu.roll(jnp.where(lane == LANES - 1, before, here), 1, axis=1)
-            source[a, b] = (
-                row_bond[PAD - 1 : tall - 1] - row_bond[PAD:tall] + shifted - here
-            )
-            return here
-
-        lax.fori_loop(0, blocks, columns, jnp.zeros((strip, LANES), f32))
+        col_bond[...] = jnp.zeros_like(col_bond)
+
+        def columns(b, _, a=a):
+            def cells(first, block):
+                return ext[a, 0, block, first : first + SEG], ext[a, 1, block, first : first + SEG]
+
+            groups = strip // SEG
+            re, im = cells(0, b)
+            above = bond(re, im, power_of(re, im), *cells(1, b))
+            edge[a, b] = -above[SEG - 1 :]
+            batch = min(BATCH, groups)
+            for g0 in range(0, groups, batch):
+                firsts = [PAD + (g0 + i) * SEG for i in range(batch)]
+                here = [cells(first, b) for first in firsts]
+                to_right = [
+                    [
+                        pltpu.roll(jnp.where(lane == 0, after, now), LANES - 1, axis=1)
+                        for now, after in zip(here[i], cells(firsts[i], b + 1))
+                    ]
+                    for i in range(batch)
+                ]
+                powers = [power_of(*here[i]) for i in range(batch)]
+                downs = [bond(*here[i], powers[i], *cells(firsts[i] + 1, b)) for i in range(batch)]
+                if g0 + batch == groups:
+                    downs[-1] = jnp.where(sub == SEG - 1, 0.0, downs[-1])
+                rights = [bond(*here[i], powers[i], *to_right[i]) for i in range(batch)]
+                rows = [slice((g0 + i) * SEG, (g0 + i + 1) * SEG) for i in range(batch)]
+                from_left = [
+                    pltpu.roll(
+                        jnp.where(lane == LANES - 1, col_bond[rows[i]], rights[i]), 1, axis=1
+                    )
+                    for i in range(batch)
+                ]
+                values = []
+                for i in range(batch):
+                    from_above = pltpu.roll(
+                        jnp.where(sub == SEG - 1, above, downs[i]), 1, axis=0
+                    )
+                    above = downs[i]
+                    values.append(from_above - downs[i] + from_left[i] - rights[i])
+                for i in range(batch):
+                    col_bond[rows[i]] = rights[i]
+                    source[a, b, rows[i]] = values[i]
+            return 0
+
+        lax.fori_loop(0, blocks, columns, 0)
 
     def fold(b, _):
         lanes = pl.ds(pl.multiple_of(b * LANES, LANES), LANES)
@@ -362,6 +507,15 @@
                     high, low = split_pair(values)
                     rows_in[h, at : at + 2 * SEG, lanes] = high
                     rows_in[h, count + at : count + at + 2 * SEG, lanes] = low
+        edges = [jnp.concatenate([edge[a, i] for a in range(angles)], 0) for i in (b, blocks - 1 - b)]
+        fill = jnp.zeros((2 * PAD - angles, LANES), f32)
+        lower, upper = (jnp.concatenate([rows, fill], 0) for rows in edges)
+        upper = reversed_lanes(upper)
+        at = angles * strip
+        for h, values in enumerate((lower + upper, lower - upper)):
+            high, low = split_pair(values)
+            rows_in[h, at : at + 2 * PAD, lanes] = high
+            rows_in[h, count + at : count + at + 2 * PAD, lanes] = low
         return 0
 
     lax.fori_loop(0, half_blocks, fold, 0)
@@ -399,12 +553,15 @@
                     tail_z = tail_z + jnp.where(
                         sub < SEG - k, factor * pltpu.roll(tail_z, SEG - k, axis=0), 0.0
                     )
-                carry_y[a, :, spots] = jnp.where(sub >= 1, pltpu.roll(tail_y, 1, axis=0), 0.0)
+                above = values[angles * strip + a : angles * strip + a + 1]
+                carry_y[a, :, spots] = (
+                    jnp.where(sub >= 1, pltpu.roll(tail_y, 1, axis=0), 0.0) + segs[:, spots] * above
+                )
                 carry_z[a, :, spots] = jnp.where(
                     sub < SEG - 1, pltpu.roll(tail_z, SEG - 1, axis=0), 0.0
                 )
-                ends[0, a : a + 1, spots] = tail_z[0:1]
-                ends[1, a : a + 1, spots] = tail_y[SEG - 1 : SEG]
+                ends[0, a : a + 1, spots] = tail_z[0:1] + scan[5:6, spots] * above
+                ends[1, a : a + 1, spots] = tail_y[SEG - 1 : SEG] + scan[6:7, spots] * above
             return 0
 
         lax.fori_loop(0, half // wide, transform, 0)
@@ -414,13 +571,13 @@
             store(a, b).wait()
 
 
-def run_update(tabs, field, top, bottom, scan, table, first_piece, pieces):
+def run_update(tabs, field, package, halo, scan, segs, tables, pieces, center):
     angles, _, strip, grid = field.shape
     reach = len(pieces) - 1
     blocks = grid // LANES
     half = grid // 2
     return pl.pallas_call(
-        functools.partial(update_kernel, reach),
+        functools.partial(update_kernel, reach, center),
         out_shape=[
             jax.ShapeDtypeStruct(field.shape, f32),
             jax.ShapeDtypeStruct((angles, strip, grid), f32),
@@ -428,37 +585,54 @@
             jax.ShapeDtypeStruct((angles, SEG, grid), f32),
             jax.ShapeDtypeStruct((2, angles, grid), f32),
         ],
-        in_specs=[SMEM_SPEC, ANY_SPEC, VMEM_SPEC, VMEM_SPEC, VMEM_SPEC, ANY_SPEC]
-        + [VMEM_SPEC] * (reach + 2),
+        in_specs=[SMEM_SPEC] * reach
+        + [ANY_SPEC]
+        + [VMEM_SPEC] * 4
+        + [ANY_SPEC]
+        + [VMEM_SPEC] * (reach + 1),
         out_specs=[ANY_SPEC] + [VMEM_SPEC] * 4,
         scratch_shapes=[
             pltpu.VMEM((angles, 2, blocks + 1, strip + 2 * PAD, LANES), f32),
-            pltpu.VMEM((strip + 2 * PAD, LANES), f32),
+            pltpu.VMEM((strip, LANES), f32),
             pltpu.VMEM((angles, blocks, strip, LANES), f32),
-            pltpu.VMEM((2, 2 * angles * strip, half), bf16),
-            pltpu.VMEM((2, 2, half, half), bf16),
+            pltpu.VMEM((angles, blocks, 1, LANES), f32),
+            pltpu.VMEM((2, 2 * (angles * strip + 2 * PAD), half), bf16),
+            pltpu.VMEM((1, LANES), jnp.int32),
+            pltpu.VMEM(tables.shape[1:], bf16),
             pltpu.SemaphoreType.DMA((angles, blocks)),
             pltpu.SemaphoreType.DMA((angles, blocks)),
             pltpu.SemaphoreType.DMA((2, 2)),
         ],
-        compiler_params=PARAMS,
+        compiler_params=UPDATE_PARAMS,
+        cost_estimate=cost(14),
         name="update",
-    )(tabs, field, top, bottom, scan, table, first_piece, *pieces)
-
-
-def phase_kernel(inner, carry_y, carry_z, enter, scan, powers, segs, segs_back, table_hbm, out, rest, rows_in, table, sems):
+    )(*tabs, field, package, halo, scan, segs, tables, *pieces)
+
+
+def phase_kernel(inner, carry_y, carry_z, enter, scan, powers, segs, segs_back, tables, out_hbm, rest, rows_in, table, out, table_sems, out_sems):
     angles, strip, grid = inner.shape
     half = grid // 2
     steps = strip // SEG
     count = angles * strip
     half_blocks = half // LANES
-
-    def load_table(h, k):
-        return pltpu.make_async_copy(table_hbm.at[k, h], table.at[k, h], sems.at[k, h])
-
-    for h in range(2):
-        for k in range(2):
-            load_table(h, k).start()
+    wide = min(2 * LANES, half)
+    chunks = half // wide
+
+    def load_table(c):
+        lanes = pl.ds(pl.multiple_of(c * wide, wide), wide)
+        return pltpu.make_async_copy(
+            tables.at[1, :, :, :, lanes], table.at[:, :, :, lanes], table_sems.at[c]
+        )
+
+    def store(c, side):
+        start = c * wide if side == 0 else grid - (c + 1) * wide
+        lanes = pl.ds(pl.multiple_of(start, wide), wide)
+        return pltpu.make_async_copy(
+            out.at[:, :, lanes], out_hbm.at[:, :, lanes], out_sems.at[c, side]
+        )
+
+    for c in range(chunks):
+        load_table(c).start()
 
     def solve(b, _):
         spots = pl.ds(pl.multiple_of(b * LANES, LANES), LANES)
@@ -486,13 +660,10 @@
         return 0
 
     lax.fori_loop(0, half_blocks, split, 0)
-    for h in range(2):
-        for k in range(2):
-            load_table(h, k).wait()
-    wide = min(2 * LANES, half)
 
     def back(c, _):
         lanes = pl.ds(pl.multiple_of(c * wide, wide), wide)
+        load_table(c).wait()
         even, odd = (
             three_pass(rows_in[h], count, table[0, h, :, lanes], table[1, h, :, lanes])
             for h in range(2)
@@ -508,28 +679,37 @@
                 out[a, :, spot] = reversed_lanes(
                     mirrored[a * strip : (a + 1) * strip, k * LANES : (k + 1) * LANES]
                 )
+        for side in range(2):
+            store(c, side).start()
         return 0
 
-    lax.fori_loop(0, half // wide, back, 0)
-
-
-def run_phase(inner, carry_y, carry_z, enter, scan, powers, segs, segs_back, table):
+    lax.fori_loop(0, chunks, back, 0)
+    for c in range(chunks):
+        for side in range(2):
+            store(c, side).wait()
+
+
+def run_phase(inner, carry_y, carry_z, enter, scan, powers, segs, segs_back, tables):
     angles, strip, grid = inner.shape
     half = grid // 2
+    chunks = half // min(2 * LANES, half)
     return pl.pallas_call(
         phase_kernel,
         out_shape=jax.ShapeDtypeStruct((angles, strip, grid), f32),
         in_specs=[VMEM_SPEC] * 8 + [ANY_SPEC],
-        out_specs=VMEM_SPEC,
+        out_specs=ANY_SPEC,
         scratch_shapes=[
             pltpu.VMEM((angles, grid // LANES, strip, LANES), f32),
             pltpu.VMEM((2, 2 * angles * strip, half), bf16),
-            pltpu.VMEM((2, 2, half, half), bf16),
-            pltpu.SemaphoreType.DMA((2, 2)),
+            pltpu.VMEM(tables.shape[1:], bf16),
+            pltpu.VMEM((angles, strip, grid), f32),
+            pltpu.SemaphoreType.DMA((chunks,)),
+            pltpu.SemaphoreType.DMA((chunks, 2)),
         ],
-        compiler_params=PARAMS,
+        compiler_params=PHASE_PARAMS,
+        cost_estimate=cost(7),
         name="phase",
-    )(inner, carry_y, carry_z, enter, scan, powers, segs, segs_back, table)
+    )(inner, carry_y, carry_z, enter, scan, powers, segs, segs_back, tables)
 
 
 def passed_along(x, by):
@@ -572,34 +752,48 @@
     caps, frame = measured.shape[0], measured.shape[1]
     reach = frame // strip
     center = reach // 2
-    table = cosine_halves(grid)
-    forward_table = jnp.asarray(split_table(np.swapaxes(table, 1, 2)))
-    back_table = jnp.asarray(split_table(table))
+    halves = cosine_halves(grid)
+    tables = jnp.asarray(np.stack([split_table(np.swapaxes(halves, 1, 2)), split_table(halves)]))
     scan, powers, segs, segs_back, strips, closing = (
         jnp.asarray(x) for x in decay_tables(grid, strip)
     )
 
-    own_tab = jnp.concatenate([frame_table.reshape(-1), frame_count])
-    tabs = {j: own_tab if j == 0 else passed_along(own_tab, j) for j in range(-1, reach + 1)}
+    own_tab = jnp.concatenate(
+        [frame_table, jnp.broadcast_to(frame_count[None, :], (caps, 1))], axis=1
+    )
+    far = [j for j in range(1, reach + 1) if j != center]
+    tabs = {0: own_tab}
+    for j in far:
+        tabs[j] = passed_along(own_tab, j)
     measured_here = passed_along(measured, center)
-    bottom = passed_along(object_field[:, :, :1], -1)
-    top = passed_along(object_field[:, :, strip - 1 :], 1)
-    windows = []
-    for j in range(reach + 1):
-        window = extract(tabs[j], object_field, caps, frame)
-        windows.append(window if j == center else passed_along(window, center - j))
-    first_piece, *pieces = run_frames(tabs[center], probe, measured_here, windows, center)
-    first_piece = passed_along(first_piece, -1 - center)
+    package = pack(own_tab, object_field, caps, frame)
+    windows = {}
+    for j in far:
+        window, package = extract(tabs[j], False, object_field, caps, frame, package)
+        windows[j] = passed_along(window, center - j)
+    arrived = passed_along(package, center)
+    at_halo, halo_rows = package_rows(caps, strip, frame, angles, grid)
+    halo = slice(at_halo, at_halo + 3 * halo_rows)
+    top = arrived[halo] if center == 1 else passed_along(package[halo], 1)
+    windows[center] = extract(arrived, True, object_field, caps, frame)
+    pieces = run_frames(arrived, measured_here, probe, [windows[j] for j in range(1, reach + 1)], center)
     pieces = [
         piece if j == center else passed_along(piece, j - center) for j, piece in enumerate(pieces)
     ]
-    all_tabs = jnp.stack([tabs[j] for j in range(-1, reach + 1)])
     updated, inner, carry_y, carry_z, ends = run_update(
-        all_tabs, object_field, top, bottom, scan, forward_table, first_piece, pieces
+        [tabs[j] for j in range(reach + 1) if j != center],
+        object_field,
+        arrived,
+        top,
+        scan,
+        segs,
+        tables,
+        pieces,
+        center,
     )
     enter = entering_values(ends, strips, closing)
     phase_map = run_phase(
-        inner, carry_y, carry_z, enter, scan, powers, segs, segs_back, back_table
+        inner, carry_y, carry_z, enter, scan, powers, segs, segs_back, tables
     )
     return (updated, phase_map)
 

time: 95.9 us -> 77.8 us (0.81); the launches traced: 94.1 us -> 78.1 us
  Pallas kernels: 37 us -> 24.7 us
  waiting for transfers between devices: 11.6 us -> 9.15 us
  starting transfers between devices: 39.2 us -> 36.8 us
  local copies, waits for them, and re-layouts: 4.18 us -> 5.51 us
    ppermute x11 -> x6, starting transfers between devices: 29.9 us -> 21.3 us  [passed_along(): return lax.ppermute(x, 'tile', pairs)]
    pallas_call x5, Pallas kernels: 26.2 us -> 17.8 us  [the longest x1 14.8 us: run_update(): pl.pallas_call(functools.partial(update_kernel, reach, center), out_shape...]
    ppermute x4, starting transfers between devices: 9.29 us -> 15.5 us  [entering_values(): lax.ppermute(jnp.stack([head, tail]), 'tile', [(i, i ^ width) for i in ra...]
    pallas_call x1, Pallas kernels: 10.8 us -> 6.87 us  [run_phase(): pl.pallas_call(phase_kernel, out_shape=jax.ShapeDtypeStruct((angles, stri...]
    ppermute x11 -> x6, waiting for transfers between devices: 5.65 us -> 2.64 us  [passed_along(): return lax.ppermute(x, 'tile', pairs)]
    unnamed x22 -> x30, local copies, waits for them, and re-layouts: 1.11 us -> 3.33 us
    slice x1, local copies, waits for them, and re-layouts: 1.08 us -> 0.01 us  [body(): top = arrived[halo] if center == 1 else passed_along(package[halo], 1)]
  transfers between devices with their start and end apart: 15 -> 10, of which waited for: 5 -> 6; matrix products, arithmetic and copies ran while one was open for 3% -> 2% of each run, Pallas kernels for 9% -> 2%
where the time goes in v2:
time: 77.8 us; the launch traced here: 78.1 us
  starting transfers between devices  36.8 us (47%)
  Pallas kernels  24.7 us (32%)
  waiting for transfers between devices  9.15 us (12%)
  local copies, waits for them, and re-layouts  5.51 us (7%)
  between operations  1.59 us (2%)
    ppermute x6, starting transfers between devices, passed_along(): return lax.ppermute(x, 'tile', pairs)  21.3 us
    ppermute x4, starting transfers between devices, entering_values(): lax.ppermute(jnp.stack([head, tail]), 'tile', [(i, i ^ width) for i in ra...  15.5 us
    pallas_call x1, Pallas kernels, run_update(): pl.pallas_call(functools.partial(update_kernel, reach, center), out_shape...  14.8 us
    pallas_call x1, Pallas kernels, run_phase(): pl.pallas_call(phase_kernel, out_shape=jax.ShapeDtypeStruct((angles, stri...  6.87 us
    ppermute x4, waiting for transfers between devices, entering_values(): lax.ppermute(jnp.stack([head, tail]), 'tile', [(i, i ^ width) for i in ra...  6.52 us
    unnamed x30, local copies, waits for them, and re-layouts  3.33 us
    ppermute x6, waiting for transfers between devices, passed_along(): return lax.ppermute(x, 'tile', pairs)  2.64 us
    pallas_call x2, Pallas kernels, extract(): pl.pallas_call(functools.partial(extract_kernel, coded), out_shape=[windo...  1.58 us
  transfers between devices with their start and end apart: 10, of which 6 were waited for; matrix products, arithmetic and copies ran while one was open for 2% of the time, Pallas kernels for 2%

profile of v2, /device:TPU:0, one launch (start us, length us, event | category | flops | bytes accessed | tf_op | source)
XLA Modules:
  0.0 78.1 jit_solution(11340099264820678374)
XLA Ops:
  1.3 0.7 concatenate.3.tab.refs_0_
  2.0 4.9 %collective-permute-start = (s32[2,4]{1,0:T(2,128)S(1)}, s32[2,4]{1,0:T(2,128)S(1)}, u32[]{:S(2)}, u32[]{:S(2)}) collective-permute-start(s32[2,4]{1,0:T(2,128)S(1)} %concatenate.3.tab.refs_0_), channel_id=1, source_target_pairs={{0,2},{1,3},{2,4},{3,5},{4,6},{5,7},{6,8},{7,9},{8,10},{9,11},{10,... | collective-permute-start | bytes 104 | tf_op jit(solution)/shard_map/ppermute | solution.py:718
  6.8 0.0 copy-start
  6.8 2.2 %copy-done = f32[2,2,128,2048]{3,2,1,0:T(8,128)S(1)} copy-done((f32[2,2,128,2048]{3,2,1,0:T(8,128)S(1)}, f32[2,2,128,2048]{3,2,1,0:T(8,128)}, u32[]{:S(2)}) %copy-start) | copy-done | bytes 4194328
  9.0 0.0 copy-start.1
  9.0 0.0 copy-start.14
  9.0 1.1 %pack.1.rest_0_ = bf16[624,256]{1,0:T(8,128)(2,1)S(1)} custom-call(s32[2,4]{1,0:T(2,128)S(1)} %concatenate.3.tab.refs_0_, f32[2,2,128,2048]{3,2,1,0:T(8,128)S(1)} %copy-done), custom_call_target="tpu_custom_call" | custom-call | bytes 18000000 | tf_op jit(solution)/shard_map/pack/pallas_call | solution.py:179
  10.1 0.0 copy-start.2
  10.1 0.0 copy-start.3
  10.1 0.0 copy-start.4
  10.1 0.0 collective-permute-done.tab.refs_1_
  10.1 1.1 %copy-done.1 = f32[2,2,128,2048]{3,2,1,0:T(8,128)S(1)} copy-done((f32[2,2,128,2048]{3,2,1,0:T(8,128)S(1)}, f32[2,2,128,2048]{3,2,1,0:T(8,128)}, u32[]{:S(2)}) %copy-start.1) | copy-done | bytes 4194328
  11.2 1.0 %extract.2 = (bf16[2,2,128,256]{3,2,1,0:T(8,128)(2,1)S(1)}, bf16[624,256]{1,0:T(8,128)(2,1)S(1)}) custom-call(s32[2,4]{1,0:T(2,128)S(1)} %collective-permute-done.tab.refs_1_, f32[2,2,128,2048]{3,2,1,0:T(8,128)S(1)} %copy-done.1, bf16[624,256]{1,0:T(8,128)(2,1)S(1)} %pack.1.rest_0_), custom_call_target="tpu_custom_call", output_to_operand_aliasing={{1}: (2, {})} | custom-call | bytes 6000000 | tf_op jit(solution)/shard_map/extract/pallas_call | solution.py:212
  12.2 0.0 copy-start.5
  12.2 0.0 copy-start.6
  12.2 1.6 %collective-permute-start.1 = (bf16[624,256]{1,0:T(8,128)(2,1)S(1)}, bf16[624,256]{1,0:T(8,128)(2,1)S(1)}, u32[]{:S(2)}, u32[]{:S(2)}) collective-permute-start(bf16[624,256]{1,0:T(8,128)(2,1)S(1)} %get-tuple-element.12), channel_id=1, source_target_pairs={{0,1},{1,2},{2,3},{3,4},{4,5},{5,6},{6,7},{7,8},{8,9},{9,10},{10,1... | collective-permute-start | bytes 958472 | tf_op jit(solution)/shard_map/ppermute | solution.py:718
  13.8 0.0 copy-done.14
  13.8 4.0 %collective-permute-start.2 = (bf16[2,256,256]{2,1,0:T(8,128)(2,1)S(1)}, bf16[2,256,256]{2,1,0:T(8,128)(2,1)S(1)}, u32[]{:S(2)}, u32[]{:S(2)}) collective-permute-start(bf16[2,256,256]{2,1,0:T(8,128)(2,1)S(1)} %copy-done.14), channel_id=1, source_target_pairs={{0,1},{1,2},{2,3},{3,4},{4,5},{5,6},{6,7},{7,8},{8,9},{9,10},{10,1... | collective-permute-start | bytes 786440 | tf_op jit(solution)/shard_map/ppermute | solution.py:718
  17.8 1.3 %collective-permute-start.3 = (bf16[2,2,128,256]{3,2,1,0:T(8,128)(2,1)S(1)}, bf16[2,2,128,256]{3,2,1,0:T(8,128)(2,1)S(1)}, u32[]{:S(2)}, u32[]{:S(2)}) collective-permute-start(bf16[2,2,128,256]{3,2,1,0:T(8,128)(2,1)S(1)} %get-tuple-element.13), channel_id=1, source_target_pairs={{1,0},{2,1},{3,2},{4,3},{5,4},{6,5},{7,6},{8,7},{9,8},{10,9},{11,1... | collective-permute-start | bytes 786440 | tf_op jit(solution)/shard_map/ppermute | solution.py:718
  19.1 0.0 collective-permute-done.1.tab.package.refs_3_
  19.1 0.6 extract.3.rest_0_
  19.8 0.0 collective-permute-done.2.measured
  19.8 1.5 %collective-permute-done.3.rest_1_ = bf16[2,2,128,256]{3,2,1,0:T(8,128)(2,1)S(1)} collective-permute-done((bf16[2,2,128,256]{3,2,1,0:T(8,128)(2,1)S(1)}, bf16[2,2,128,256]{3,2,1,0:T(8,128)(2,1)S(1)}, u32[]{:S(2)}, u32[]{:S(2)}) %collective-permute-start.3) | collective-permute-done | bytes 262176 | tf_op jit(solution)/shard_map/ppermute | solution.py:718
  21.3 0.0 copy-done.2
  21.3 0.0 copy-done.3
  21.3 0.0 copy-done.4
  21.3 0.4 frames.1
  21.6 1.3 %collective-permute-start.4 = (bf16[2,2,144,256]{3,2,1,0:T(8,128)(2,1)S(1)}, bf16[2,2,144,256]{3,2,1,0:T(8,128)(2,1)S(1)}, u32[]{:S(2)}, u32[]{:S(2)}) collective-permute-start(bf16[2,2,144,256]{3,2,1,0:T(8,128)(2,1)S(1)} %get-tuple-element.14), channel_id=1, source_target_pairs={{1,0},{2,1},{3,2},{4,3},{5,4},{6,5},{7,6},{8,7},{9,8},{10,9},{11,1... | collective-permute-start | bytes 884744 | tf_op jit(solution)/shard_map/ppermute | solution.py:718
  22.9 8.3 %collective-permute-start.5 = (bf16[2,2,144,256]{3,2,1,0:T(8,128)(2,1)S(1)}, bf16[2,2,144,256]{3,2,1,0:T(8,128)(2,1)S(1)}, u32[]{:S(2)}, u32[]{:S(2)}) collective-permute-start(bf16[2,2,144,256]{3,2,1,0:T(8,128)(2,1)S(1)} %get-tuple-element.16), channel_id=1, source_target_pairs={{0,1},{1,2},{2,3},{3,4},{4,5},{5,6},{6,7},{7,8},{8,9},{9,10},{10,1... | collective-permute-start | bytes 884744 | tf_op jit(solution)/shard_map/ppermute | solution.py:718
  31.2 0.0 collective-permute-done.4.refs_8_
  31.2 1.1 %collective-permute-done.5.refs_10_ = bf16[2,2,144,256]{3,2,1,0:T(8,128)(2,1)S(1)} collective-permute-done((bf16[2,2,144,256]{3,2,1,0:T(8,128)(2,1)S(1)}, bf16[2,2,144,256]{3,2,1,0:T(8,128)(2,1)S(1)}, u32[]{:S(2)}, u32[]{:S(2)}) %collective-permute-start.5) | collective-permute-done | bytes 294944 | tf_op jit(solution)/shard_map/ppermute | solution.py:718
  32.4 0.0 copy-done.5
  32.4 0.0 copy-done.6
  32.4 0.0 copy-start.13
  32.4 0.0 copy-start.12
  32.4 0.0 copy-start.11
  32.4 0.0 copy-start.9
  32.4 0.0 copy-start.10
  32.4 0.0 copy-start.7
  32.5 0.0 copy-start.8
  32.5 14.8 %update.1 = (f32[2,2,128,2048]{3,2,1,0:T(8,128)}, f32[2,128,2048]{2,1,0:T(8,128)S(1)}, f32[2,8,2048]{2,1,0:T(8,128)S(1)}, f32[2,8,2048]{2,1,0:T(8,128)S(1)}, f32[2,2,2048]{2,1,0:T(2,128)S(1)}) custom-call(s32[2,4]{1,0:T(2,128)S(1)} %concatenate.3.tab.refs_0_, s32[2,4]{1,0:T(2,128)S(1)} %collective-permute-done.tab.refs_1_, ...), custom_call_target="tpu_custom_call" | custom-call | bytes 42000000 | tf_op jit(solution)/shard_map/update/pallas_call | solution.py:579
  47.3 7.7 %collective-permute-start.6 = (f32[2,2,2048]{2,1,0:T(2,128)S(1)}, f32[2,2,2048]{2,1,0:T(2,128)S(1)}, u32[]{:S(2)}, u32[]{:S(2)}) collective-permute-start(f32[2,2,2048]{2,1,0:T(2,128)S(1)} %get-tuple-element.21), channel_id=1, source_target_pairs={{0,1},{1,0},{2,3},{3,2},{4,5},{5,4},{6,7},{7,6},{8,9},{9,8},{10,11... | collective-permute-start | bytes 98312 | tf_op jit(solution)/shard_map/ppermute | solution.py:730
  55.0 0.9 %collective-permute-done.6 = f32[2,2,2048]{2,1,0:T(2,128)S(1)} collective-permute-done((f32[2,2,2048]{2,1,0:T(2,128)S(1)}, f32[2,2,2048]{2,1,0:T(2,128)S(1)}, u32[]{:S(2)}, u32[]{:S(2)}) %collective-permute-start.6) | collective-permute-done | bytes 32800 | tf_op jit(solution)/shard_map/ppermute | solution.py:730
  55.9 0.0 copy-done.13
  55.9 3.1 %collective-permute-start.7 = (f32[2,2,2048]{2,1,0:T(2,128)S(1)}, f32[2,2,2048]{2,1,0:T(2,128)S(1)}, u32[]{:S(2)}, u32[]{:S(2)}) collective-permute-start(f32[2,2,2048]{2,1,0:T(2,128)S(1)} %pad_maximum_fusion), channel_id=1, source_target_pairs={{0,2},{1,3},{2,0},{3,1},{4,6},{5,7},{6,4},{7,5},{8,10},{9,11},{10,... | collective-permute-start | bytes 98312 | tf_op jit(solution)/shard_map/ppermute | solution.py:730
  59.1 1.9 %collective-permute-done.7 = f32[2,2,2048]{2,1,0:T(2,128)S(1)} collective-permute-done((f32[2,2,2048]{2,1,0:T(2,128)S(1)}, f32[2,2,2048]{2,1,0:T(2,128)S(1)}, u32[]{:S(2)}, u32[]{:S(2)}) %collective-permute-start.7) | collective-permute-done | bytes 32800 | tf_op jit(solution)/shard_map/ppermute | solution.py:730
  61.0 0.0 copy-done.12
  61.0 3.2 %collective-permute-start.8 = (f32[2,2,2048]{2,1,0:T(2,128)S(1)}, f32[2,2,2048]{2,1,0:T(2,128)S(1)}, u32[]{:S(2)}, u32[]{:S(2)}) collective-permute-start(f32[2,2,2048]{2,1,0:T(2,128)S(1)} %pad_maximum_fusion.1), channel_id=1, source_target_pairs={{0,4},{1,5},{2,6},{3,7},{4,0},{5,1},{6,2},{7,3},{8,12},{9,13},{10,... | collective-permute-start | bytes 98312 | tf_op jit(solution)/shard_map/ppermute | solution.py:730
  64.2 1.9 %collective-permute-done.8 = f32[2,2,2048]{2,1,0:T(2,128)S(1)} collective-permute-done((f32[2,2,2048]{2,1,0:T(2,128)S(1)}, f32[2,2,2048]{2,1,0:T(2,128)S(1)}, u32[]{:S(2)}, u32[]{:S(2)}) %collective-permute-start.8) | collective-permute-done | bytes 32800 | tf_op jit(solution)/shard_map/ppermute | solution.py:730
  66.1 0.0 copy-done.11
  66.1 1.5 %collective-permute-start.9 = (f32[2,2,2048]{2,1,0:T(2,128)S(1)}, f32[2,2,2048]{2,1,0:T(2,128)S(1)}, u32[]{:S(2)}, u32[]{:S(2)}) collective-permute-start(f32[2,2,2048]{2,1,0:T(2,128)S(1)} %pad_maximum_fusion.2), channel_id=1, source_target_pairs={{0,8},{1,9},{2,10},{3,11},{4,12},{5,13},{6,14},{7,15},{8,0},{9,1},... | collective-permute-start | bytes 98312 | tf_op jit(solution)/shard_map/ppermute | solution.py:730
  67.6 1.5 %constant_dynamic-slice_fusion.7 = (f32[1,2048]{1,0:T(1,128)S(1)}, f32[1,2048]{1,0:T(1,128)S(1)}, f32[1,2048]{1,0:T(1,128)S(1)}, f32[1,2048]{1,0:T(1,128)S(1)}, ...) fusion(f32[17,2048]{1,0:T(8,128)} %constant.55.clone, ...), kind=kLoop, calls=%fused_computation.21 | loop fusion | bytes 131104 | tf_op jit(solution)/shard_map/dynamic_slice | solution.py:727
  69.2 1.9 %collective-permute-done.9 = f32[2,2,2048]{2,1,0:T(2,128)S(1)} collective-permute-done((f32[2,2,2048]{2,1,0:T(2,128)S(1)}, f32[2,2,2048]{2,1,0:T(2,128)S(1)}, u32[]{:S(2)}, u32[]{:S(2)}) %collective-permute-start.9) | collective-permute-done | bytes 32800 | tf_op jit(solution)/shard_map/ppermute | solution.py:730
  71.0 0.0 copy-done.9
  71.0 0.0 copy-done.10
  71.0 0.1 multiply_add_fusion
  71.1 0.1 multiply_add_fusion.1
  71.2 0.0 copy-done.7
  71.2 0.0 copy-done.8
  71.2 6.9 %phase.1 = f32[2,128,2048]{2,1,0:T(8,128)} custom-call(f32[2,128,2048]{2,1,0:T(8,128)S(1)} %get-tuple-element.18.inner, f32[2,8,2048]{2,1,0:T(8,128)S(1)} %get-tuple-element.19.carry_y, f32[2,8,2048]{2,1,0:T(8,128)S(1)} %get-tuple-element.20.carry_z, f32[2,2,2048]{2,1,0:T(2,128)S(1)} %pad_maximum_fusion.3.enter, f32[7,2048]{1,0:T(8,128)S(1)} %copy-done.6, ...), custom_call_target="tpu_custom_call" | custom-call | bytes 21000000 | tf_op jit(solution)/shard_map/phase/pallas_call | solution.py:696
  (8 shorter events, 0.2 us)
Async XLA Ops:
  2.0 8.2 %collective-permute-start = (s32[2,4]{1,0:T(2,128)S(1)}, s32[2,4]{1,0:T(2,128)S(1)}, u32[]{:S(2)}, u32[]{:S(2)}) collective-permute-start(s32[2,4]{1,0:T(2,128)S(1)} %concatenate.3.tab.refs_0_), channel_id=1, source_target_pairs={{0,2},{1,3},{2,4},{3,5},{4,6},{5,7},{6,8},{7,9},{8,10},{9,11},{10,... | collective-permute-start | bytes 104 | tf_op jit(solution)/shard_map/ppermute | solution.py:718
  6.8 2.2 %copy-start = (f32[2,2,128,2048]{3,2,1,0:T(8,128)S(1)}, f32[2,2,128,2048]{3,2,1,0:T(8,128)}, u32[]{:S(2)}) copy-start(f32[2,2,128,2048]{3,2,1,0:T(8,128)} %refs_2_.1) | copy-start | bytes 12582916
  9.0 2.2 %copy-start.1 = (f32[2,2,128,2048]{3,2,1,0:T(8,128)S(1)}, f32[2,2,128,2048]{3,2,1,0:T(8,128)}, u32[]{:S(2)}) copy-start(f32[2,2,128,2048]{3,2,1,0:T(8,128)} %refs_2_.1) | copy-start | bytes 12582916
  9.0 4.8 %copy-start.14 = (bf16[2,256,256]{2,1,0:T(8,128)(2,1)S(1)}, bf16[2,256,256]{2,1,0:T(8,128)(2,1)}, u32[]{:S(2)}) copy-start(bf16[2,256,256]{2,1,0:T(8,128)(2,1)} %param.16) | copy-start | bytes 786436
  10.1 11.2 %copy-start.2 = (f32[2,256,256]{2,1,0:T(8,128)S(1)}, f32[2,256,256]{2,1,0:T(8,128)}, u32[]{:S(2)}) copy-start(f32[2,256,256]{2,1,0:T(8,128)} %probe.1) | copy-start | bytes 1572868
  10.1 11.2 %copy-start.3 = (bf16[512,512]{1,0:T(8,128)(2,1)S(1)}, bf16[512,512]{1,0:T(8,128)(2,1)}, u32[]{:S(2)}) copy-start(bf16[512,512]{1,0:T(8,128)(2,1)} %constant.58.clone.right) | copy-start | bytes 1572868
  10.1 11.1 %copy-start.4 = (bf16[512,512]{1,0:T(8,128)(2,1)S(1)}, bf16[512,512]{1,0:T(8,128)(2,1)}, u32[]{:S(2)}) copy-start(bf16[512,512]{1,0:T(8,128)(2,1)} %constant.57.clone.left) | copy-start | bytes 1572868
  12.2 20.2 %copy-start.5 = (f32[8,2048]{1,0:T(8,128)S(1)}, f32[8,2048]{1,0:T(8,128)}, u32[]{:S(2)}) copy-start(f32[8,2048]{1,0:T(8,128)} %constant.53.clone.refs_6_.segs) | copy-start | bytes 196612
  12.2 20.2 %copy-start.6 = (f32[7,2048]{1,0:T(8,128)S(1)}, f32[7,2048]{1,0:T(8,128)}, u32[]{:S(2)}) copy-start(f32[7,2048]{1,0:T(8,128)} %constant.51.clone.refs_5_.scan) | copy-start | bytes 172036
  12.2 6.9 %collective-permute-start.1 = (bf16[624,256]{1,0:T(8,128)(2,1)S(1)}, bf16[624,256]{1,0:T(8,128)(2,1)S(1)}, u32[]{:S(2)}, u32[]{:S(2)}) collective-permute-start(bf16[624,256]{1,0:T(8,128)(2,1)S(1)} %get-tuple-element.12), channel_id=1, source_target_pairs={{0,1},{1,2},{2,3},{3,4},{4,5},{5,6},{6,7},{7,8},{8,9},{9,10},{10,1... | collective-permute-start | bytes 958472 | tf_op jit(solution)/shard_map/ppermute | solution.py:718
  13.8 5.9 %collective-permute-start.2 = (bf16[2,256,256]{2,1,0:T(8,128)(2,1)S(1)}, bf16[2,256,256]{2,1,0:T(8,128)(2,1)S(1)}, u32[]{:S(2)}, u32[]{:S(2)}) collective-permute-start(bf16[2,256,256]{2,1,0:T(8,128)(2,1)S(1)} %copy-done.14), channel_id=1, source_target_pairs={{0,1},{1,2},{2,3},{3,4},{4,5},{5,6},{6,7},{7,8},{8,9},{9,10},{10,1... | collective-permute-start | bytes 786440 | tf_op jit(solution)/shard_map/ppermute | solution.py:718
  17.8 3.4 %collective-permute-start.3 = (bf16[2,2,128,256]{3,2,1,0:T(8,128)(2,1)S(1)}, bf16[2,2,128,256]{3,2,1,0:T(8,128)(2,1)S(1)}, u32[]{:S(2)}, u32[]{:S(2)}) collective-permute-start(bf16[2,2,128,256]{3,2,1,0:T(8,128)(2,1)S(1)} %get-tuple-element.13), channel_id=1, source_target_pairs={{1,0},{2,1},{3,2},{4,3},{5,4},{6,5},{7,6},{8,7},{9,8},{10,9},{11,1... | collective-permute-start | bytes 786440 | tf_op jit(solution)/shard_map/ppermute | solution.py:718
  21.6 9.6 %collective-permute-start.4 = (bf16[2,2,144,256]{3,2,1,0:T(8,128)(2,1)S(1)}, bf16[2,2,144,256]{3,2,1,0:T(8,128)(2,1)S(1)}, u32[]{:S(2)}, u32[]{:S(2)}) collective-permute-start(bf16[2,2,144,256]{3,2,1,0:T(8,128)(2,1)S(1)} %get-tuple-element.14), channel_id=1, source_target_pairs={{1,0},{2,1},{3,2},{4,3},{5,4},{6,5},{7,6},{8,7},{9,8},{10,9},{11,1... | collective-permute-start | bytes 884744 | tf_op jit(solution)/shard_map/ppermute | solution.py:718
  22.9 9.5 %collective-permute-start.5 = (bf16[2,2,144,256]{3,2,1,0:T(8,128)(2,1)S(1)}, bf16[2,2,144,256]{3,2,1,0:T(8,128)(2,1)S(1)}, u32[]{:S(2)}, u32[]{:S(2)}) collective-permute-start(bf16[2,2,144,256]{3,2,1,0:T(8,128)(2,1)S(1)} %get-tuple-element.16), channel_id=1, source_target_pairs={{0,1},{1,2},{2,3},{3,4},{4,5},{5,6},{6,7},{7,8},{8,9},{9,10},{10,1... | collective-permute-start | bytes 884744 | tf_op jit(solution)/shard_map/ppermute | solution.py:718
  32.4 23.5 %copy-start.13 = (f32[2048]{0:T(1024)S(1)}, f32[2048]{0:T(1024)}, u32[]{:S(2)}) copy-start(f32[2048]{0:T(1024)} %constant.67) | copy-start | bytes 24580
  32.4 28.6 %copy-start.12 = (f32[2048]{0:T(1024)S(1)}, f32[2048]{0:T(1024)}, u32[]{:S(2)}) copy-start(f32[2048]{0:T(1024)} %constant.69) | copy-start | bytes 24580
  32.4 33.7 %copy-start.11 = (f32[2048]{0:T(1024)S(1)}, f32[2048]{0:T(1024)}, u32[]{:S(2)}) copy-start(f32[2048]{0:T(1024)} %constant.71) | copy-start | bytes 24580
  32.4 38.6 %copy-start.9 = (f32[2048]{0:T(1024)S(1)}, f32[2048]{0:T(1024)}, u32[]{:S(2)}) copy-start(f32[2048]{0:T(1024)} %constant.75) | copy-start | bytes 24580
  32.4 38.6 %copy-start.10 = (f32[2048]{0:T(1024)S(1)}, f32[2048]{0:T(1024)}, u32[]{:S(2)}) copy-start(f32[2048]{0:T(1024)} %constant.73) | copy-start | bytes 24580
  32.4 38.7 %copy-start.7 = (f32[16,2048]{1,0:T(8,128)S(1)}, f32[16,2048]{1,0:T(8,128)}, u32[]{:S(2)}) copy-start(f32[16,2048]{1,0:T(8,128)} %constant.52.clone.powers) | copy-start | bytes 393220
  32.5 38.7 %copy-start.8 = (f32[8,2048]{1,0:T(8,128)S(1)}, f32[8,2048]{1,0:T(8,128)}, u32[]{:S(2)}) copy-start(f32[8,2048]{1,0:T(8,128)} %constant.54.clone.segs_back) | copy-start | bytes 196612
  47.3 8.6 %collective-permute-start.6 = (f32[2,2,2048]{2,1,0:T(2,128)S(1)}, f32[2,2,2048]{2,1,0:T(2,128)S(1)}, u32[]{:S(2)}, u32[]{:S(2)}) collective-permute-start(f32[2,2,2048]{2,1,0:T(2,128)S(1)} %get-tuple-element.21), channel_id=1, source_target_pairs={{0,1},{1,0},{2,3},{3,2},{4,5},{5,4},{6,7},{7,6},{8,9},{9,8},{10,11... | collective-permute-start | bytes 98312 | tf_op jit(solution)/shard_map/ppermute | solution.py:730
  55.9 5.0 %collective-permute-start.7 = (f32[2,2,2048]{2,1,0:T(2,128)S(1)}, f32[2,2,2048]{2,1,0:T(2,128)S(1)}, u32[]{:S(2)}, u32[]{:S(2)}) collective-permute-start(f32[2,2,2048]{2,1,0:T(2,128)S(1)} %pad_maximum_fusion), channel_id=1, source_target_pairs={{0,2},{1,3},{2,0},{3,1},{4,6},{5,7},{6,4},{7,5},{8,10},{9,11},{10,... | collective-permute-start | bytes 98312 | tf_op jit(solution)/shard_map/ppermute | solution.py:730
  61.0 5.1 %collective-permute-start.8 = (f32[2,2,2048]{2,1,0:T(2,128)S(1)}, f32[2,2,2048]{2,1,0:T(2,128)S(1)}, u32[]{:S(2)}, u32[]{:S(2)}) collective-permute-start(f32[2,2,2048]{2,1,0:T(2,128)S(1)} %pad_maximum_fusion.1), channel_id=1, source_target_pairs={{0,4},{1,5},{2,6},{3,7},{4,0},{5,1},{6,2},{7,3},{8,12},{9,13},{10,... | collective-permute-start | bytes 98312 | tf_op jit(solution)/shard_map/ppermute | solution.py:730
  66.1 4.9 %collective-permute-start.9 = (f32[2,2,2048]{2,1,0:T(2,128)S(1)}, f32[2,2,2048]{2,1,0:T(2,128)S(1)}, u32[]{:S(2)}, u32[]{:S(2)}) collective-permute-start(f32[2,2,2048]{2,1,0:T(2,128)S(1)} %pad_maximum_fusion.2), channel_id=1, source_target_pairs={{0,8},{1,9},{2,10},{3,11},{4,12},{5,13},{6,14},{7,15},{8,0},{9,1},... | collective-permute-start | bytes 98312 | tf_op jit(solution)/shard_map/ppermute | solution.py:730

commit v3 on v2

--- a/solution.py
+++ b/solution.py
@@ -23,12 +23,12 @@
 SMEM_SPEC = pl.BlockSpec(memory_space=pltpu.SMEM)
 ANY_SPEC = pl.BlockSpec(memory_space=pl.ANY)
 PARAMS = pltpu.CompilerParams(vmem_limit_bytes=26 * 1024 * 1024)
-UPDATE_PARAMS = pltpu.CompilerParams(vmem_limit_bytes=44 * 1024 * 1024)
+UPDATE_PARAMS = pltpu.CompilerParams(vmem_limit_bytes=32 * 1024 * 1024)
 PHASE_PARAMS = pltpu.CompilerParams(vmem_limit_bytes=46 * 1024 * 1024)
 DIGIT = 64
 CODE_ROWS = 16
 FIELDS = 4
-BATCH = 8
+BATCH = 16
 
 
 def cost(micros):
@@ -345,11 +345,11 @@
 
 def update_kernel(reach, center, *refs):
     tabs = refs[:reach]
-    field, package, halo, scan, segs, tables, *rest = refs[reach:]
+    field, package, halo, scan, segs, table, *rest = refs[reach:]
     tabs = tabs[:center] + (None,) + tabs[center:]
     pieces = rest[: reach + 1]
     updated, inner, carry_y, carry_z, ends = rest[reach + 1 : reach + 6]
-    ext, col_bond, source, edge, rows_in, ints, table, load_sems, store_sems, table_sems = rest[reach + 6 :]
+    ext, col_bond, source, edge, rows_in, ints, load_sems, store_sems = rest[reach + 6 :]
     angles, _, strip, grid = field.shape
     blocks = grid // LANES
     half_blocks = blocks // 2
@@ -376,18 +376,9 @@
             store_sems.at[a, b],
         )
 
-    def load_table(h, k):
-        return pltpu.make_async_copy(
-            tables.at[0, k, h], table.at[k, h], table_sems.at[k, h]
-        )
-
     for a in range(angles):
         for b in range(blocks):
             load(a, b).start()
-    for h in range(2):
-        for k in range(2):
-            load_table(h, k).start()
-
     halo_rows = halo.shape[0] // 3
     top = sum(halo[i * halo_rows : (i + 1) * halo_rows].astype(f32) for i in range(3))
     per_row = grid // frame
@@ -485,7 +476,7 @@
                     source[a, b, rows[i]] = values[i]
             return 0
 
-        lax.fori_loop(0, blocks, columns, 0)
+        lax.fori_loop(0, blocks, columns, 0, unroll=2)
 
     def fold(b, _):
         lanes = pl.ds(pl.multiple_of(b * LANES, LANES), LANES)
@@ -518,13 +509,11 @@
             rows_in[h, count + at : count + at + 2 * PAD, lanes] = low
         return 0
 
-    lax.fori_loop(0, half_blocks, fold, 0)
+    lax.fori_loop(0, half_blocks, fold, 0, unroll=2)
 
     wide = min(2 * LANES, half)
     sub = lax.broadcasted_iota(jnp.int32, (SEG, wide), 0)
     for h in range(2):
-        for k in range(2):
-            load_table(h, k).wait()
 
         def transform(c, _, h=h):
             lanes = pl.ds(pl.multiple_of(c * wide, wide), wide)
@@ -564,7 +553,7 @@
                 ends[1, a : a + 1, spots] = tail_y[SEG - 1 : SEG] + scan[6:7, spots] * above
             return 0
 
-        lax.fori_loop(0, half // wide, transform, 0)
+        lax.fori_loop(0, half // wide, transform, 0, unroll=4)
 
     for a in range(angles):
         for b in range(blocks):
@@ -587,9 +576,7 @@
         ],
         in_specs=[SMEM_SPEC] * reach
         + [ANY_SPEC]
-        + [VMEM_SPEC] * 4
-        + [ANY_SPEC]
-        + [VMEM_SPEC] * (reach + 1),
+        + [VMEM_SPEC] * (reach + 6),
         out_specs=[ANY_SPEC] + [VMEM_SPEC] * 4,
         scratch_shapes=[
             pltpu.VMEM((angles, 2, blocks + 1, strip + 2 * PAD, LANES), f32),
@@ -598,10 +585,8 @@
             pltpu.VMEM((angles, blocks, 1, LANES), f32),
             pltpu.VMEM((2, 2 * (angles * strip + 2 * PAD), half), bf16),
             pltpu.VMEM((1, LANES), jnp.int32),
-            pltpu.VMEM(tables.shape[1:], bf16),
             pltpu.SemaphoreType.DMA((angles, blocks)),
             pltpu.SemaphoreType.DMA((angles, blocks)),
-            pltpu.SemaphoreType.DMA((2, 2)),
         ],
         compiler_params=UPDATE_PARAMS,
         cost_estimate=cost(14),
@@ -648,7 +633,7 @@
                 )
         return 0
 
-    lax.fori_loop(0, 2 * half_blocks, solve, 0)
+    lax.fori_loop(0, 2 * half_blocks, solve, 0, unroll=2)
 
     def split(b, _):
         lanes = pl.ds(pl.multiple_of(b * LANES, LANES), LANES)
@@ -659,7 +644,7 @@
                 rows_in[h, count + a * strip : count + (a + 1) * strip, lanes] = low
         return 0
 
-    lax.fori_loop(0, half_blocks, split, 0)
+    lax.fori_loop(0, half_blocks, split, 0, unroll=2)
 
     def back(c, _):
         lanes = pl.ds(pl.multiple_of(c * wide, wide), wide)
@@ -683,7 +668,7 @@
             store(c, side).start()
         return 0
 
-    lax.fori_loop(0, chunks, back, 0)
+    lax.fori_loop(0, chunks, back, 0, unroll=4)
     for c in range(chunks):
         for side in range(2):
             store(c, side).wait()
@@ -753,6 +738,7 @@
     reach = frame // strip
     center = reach // 2
     halves = cosine_halves(grid)
+    forward = jnp.asarray(split_table(np.swapaxes(halves, 1, 2)))
     tables = jnp.asarray(np.stack([split_table(np.swapaxes(halves, 1, 2)), split_table(halves)]))
     scan, powers, segs, segs_back, strips, closing = (
         jnp.asarray(x) for x in decay_tables(grid, strip)
@@ -787,7 +773,7 @@
         top,
         scan,
         segs,
-        tables,
+        forward,
         pieces,
         center,
     )

time: 77.8 us -> 73.8 us (0.949); the launches traced: 78.1 us -> 73.2 us
  Pallas kernels: 24.7 us -> 20.8 us
    pallas_call x1, Pallas kernels: 14.8 us -> 11.1 us  [run_update(): pl.pallas_call(functools.partial(update_kernel, reach, center), out_shape...]
    unnamed x30 -> x32, local copies, waits for them, and re-layouts: 3.33 us -> 3.33 us
where the time goes in v3:
time: 73.8 us; the launch traced here: 73.2 us
  starting transfers between devices  36.7 us (50%)
  Pallas kernels  20.8 us (28%)
  waiting for transfers between devices  8.43 us (11%)
  local copies, waits for them, and re-layouts  5.24 us (7%)
  between operations  1.76 us (2%)
    ppermute x6, starting transfers between devices, passed_along(): return lax.ppermute(x, 'tile', pairs)  21.5 us
    ppermute x4, starting transfers between devices, entering_values(): lax.ppermute(jnp.stack([head, tail]), 'tile', [(i, i ^ width) for i in ra...  15.2 us
    pallas_call x1, Pallas kernels, run_update(): pl.pallas_call(functools.partial(update_kernel, reach, center), out_shape...  11.1 us
    pallas_call x1, Pallas kernels, run_phase(): pl.pallas_call(phase_kernel, out_shape=jax.ShapeDtypeStruct((angles, stri...  6.71 us
    ppermute x4, waiting for transfers between devices, entering_values(): lax.ppermute(jnp.stack([head, tail]), 'tile', [(i, i ^ width) for i in ra...  5.79 us
    unnamed x32, local copies, waits for them, and re-layouts  3.33 us
    ppermute x6, waiting for transfers between devices, passed_along(): return lax.ppermute(x, 'tile', pairs)  2.64 us
    pallas_call x2, Pallas kernels, extract(): pl.pallas_call(functools.partial(extract_kernel, coded), out_shape=[windo...  1.58 us
  transfers between devices with their start and end apart: 10, of which 6 were waited for; matrix products, arithmetic and copies ran while one was open for 2% of the time, Pallas kernels for 2%

profile of v3, /device:TPU:0, one launch (start us, length us, event | category | flops | bytes accessed | tf_op | source)
XLA Modules:
  0.0 73.2 jit_solution(3566361655033575317)
XLA Ops:
  1.3 0.7 concatenate.3.tab.refs_0_
  2.0 4.9 %collective-permute-start = (s32[2,4]{1,0:T(2,128)S(1)}, s32[2,4]{1,0:T(2,128)S(1)}, u32[]{:S(2)}, u32[]{:S(2)}) collective-permute-start(s32[2,4]{1,0:T(2,128)S(1)} %concatenate.3.tab.refs_0_), channel_id=1, source_target_pairs={{0,2},{1,3},{2,4},{3,5},{4,6},{5,7},{6,8},{7,9},{8,10},{9,11},{10,... | collective-permute-start | bytes 104 | tf_op jit(solution)/shard_map/ppermute | solution.py:703
  6.8 0.0 copy-start
  6.8 2.2 %copy-done = f32[2,2,128,2048]{3,2,1,0:T(8,128)S(1)} copy-done((f32[2,2,128,2048]{3,2,1,0:T(8,128)S(1)}, f32[2,2,128,2048]{3,2,1,0:T(8,128)}, u32[]{:S(2)}) %copy-start) | copy-done | bytes 4194328
  9.0 0.0 copy-start.1
  9.0 0.0 copy-start.15
  9.0 1.1 %pack.1.rest_0_ = bf16[624,256]{1,0:T(8,128)(2,1)S(1)} custom-call(s32[2,4]{1,0:T(2,128)S(1)} %concatenate.3.tab.refs_0_, f32[2,2,128,2048]{3,2,1,0:T(8,128)S(1)} %copy-done), custom_call_target="tpu_custom_call" | custom-call | bytes 18000000 | tf_op jit(solution)/shard_map/pack/pallas_call | solution.py:179
  10.1 0.0 copy-start.3
  10.1 0.0 copy-start.4
  10.1 0.0 copy-start.5
  10.1 0.0 collective-permute-done.tab.refs_1_
  10.1 1.1 %copy-done.1 = f32[2,2,128,2048]{3,2,1,0:T(8,128)S(1)} copy-done((f32[2,2,128,2048]{3,2,1,0:T(8,128)S(1)}, f32[2,2,128,2048]{3,2,1,0:T(8,128)}, u32[]{:S(2)}) %copy-start.1) | copy-done | bytes 4194328
  11.2 0.0 copy-start.2
  11.2 1.0 %extract.2 = (bf16[2,2,128,256]{3,2,1,0:T(8,128)(2,1)S(1)}, bf16[624,256]{1,0:T(8,128)(2,1)S(1)}) custom-call(s32[2,4]{1,0:T(2,128)S(1)} %collective-permute-done.tab.refs_1_, f32[2,2,128,2048]{3,2,1,0:T(8,128)S(1)} %copy-done.1, bf16[624,256]{1,0:T(8,128)(2,1)S(1)} %pack.1.rest_0_), custom_call_target="tpu_custom_call", output_to_operand_aliasing={{1}: (2, {})} | custom-call | bytes 6000000 | tf_op jit(solution)/shard_map/extract/pallas_call | solution.py:212
  12.2 0.0 copy-start.6
  12.2 0.0 copy-start.7
  12.2 1.9 %collective-permute-start.1 = (bf16[624,256]{1,0:T(8,128)(2,1)S(1)}, bf16[624,256]{1,0:T(8,128)(2,1)S(1)}, u32[]{:S(2)}, u32[]{:S(2)}) collective-permute-start(bf16[624,256]{1,0:T(8,128)(2,1)S(1)} %get-tuple-element.12), channel_id=1, source_target_pairs={{0,1},{1,2},{2,3},{3,4},{4,5},{5,6},{6,7},{7,8},{8,9},{9,10},{10,1... | collective-permute-start | bytes 958472 | tf_op jit(solution)/shard_map/ppermute | solution.py:703
  14.1 0.0 copy-done.15
  14.1 3.9 %collective-permute-start.2 = (bf16[2,256,256]{2,1,0:T(8,128)(2,1)S(1)}, bf16[2,256,256]{2,1,0:T(8,128)(2,1)S(1)}, u32[]{:S(2)}, u32[]{:S(2)}) collective-permute-start(bf16[2,256,256]{2,1,0:T(8,128)(2,1)S(1)} %copy-done.15), channel_id=1, source_target_pairs={{0,1},{1,2},{2,3},{3,4},{4,5},{5,6},{6,7},{7,8},{8,9},{9,10},{10,1... | collective-permute-start | bytes 786440 | tf_op jit(solution)/shard_map/ppermute | solution.py:703
  18.0 1.3 %collective-permute-start.3 = (bf16[2,2,128,256]{3,2,1,0:T(8,128)(2,1)S(1)}, bf16[2,2,128,256]{3,2,1,0:T(8,128)(2,1)S(1)}, u32[]{:S(2)}, u32[]{:S(2)}) collective-permute-start(bf16[2,2,128,256]{3,2,1,0:T(8,128)(2,1)S(1)} %get-tuple-element.13), channel_id=1, source_target_pairs={{1,0},{2,1},{3,2},{4,3},{5,4},{6,5},{7,6},{8,7},{9,8},{10,9},{11,1... | collective-permute-start | bytes 786440 | tf_op jit(solution)/shard_map/ppermute | solution.py:703
  19.3 0.0 collective-permute-done.1.tab.package.refs_3_
  19.3 0.6 extract.3.rest_0_
  19.9 0.0 collective-permute-done.2.measured
  19.9 1.5 %collective-permute-done.3.rest_1_ = bf16[2,2,128,256]{3,2,1,0:T(8,128)(2,1)S(1)} collective-permute-done((bf16[2,2,128,256]{3,2,1,0:T(8,128)(2,1)S(1)}, bf16[2,2,128,256]{3,2,1,0:T(8,128)(2,1)S(1)}, u32[]{:S(2)}, u32[]{:S(2)}) %collective-permute-start.3) | collective-permute-done | bytes 262176 | tf_op jit(solution)/shard_map/ppermute | solution.py:703
  21.4 0.0 copy-done.3
  21.4 0.0 copy-done.4
  21.4 0.0 copy-done.5
  21.4 0.4 frames.1
  21.8 1.3 %collective-permute-start.4 = (bf16[2,2,144,256]{3,2,1,0:T(8,128)(2,1)S(1)}, bf16[2,2,144,256]{3,2,1,0:T(8,128)(2,1)S(1)}, u32[]{:S(2)}, u32[]{:S(2)}) collective-permute-start(bf16[2,2,144,256]{3,2,1,0:T(8,128)(2,1)S(1)} %get-tuple-element.14), channel_id=1, source_target_pairs={{1,0},{2,1},{3,2},{4,3},{5,4},{6,5},{7,6},{8,7},{9,8},{10,9},{11,1... | collective-permute-start | bytes 884744 | tf_op jit(solution)/shard_map/ppermute | solution.py:703
  23.1 8.3 %collective-permute-start.5 = (bf16[2,2,144,256]{3,2,1,0:T(8,128)(2,1)S(1)}, bf16[2,2,144,256]{3,2,1,0:T(8,128)(2,1)S(1)}, u32[]{:S(2)}, u32[]{:S(2)}) collective-permute-start(bf16[2,2,144,256]{3,2,1,0:T(8,128)(2,1)S(1)} %get-tuple-element.16), channel_id=1, source_target_pairs={{0,1},{1,2},{2,3},{3,4},{4,5},{5,6},{6,7},{7,8},{8,9},{9,10},{10,1... | collective-permute-start | bytes 884744 | tf_op jit(solution)/shard_map/ppermute | solution.py:703
  31.4 0.0 collective-permute-done.4.refs_8_
  31.4 1.1 %collective-permute-done.5.refs_10_ = bf16[2,2,144,256]{3,2,1,0:T(8,128)(2,1)S(1)} collective-permute-done((bf16[2,2,144,256]{3,2,1,0:T(8,128)(2,1)S(1)}, bf16[2,2,144,256]{3,2,1,0:T(8,128)(2,1)S(1)}, u32[]{:S(2)}, u32[]{:S(2)}) %collective-permute-start.5) | collective-permute-done | bytes 294944 | tf_op jit(solution)/shard_map/ppermute | solution.py:703
  32.5 0.0 copy-done.2
  32.5 0.0 copy-done.6
  32.5 0.0 copy-done.7
  32.5 0.0 copy-start.14
  32.5 0.0 copy-start.13
  32.6 0.0 copy-start.12
  32.6 0.0 copy-start.10
  32.6 0.0 copy-start.11
  32.6 0.0 copy-start.8
  32.6 0.0 copy-start.9
  32.6 11.1 %update.1 = (f32[2,2,128,2048]{3,2,1,0:T(8,128)}, f32[2,128,2048]{2,1,0:T(8,128)S(1)}, f32[2,8,2048]{2,1,0:T(8,128)S(1)}, f32[2,8,2048]{2,1,0:T(8,128)S(1)}, f32[2,2,2048]{2,1,0:T(2,128)S(1)}) custom-call(s32[2,4]{1,0:T(2,128)S(1)} %concatenate.3.tab.refs_0_, s32[2,4]{1,0:T(2,128)S(1)} %collective-permute-done.tab.refs_1_, ...), custom_call_target="tpu_custom_call" | custom-call | bytes 42000000 | tf_op jit(solution)/shard_map/update/pallas_call | solution.py:568
  43.7 7.6 %collective-permute-start.6 = (f32[2,2,2048]{2,1,0:T(2,128)S(1)}, f32[2,2,2048]{2,1,0:T(2,128)S(1)}, u32[]{:S(2)}, u32[]{:S(2)}) collective-permute-start(f32[2,2,2048]{2,1,0:T(2,128)S(1)} %get-tuple-element.21), channel_id=1, source_target_pairs={{0,1},{1,0},{2,3},{3,2},{4,5},{5,4},{6,7},{7,6},{8,9},{9,8},{10,11... | collective-permute-start | bytes 98312 | tf_op jit(solution)/shard_map/ppermute | solution.py:715
  51.3 0.9 %collective-permute-done.6 = f32[2,2,2048]{2,1,0:T(2,128)S(1)} collective-permute-done((f32[2,2,2048]{2,1,0:T(2,128)S(1)}, f32[2,2,2048]{2,1,0:T(2,128)S(1)}, u32[]{:S(2)}, u32[]{:S(2)}) %collective-permute-start.6) | collective-permute-done | bytes 32800 | tf_op jit(solution)/shard_map/ppermute | solution.py:715
  52.2 0.0 copy-done.14
  52.3 3.0 %collective-permute-start.7 = (f32[2,2,2048]{2,1,0:T(2,128)S(1)}, f32[2,2,2048]{2,1,0:T(2,128)S(1)}, u32[]{:S(2)}, u32[]{:S(2)}) collective-permute-start(f32[2,2,2048]{2,1,0:T(2,128)S(1)} %pad_maximum_fusion), channel_id=1, source_target_pairs={{0,2},{1,3},{2,0},{3,1},{4,6},{5,7},{6,4},{7,5},{8,10},{9,11},{10,... | collective-permute-start | bytes 98312 | tf_op jit(solution)/shard_map/ppermute | solution.py:715
  55.2 1.9 %collective-permute-done.7 = f32[2,2,2048]{2,1,0:T(2,128)S(1)} collective-permute-done((f32[2,2,2048]{2,1,0:T(2,128)S(1)}, f32[2,2,2048]{2,1,0:T(2,128)S(1)}, u32[]{:S(2)}, u32[]{:S(2)}) %collective-permute-start.7) | collective-permute-done | bytes 32800 | tf_op jit(solution)/shard_map/ppermute | solution.py:715
  57.1 0.0 copy-done.13
  57.2 1.8 %collective-permute-start.8 = (f32[2,2,2048]{2,1,0:T(2,128)S(1)}, f32[2,2,2048]{2,1,0:T(2,128)S(1)}, u32[]{:S(2)}, u32[]{:S(2)}) collective-permute-start(f32[2,2,2048]{2,1,0:T(2,128)S(1)} %pad_maximum_fusion.1), channel_id=1, source_target_pairs={{0,4},{1,5},{2,6},{3,7},{4,0},{5,1},{6,2},{7,3},{8,12},{9,13},{10,... | collective-permute-start | bytes 98312 | tf_op jit(solution)/shard_map/ppermute | solution.py:715
  59.0 2.2 %collective-permute-done.8 = f32[2,2,2048]{2,1,0:T(2,128)S(1)} collective-permute-done((f32[2,2,2048]{2,1,0:T(2,128)S(1)}, f32[2,2,2048]{2,1,0:T(2,128)S(1)}, u32[]{:S(2)}, u32[]{:S(2)}) %collective-permute-start.8) | collective-permute-done | bytes 32800 | tf_op jit(solution)/shard_map/ppermute | solution.py:715
  61.2 0.0 copy-done.12
  61.2 2.8 %collective-permute-start.9 = (f32[2,2,2048]{2,1,0:T(2,128)S(1)}, f32[2,2,2048]{2,1,0:T(2,128)S(1)}, u32[]{:S(2)}, u32[]{:S(2)}) collective-permute-start(f32[2,2,2048]{2,1,0:T(2,128)S(1)} %pad_maximum_fusion.2), channel_id=1, source_target_pairs={{0,8},{1,9},{2,10},{3,11},{4,12},{5,13},{6,14},{7,15},{8,0},{9,1},... | collective-permute-start | bytes 98312 | tf_op jit(solution)/shard_map/ppermute | solution.py:715
  64.0 1.2 %constant_dynamic-slice_fusion.7 = (f32[1,2048]{1,0:T(1,128)S(1)}, f32[1,2048]{1,0:T(1,128)S(1)}, f32[1,2048]{1,0:T(1,128)S(1)}, f32[1,2048]{1,0:T(1,128)S(1)}, ...) fusion(f32[17,2048]{1,0:T(8,128)} %constant.58.clone, ...), kind=kLoop, calls=%fused_computation.21 | loop fusion | bytes 131104 | tf_op jit(solution)/shard_map/dynamic_slice | solution.py:712
  65.2 0.9 %collective-permute-done.9 = f32[2,2,2048]{2,1,0:T(2,128)S(1)} collective-permute-done((f32[2,2,2048]{2,1,0:T(2,128)S(1)}, f32[2,2,2048]{2,1,0:T(2,128)S(1)}, u32[]{:S(2)}, u32[]{:S(2)}) %collective-permute-start.9) | collective-permute-done | bytes 32800 | tf_op jit(solution)/shard_map/ppermute | solution.py:715
  66.1 0.0 copy-done.10
  66.1 0.0 copy-done.11
  66.1 0.1 multiply_add_fusion
  66.2 0.1 multiply_add_fusion.1
  66.3 0.0 copy-done.8
  66.3 0.0 copy-done.9
  66.3 6.7 %phase.1 = f32[2,128,2048]{2,1,0:T(8,128)} custom-call(f32[2,128,2048]{2,1,0:T(8,128)S(1)} %get-tuple-element.18.inner, f32[2,8,2048]{2,1,0:T(8,128)S(1)} %get-tuple-element.19.carry_y, f32[2,8,2048]{2,1,0:T(8,128)S(1)} %get-tuple-element.20.carry_z, f32[2,2,2048]{2,1,0:T(2,128)S(1)} %pad_maximum_fusion.3.enter, f32[7,2048]{1,0:T(8,128)S(1)} %copy-done.7, ...), custom_call_target="tpu_custom_call" | custom-call | bytes 21000000 | tf_op jit(solution)/shard_map/phase/pallas_call | solution.py:681
  (8 shorter events, 0.2 us)
Async XLA Ops:
  2.0 8.2 %collective-permute-start = (s32[2,4]{1,0:T(2,128)S(1)}, s32[2,4]{1,0:T(2,128)S(1)}, u32[]{:S(2)}, u32[]{:S(2)}) collective-permute-start(s32[2,4]{1,0:T(2,128)S(1)} %concatenate.3.tab.refs_0_), channel_id=1, source_target_pairs={{0,2},{1,3},{2,4},{3,5},{4,6},{5,7},{6,8},{7,9},{8,10},{9,11},{10,... | collective-permute-start | bytes 104 | tf_op jit(solution)/shard_map/ppermute | solution.py:703
  6.8 2.2 %copy-start = (f32[2,2,128,2048]{3,2,1,0:T(8,128)S(1)}, f32[2,2,128,2048]{3,2,1,0:T(8,128)}, u32[]{:S(2)}) copy-start(f32[2,2,128,2048]{3,2,1,0:T(8,128)} %refs_2_.1) | copy-start | bytes 12582916
  9.0 2.2 %copy-start.1 = (f32[2,2,128,2048]{3,2,1,0:T(8,128)S(1)}, f32[2,2,128,2048]{3,2,1,0:T(8,128)}, u32[]{:S(2)}) copy-start(f32[2,2,128,2048]{3,2,1,0:T(8,128)} %refs_2_.1) | copy-start | bytes 12582916
  9.0 5.1 %copy-start.15 = (bf16[2,256,256]{2,1,0:T(8,128)(2,1)S(1)}, bf16[2,256,256]{2,1,0:T(8,128)(2,1)}, u32[]{:S(2)}) copy-start(bf16[2,256,256]{2,1,0:T(8,128)(2,1)} %param.17) | copy-start | bytes 786436
  10.1 11.3 %copy-start.3 = (f32[2,256,256]{2,1,0:T(8,128)S(1)}, f32[2,256,256]{2,1,0:T(8,128)}, u32[]{:S(2)}) copy-start(f32[2,256,256]{2,1,0:T(8,128)} %probe.1) | copy-start | bytes 1572868
  10.1 11.3 %copy-start.4 = (bf16[512,512]{1,0:T(8,128)(2,1)S(1)}, bf16[512,512]{1,0:T(8,128)(2,1)}, u32[]{:S(2)}) copy-start(bf16[512,512]{1,0:T(8,128)(2,1)} %constant.61.clone.right) | copy-start | bytes 1572868
  10.1 11.3 %copy-start.5 = (bf16[512,512]{1,0:T(8,128)(2,1)S(1)}, bf16[512,512]{1,0:T(8,128)(2,1)}, u32[]{:S(2)}) copy-start(bf16[512,512]{1,0:T(8,128)(2,1)} %constant.60.clone.left) | copy-start | bytes 1572868
  11.2 21.3 %copy-start.2 = (bf16[2,2,1024,1024]{3,2,1,0:T(8,128)(2,1)S(1)}, bf16[2,2,1024,1024]{3,2,1,0:T(8,128)(2,1)}, u32[]{:S(2)}) copy-start(bf16[2,2,1024,1024]{3,2,1,0:T(8,128)(2,1)} %constant.52.clone.refs_7_) | copy-start | bytes 25165828
  12.2 20.4 %copy-start.6 = (f32[8,2048]{1,0:T(8,128)S(1)}, f32[8,2048]{1,0:T(8,128)}, u32[]{:S(2)}) copy-start(f32[8,2048]{1,0:T(8,128)} %constant.56.clone.refs_6_.segs) | copy-start | bytes 196612
  12.2 20.3 %copy-start.7 = (f32[7,2048]{1,0:T(8,128)S(1)}, f32[7,2048]{1,0:T(8,128)}, u32[]{:S(2)}) copy-start(f32[7,2048]{1,0:T(8,128)} %constant.54.clone.refs_5_.scan) | copy-start | bytes 172036
  12.2 7.1 %collective-permute-start.1 = (bf16[624,256]{1,0:T(8,128)(2,1)S(1)}, bf16[624,256]{1,0:T(8,128)(2,1)S(1)}, u32[]{:S(2)}, u32[]{:S(2)}) collective-permute-start(bf16[624,256]{1,0:T(8,128)(2,1)S(1)} %get-tuple-element.12), channel_id=1, source_target_pairs={{0,1},{1,2},{2,3},{3,4},{4,5},{5,6},{6,7},{7,8},{8,9},{9,10},{10,1... | collective-permute-start | bytes 958472 | tf_op jit(solution)/shard_map/ppermute | solution.py:703
  14.1 5.8 %collective-permute-start.2 = (bf16[2,256,256]{2,1,0:T(8,128)(2,1)S(1)}, bf16[2,256,256]{2,1,0:T(8,128)(2,1)S(1)}, u32[]{:S(2)}, u32[]{:S(2)}) collective-permute-start(bf16[2,256,256]{2,1,0:T(8,128)(2,1)S(1)} %copy-done.15), channel_id=1, source_target_pairs={{0,1},{1,2},{2,3},{3,4},{4,5},{5,6},{6,7},{7,8},{8,9},{9,10},{10,1... | collective-permute-start | bytes 786440 | tf_op jit(solution)/shard_map/ppermute | solution.py:703
  18.0 3.4 %collective-permute-start.3 = (bf16[2,2,128,256]{3,2,1,0:T(8,128)(2,1)S(1)}, bf16[2,2,128,256]{3,2,1,0:T(8,128)(2,1)S(1)}, u32[]{:S(2)}, u32[]{:S(2)}) collective-permute-start(bf16[2,2,128,256]{3,2,1,0:T(8,128)(2,1)S(1)} %get-tuple-element.13), channel_id=1, source_target_pairs={{1,0},{2,1},{3,2},{4,3},{5,4},{6,5},{7,6},{8,7},{9,8},{10,9},{11,1... | collective-permute-start | bytes 786440 | tf_op jit(solution)/shard_map/ppermute | solution.py:703
  21.8 9.6 %collective-permute-start.4 = (bf16[2,2,144,256]{3,2,1,0:T(8,128)(2,1)S(1)}, bf16[2,2,144,256]{3,2,1,0:T(8,128)(2,1)S(1)}, u32[]{:S(2)}, u32[]{:S(2)}) collective-permute-start(bf16[2,2,144,256]{3,2,1,0:T(8,128)(2,1)S(1)} %get-tuple-element.14), channel_id=1, source_target_pairs={{1,0},{2,1},{3,2},{4,3},{5,4},{6,5},{7,6},{8,7},{9,8},{10,9},{11,1... | collective-permute-start | bytes 884744 | tf_op jit(solution)/shard_map/ppermute | solution.py:703
  23.1 9.5 %collective-permute-start.5 = (bf16[2,2,144,256]{3,2,1,0:T(8,128)(2,1)S(1)}, bf16[2,2,144,256]{3,2,1,0:T(8,128)(2,1)S(1)}, u32[]{:S(2)}, u32[]{:S(2)}) collective-permute-start(bf16[2,2,144,256]{3,2,1,0:T(8,128)(2,1)S(1)} %get-tuple-element.16), channel_id=1, source_target_pairs={{0,1},{1,2},{2,3},{3,4},{4,5},{5,6},{6,7},{7,8},{8,9},{9,10},{10,1... | collective-permute-start | bytes 884744 | tf_op jit(solution)/shard_map/ppermute | solution.py:703
  32.5 19.7 %copy-start.14 = (f32[2048]{0:T(1024)S(1)}, f32[2048]{0:T(1024)}, u32[]{:S(2)}) copy-start(f32[2048]{0:T(1024)} %constant.70) | copy-start | bytes 24580
  32.5 24.6 %copy-start.13 = (f32[2048]{0:T(1024)S(1)}, f32[2048]{0:T(1024)}, u32[]{:S(2)}) copy-start(f32[2048]{0:T(1024)} %constant.72) | copy-start | bytes 24580
  32.6 28.6 %copy-start.12 = (f32[2048]{0:T(1024)S(1)}, f32[2048]{0:T(1024)}, u32[]{:S(2)}) copy-start(f32[2048]{0:T(1024)} %constant.74) | copy-start | bytes 24580
  32.6 33.5 %copy-start.10 = (f32[2048]{0:T(1024)S(1)}, f32[2048]{0:T(1024)}, u32[]{:S(2)}) copy-start(f32[2048]{0:T(1024)} %constant.78) | copy-start | bytes 24580
  32.6 33.5 %copy-start.11 = (f32[2048]{0:T(1024)S(1)}, f32[2048]{0:T(1024)}, u32[]{:S(2)}) copy-start(f32[2048]{0:T(1024)} %constant.76) | copy-start | bytes 24580
  32.6 33.7 %copy-start.8 = (f32[16,2048]{1,0:T(8,128)S(1)}, f32[16,2048]{1,0:T(8,128)}, u32[]{:S(2)}) copy-start(f32[16,2048]{1,0:T(8,128)} %constant.55.clone.powers) | copy-start | bytes 393220
  32.6 33.7 %copy-start.9 = (f32[8,2048]{1,0:T(8,128)S(1)}, f32[8,2048]{1,0:T(8,128)}, u32[]{:S(2)}) copy-start(f32[8,2048]{1,0:T(8,128)} %constant.57.clone.segs_back) | copy-start | bytes 196612
  43.7 8.5 %collective-permute-start.6 = (f32[2,2,2048]{2,1,0:T(2,128)S(1)}, f32[2,2,2048]{2,1,0:T(2,128)S(1)}, u32[]{:S(2)}, u32[]{:S(2)}) collective-permute-start(f32[2,2,2048]{2,1,0:T(2,128)S(1)} %get-tuple-element.21), channel_id=1, source_target_pairs={{0,1},{1,0},{2,3},{3,2},{4,5},{5,4},{6,7},{7,6},{8,9},{9,8},{10,11... | collective-permute-start | bytes 98312 | tf_op jit(solution)/shard_map/ppermute | solution.py:715
  52.3 4.9 %collective-permute-start.7 = (f32[2,2,2048]{2,1,0:T(2,128)S(1)}, f32[2,2,2048]{2,1,0:T(2,128)S(1)}, u32[]{:S(2)}, u32[]{:S(2)}) collective-permute-start(f32[2,2,2048]{2,1,0:T(2,128)S(1)} %pad_maximum_fusion), channel_id=1, source_target_pairs={{0,2},{1,3},{2,0},{3,1},{4,6},{5,7},{6,4},{7,5},{8,10},{9,11},{10,... | collective-permute-start | bytes 98312 | tf_op jit(solution)/shard_map/ppermute | solution.py:715
  57.2 4.0 %collective-permute-start.8 = (f32[2,2,2048]{2,1,0:T(2,128)S(1)}, f32[2,2,2048]{2,1,0:T(2,128)S(1)}, u32[]{:S(2)}, u32[]{:S(2)}) collective-permute-start(f32[2,2,2048]{2,1,0:T(2,128)S(1)} %pad_maximum_fusion.1), channel_id=1, source_target_pairs={{0,4},{1,5},{2,6},{3,7},{4,0},{5,1},{6,2},{7,3},{8,12},{9,13},{10,... | collective-permute-start | bytes 98312 | tf_op jit(solution)/shard_map/ppermute | solution.py:715
  61.2 4.9 %collective-permute-start.9 = (f32[2,2,2048]{2,1,0:T(2,128)S(1)}, f32[2,2,2048]{2,1,0:T(2,128)S(1)}, u32[]{:S(2)}, u32[]{:S(2)}) collective-permute-start(f32[2,2,2048]{2,1,0:T(2,128)S(1)} %pad_maximum_fusion.2), channel_id=1, source_target_pairs={{0,8},{1,9},{2,10},{3,11},{4,12},{5,13},{6,14},{7,15},{8,0},{9,1},... | collective-permute-start | bytes 98312 | tf_op jit(solution)/shard_map/ppermute | solution.py:715

commit v4 on v3

--- a/solution.py
+++ b/solution.py
@@ -299,8 +299,10 @@
             for k in range(blocks):
                 lanes = slice(k * LANES, (k + 1) * LANES)
                 for j in range(reach + 1):
+                    rim = PAD if j else 0
+                    first = j * strip + 2 * PAD
                     pieces[j][slot, part, :, lanes] = update_buf[
-                        part, k, j * strip + PAD : (j + 1) * strip + 3 * PAD
+                        part, k, first - rim : first + strip + rim
                     ].astype(pieces[j].dtype)
 
 
@@ -310,7 +312,7 @@
     left, right = fourier_blocks(frame)
     rows = (reach + 1) * strip
     piece = lambda j: jax.ShapeDtypeStruct(
-        (caps, 2, strip + 2 * PAD, frame), f32 if j == center else bf16
+        (caps, 2, strip + (2 * PAD if j else 0), frame), f32 if j == center else bf16
     )
     return pl.pallas_call(
         functools.partial(frame_kernel, reach),
@@ -394,8 +396,6 @@
         for b in range(blocks):
             load(a, b).wait()
 
-    rows = strip + 2 * PAD
-
     def add_piece(piece, tab, slot):
         @pl.when(slot < tab(0, 3))
         def _():
@@ -405,10 +405,12 @@
             shift = column - block * LANES
             for part in range(2):
                 values = piece[slot, part].astype(f32)
+                rows = values.shape[0]
+                first = PAD + (strip - rows) // 2
                 values = jnp.concatenate([values, jnp.zeros((rows, LANES), f32)], axis=1)
                 values = pltpu.roll(values, shift, axis=1)
                 for k in range(frame_blocks + 1):
-                    spot = ext.at[angle, part, block + k]
+                    spot = ext.at[angle, part, block + k, first : first + rows]
                     spot[...] += values[:, k * LANES : (k + 1) * LANES]
 
     for slot in range(caps):

time: 73.8 us -> 72.6 us (0.984)
  starting transfers between devices: 36.7 us -> 35.1 us
  waiting for transfers between devices: 8.43 us -> 9.38 us
    ppermute x6, waiting for transfers between devices: 2.64 us -> 3.6 us  [passed_along(): return lax.ppermute(x, 'tile', pairs)]
    ppermute x4, starting transfers between devices: 15.2 us -> 14.3 us  [entering_values(): lax.ppermute(jnp.stack([head, tail]), 'tile', [(i, i ^ width) for i in ra...]
where the time goes in v4:
time: 72.6 us
  starting transfers between devices  35.1 us (48%)
  Pallas kernels  20.8 us (29%)
  waiting for transfers between devices  9.38 us (13%)
  local copies, waits for them, and re-layouts  5.25 us (7%)
  between operations  1.77 us (2%)
    ppermute x6, starting transfers between devices, passed_along(): return lax.ppermute(x, 'tile', pairs)  20.8 us
    ppermute x4, starting transfers between devices, entering_values(): lax.ppermute(jnp.stack([head, tail]), 'tile', [(i, i ^ width) for i in ra...  14.3 us
    pallas_call x1, Pallas kernels, run_update(): pl.pallas_call(functools.partial(update_kernel, reach, center), out_shape...  11.1 us
    pallas_call x1, Pallas kernels, run_phase(): pl.pallas_call(phase_kernel, out_shape=jax.ShapeDtypeStruct((angles, stri...  6.71 us
    ppermute x4, waiting for transfers between devices, entering_values(): lax.ppermute(jnp.stack([head, tail]), 'tile', [(i, i ^ width) for i in ra...  5.78 us
    ppermute x6, waiting for transfers between devices, passed_along(): return lax.ppermute(x, 'tile', pairs)  3.6 us
    unnamed x32, local copies, waits for them, and re-layouts  3.34 us
    pallas_call x2, Pallas kernels, extract(): pl.pallas_call(functools.partial(extract_kernel, coded), out_shape=[windo...  1.58 us
  transfers between devices with their start and end apart: 10, of which 6 were waited for; matrix products, arithmetic and copies ran while one was open for 2% of the time, Pallas kernels for 2%

profile of v4, /device:TPU:0, one launch (start us, length us, event | category | flops | bytes accessed | tf_op | source)
XLA Modules:
  0.0 72.6 jit_solution(3979022993819606910)
XLA Ops:
  1.3 0.7 concatenate.3.tab.refs_0_
  2.0 4.9 %collective-permute-start = (s32[2,4]{1,0:T(2,128)S(1)}, s32[2,4]{1,0:T(2,128)S(1)}, u32[]{:S(2)}, u32[]{:S(2)}) collective-permute-start(s32[2,4]{1,0:T(2,128)S(1)} %concatenate.3.tab.refs_0_), channel_id=1, source_target_pairs={{0,2},{1,3},{2,4},{3,5},{4,6},{5,7},{6,8},{7,9},{8,10},{9,11},{10,... | collective-permute-start | bytes 104 | tf_op jit(solution)/shard_map/ppermute | solution.py:705
  6.8 0.0 copy-start
  6.8 2.2 %copy-done = f32[2,2,128,2048]{3,2,1,0:T(8,128)S(1)} copy-done((f32[2,2,128,2048]{3,2,1,0:T(8,128)S(1)}, f32[2,2,128,2048]{3,2,1,0:T(8,128)}, u32[]{:S(2)}) %copy-start) | copy-done | bytes 4194328
  9.0 0.0 copy-start.1
  9.0 0.0 copy-start.15
  9.0 1.1 %pack.1.rest_0_ = bf16[624,256]{1,0:T(8,128)(2,1)S(1)} custom-call(s32[2,4]{1,0:T(2,128)S(1)} %concatenate.3.tab.refs_0_, f32[2,2,128,2048]{3,2,1,0:T(8,128)S(1)} %copy-done), custom_call_target="tpu_custom_call" | custom-call | bytes 18000000 | tf_op jit(solution)/shard_map/pack/pallas_call | solution.py:179
  10.1 0.0 copy-start.3
  10.1 0.0 copy-start.4
  10.1 0.0 copy-start.5
  10.1 0.0 collective-permute-done.tab.refs_1_
  10.1 1.1 %copy-done.1 = f32[2,2,128,2048]{3,2,1,0:T(8,128)S(1)} copy-done((f32[2,2,128,2048]{3,2,1,0:T(8,128)S(1)}, f32[2,2,128,2048]{3,2,1,0:T(8,128)}, u32[]{:S(2)}) %copy-start.1) | copy-done | bytes 4194328
  11.2 0.0 copy-start.2
  11.2 1.0 %extract.2 = (bf16[2,2,128,256]{3,2,1,0:T(8,128)(2,1)S(1)}, bf16[624,256]{1,0:T(8,128)(2,1)S(1)}) custom-call(s32[2,4]{1,0:T(2,128)S(1)} %collective-permute-done.tab.refs_1_, f32[2,2,128,2048]{3,2,1,0:T(8,128)S(1)} %copy-done.1, bf16[624,256]{1,0:T(8,128)(2,1)S(1)} %pack.1.rest_0_), custom_call_target="tpu_custom_call", output_to_operand_aliasing={{1}: (2, {})} | custom-call | bytes 6000000 | tf_op jit(solution)/shard_map/extract/pallas_call | solution.py:212
  12.2 0.0 copy-start.6
  12.2 0.0 copy-start.7
  12.2 1.9 %collective-permute-start.1 = (bf16[624,256]{1,0:T(8,128)(2,1)S(1)}, bf16[624,256]{1,0:T(8,128)(2,1)S(1)}, u32[]{:S(2)}, u32[]{:S(2)}) collective-permute-start(bf16[624,256]{1,0:T(8,128)(2,1)S(1)} %get-tuple-element.12), channel_id=1, source_target_pairs={{0,1},{1,2},{2,3},{3,4},{4,5},{5,6},{6,7},{7,8},{8,9},{9,10},{10,1... | collective-permute-start | bytes 958472 | tf_op jit(solution)/shard_map/ppermute | solution.py:705
  14.1 0.0 copy-done.15
  14.1 3.9 %collective-permute-start.2 = (bf16[2,256,256]{2,1,0:T(8,128)(2,1)S(1)}, bf16[2,256,256]{2,1,0:T(8,128)(2,1)S(1)}, u32[]{:S(2)}, u32[]{:S(2)}) collective-permute-start(bf16[2,256,256]{2,1,0:T(8,128)(2,1)S(1)} %copy-done.15), channel_id=1, source_target_pairs={{0,1},{1,2},{2,3},{3,4},{4,5},{5,6},{6,7},{7,8},{8,9},{9,10},{10,1... | collective-permute-start | bytes 786440 | tf_op jit(solution)/shard_map/ppermute | solution.py:705
  18.0 1.3 %collective-permute-start.3 = (bf16[2,2,128,256]{3,2,1,0:T(8,128)(2,1)S(1)}, bf16[2,2,128,256]{3,2,1,0:T(8,128)(2,1)S(1)}, u32[]{:S(2)}, u32[]{:S(2)}) collective-permute-start(bf16[2,2,128,256]{3,2,1,0:T(8,128)(2,1)S(1)} %get-tuple-element.13), channel_id=1, source_target_pairs={{1,0},{2,1},{3,2},{4,3},{5,4},{6,5},{7,6},{8,7},{9,8},{10,9},{11,1... | collective-permute-start | bytes 786440 | tf_op jit(solution)/shard_map/ppermute | solution.py:705
  19.3 0.0 collective-permute-done.1.tab.package.refs_3_
  19.3 0.6 extract.3.rest_0_
  19.9 0.0 collective-permute-done.2.measured
  19.9 1.5 %collective-permute-done.3.rest_1_ = bf16[2,2,128,256]{3,2,1,0:T(8,128)(2,1)S(1)} collective-permute-done((bf16[2,2,128,256]{3,2,1,0:T(8,128)(2,1)S(1)}, bf16[2,2,128,256]{3,2,1,0:T(8,128)(2,1)S(1)}, u32[]{:S(2)}, u32[]{:S(2)}) %collective-permute-start.3) | collective-permute-done | bytes 262176 | tf_op jit(solution)/shard_map/ppermute | solution.py:705
  21.4 0.0 copy-done.3
  21.4 0.0 copy-done.4
  21.4 0.0 copy-done.5
  21.4 0.4 frames.1
  21.8 7.6 %collective-permute-start.5 = (bf16[2,2,144,256]{3,2,1,0:T(8,128)(2,1)S(1)}, bf16[2,2,144,256]{3,2,1,0:T(8,128)(2,1)S(1)}, u32[]{:S(2)}, u32[]{:S(2)}) collective-permute-start(bf16[2,2,144,256]{3,2,1,0:T(8,128)(2,1)S(1)} %get-tuple-element.16), channel_id=1, source_target_pairs={{0,1},{1,2},{2,3},{3,4},{4,5},{5,6},{6,7},{7,8},{8,9},{9,10},{10,1... | collective-permute-start | bytes 884744 | tf_op jit(solution)/shard_map/ppermute | solution.py:705
  29.4 1.3 %collective-permute-start.4 = (bf16[2,2,128,256]{3,2,1,0:T(8,128)(2,1)S(1)}, bf16[2,2,128,256]{3,2,1,0:T(8,128)(2,1)S(1)}, u32[]{:S(2)}, u32[]{:S(2)}) collective-permute-start(bf16[2,2,128,256]{3,2,1,0:T(8,128)(2,1)S(1)} %get-tuple-element.14), channel_id=1, source_target_pairs={{1,0},{2,1},{3,2},{4,3},{5,4},{6,5},{7,6},{8,7},{9,8},{10,9},{11,1... | collective-permute-start | bytes 786440 | tf_op jit(solution)/shard_map/ppermute | solution.py:705
  30.7 2.1 %collective-permute-done.4.refs_8_ = bf16[2,2,128,256]{3,2,1,0:T(8,128)(2,1)S(1)} collective-permute-done((bf16[2,2,128,256]{3,2,1,0:T(8,128)(2,1)S(1)}, bf16[2,2,128,256]{3,2,1,0:T(8,128)(2,1)S(1)}, u32[]{:S(2)}, u32[]{:S(2)}) %collective-permute-start.4) | collective-permute-done | bytes 262176 | tf_op jit(solution)/shard_map/ppermute | solution.py:705
  32.8 0.0 collective-permute-done.5.refs_10_
  32.8 0.0 copy-done.2
  32.8 0.0 copy-done.6
  32.8 0.0 copy-done.7
  32.8 0.0 copy-start.14
  32.9 0.0 copy-start.13
  32.9 0.0 copy-start.12
  32.9 0.0 copy-start.10
  32.9 0.0 copy-start.11
  32.9 0.0 copy-start.8
  32.9 0.0 copy-start.9
  32.9 11.1 %update.1 = (f32[2,2,128,2048]{3,2,1,0:T(8,128)}, f32[2,128,2048]{2,1,0:T(8,128)S(1)}, f32[2,8,2048]{2,1,0:T(8,128)S(1)}, f32[2,8,2048]{2,1,0:T(8,128)S(1)}, f32[2,2,2048]{2,1,0:T(2,128)S(1)}) custom-call(s32[2,4]{1,0:T(2,128)S(1)} %concatenate.3.tab.refs_0_, s32[2,4]{1,0:T(2,128)S(1)} %collective-permute-done.tab.refs_1_, ...), custom_call_target="tpu_custom_call" | custom-call | bytes 42000000 | tf_op jit(solution)/shard_map/update/pallas_call | solution.py:570
  44.0 5.4 %collective-permute-start.6 = (f32[2,2,2048]{2,1,0:T(2,128)S(1)}, f32[2,2,2048]{2,1,0:T(2,128)S(1)}, u32[]{:S(2)}, u32[]{:S(2)}) collective-permute-start(f32[2,2,2048]{2,1,0:T(2,128)S(1)} %get-tuple-element.21), channel_id=1, source_target_pairs={{0,1},{1,0},{2,3},{3,2},{4,5},{5,4},{6,7},{7,6},{8,9},{9,8},{10,11... | collective-permute-start | bytes 98312 | tf_op jit(solution)/shard_map/ppermute | solution.py:717
  49.4 0.9 %collective-permute-done.6 = f32[2,2,2048]{2,1,0:T(2,128)S(1)} collective-permute-done((f32[2,2,2048]{2,1,0:T(2,128)S(1)}, f32[2,2,2048]{2,1,0:T(2,128)S(1)}, u32[]{:S(2)}, u32[]{:S(2)}) %collective-permute-start.6) | collective-permute-done | bytes 32800 | tf_op jit(solution)/shard_map/ppermute | solution.py:717
  50.3 0.0 copy-done.14
  50.3 2.8 %collective-permute-start.7 = (f32[2,2,2048]{2,1,0:T(2,128)S(1)}, f32[2,2,2048]{2,1,0:T(2,128)S(1)}, u32[]{:S(2)}, u32[]{:S(2)}) collective-permute-start(f32[2,2,2048]{2,1,0:T(2,128)S(1)} %pad_maximum_fusion), channel_id=1, source_target_pairs={{0,2},{1,3},{2,0},{3,1},{4,6},{5,7},{6,4},{7,5},{8,10},{9,11},{10,... | collective-permute-start | bytes 98312 | tf_op jit(solution)/shard_map/ppermute | solution.py:717
  53.1 1.9 %collective-permute-done.7 = f32[2,2,2048]{2,1,0:T(2,128)S(1)} collective-permute-done((f32[2,2,2048]{2,1,0:T(2,128)S(1)}, f32[2,2,2048]{2,1,0:T(2,128)S(1)}, u32[]{:S(2)}, u32[]{:S(2)}) %collective-permute-start.7) | collective-permute-done | bytes 32800 | tf_op jit(solution)/shard_map/ppermute | solution.py:717
  55.0 0.0 copy-done.13
  55.0 1.8 %collective-permute-start.8 = (f32[2,2,2048]{2,1,0:T(2,128)S(1)}, f32[2,2,2048]{2,1,0:T(2,128)S(1)}, u32[]{:S(2)}, u32[]{:S(2)}) collective-permute-start(f32[2,2,2048]{2,1,0:T(2,128)S(1)} %pad_maximum_fusion.1), channel_id=1, source_target_pairs={{0,4},{1,5},{2,6},{3,7},{4,0},{5,1},{6,2},{7,3},{8,12},{9,13},{10,... | collective-permute-start | bytes 98312 | tf_op jit(solution)/shard_map/ppermute | solution.py:717
  56.9 2.2 %collective-permute-done.8 = f32[2,2,2048]{2,1,0:T(2,128)S(1)} collective-permute-done((f32[2,2,2048]{2,1,0:T(2,128)S(1)}, f32[2,2,2048]{2,1,0:T(2,128)S(1)}, u32[]{:S(2)}, u32[]{:S(2)}) %collective-permute-start.8) | collective-permute-done | bytes 32800 | tf_op jit(solution)/shard_map/ppermute | solution.py:717
  59.0 0.0 copy-done.12
  59.1 4.3 %collective-permute-start.9 = (f32[2,2,2048]{2,1,0:T(2,128)S(1)}, f32[2,2,2048]{2,1,0:T(2,128)S(1)}, u32[]{:S(2)}, u32[]{:S(2)}) collective-permute-start(f32[2,2,2048]{2,1,0:T(2,128)S(1)} %pad_maximum_fusion.2), channel_id=1, source_target_pairs={{0,8},{1,9},{2,10},{3,11},{4,12},{5,13},{6,14},{7,15},{8,0},{9,1},... | collective-permute-start | bytes 98312 | tf_op jit(solution)/shard_map/ppermute | solution.py:717
  63.4 1.2 %constant_dynamic-slice_fusion.7 = (f32[1,2048]{1,0:T(1,128)S(1)}, f32[1,2048]{1,0:T(1,128)S(1)}, f32[1,2048]{1,0:T(1,128)S(1)}, f32[1,2048]{1,0:T(1,128)S(1)}, ...) fusion(f32[17,2048]{1,0:T(8,128)} %constant.58.clone, ...), kind=kLoop, calls=%fused_computation.21 | loop fusion | bytes 131104 | tf_op jit(solution)/shard_map/dynamic_slice | solution.py:714
  64.6 0.9 %collective-permute-done.9 = f32[2,2,2048]{2,1,0:T(2,128)S(1)} collective-permute-done((f32[2,2,2048]{2,1,0:T(2,128)S(1)}, f32[2,2,2048]{2,1,0:T(2,128)S(1)}, u32[]{:S(2)}, u32[]{:S(2)}) %collective-permute-start.9) | collective-permute-done | bytes 32800 | tf_op jit(solution)/shard_map/ppermute | solution.py:717
  65.5 0.0 copy-done.10
  65.5 0.0 copy-done.11
  65.5 0.1 multiply_add_fusion
  65.6 0.1 multiply_add_fusion.1
  65.7 0.0 copy-done.8
  65.7 0.0 copy-done.9
  65.7 6.7 %phase.1 = f32[2,128,2048]{2,1,0:T(8,128)} custom-call(f32[2,128,2048]{2,1,0:T(8,128)S(1)} %get-tuple-element.18.inner, f32[2,8,2048]{2,1,0:T(8,128)S(1)} %get-tuple-element.19.carry_y, f32[2,8,2048]{2,1,0:T(8,128)S(1)} %get-tuple-element.20.carry_z, f32[2,2,2048]{2,1,0:T(2,128)S(1)} %pad_maximum_fusion.3.enter, f32[7,2048]{1,0:T(8,128)S(1)} %copy-done.7, ...), custom_call_target="tpu_custom_call" | custom-call | bytes 21000000 | tf_op jit(solution)/shard_map/phase/pallas_call | solution.py:683
  (8 shorter events, 0.2 us)
Async XLA Ops:
  2.0 8.2 %collective-permute-start = (s32[2,4]{1,0:T(2,128)S(1)}, s32[2,4]{1,0:T(2,128)S(1)}, u32[]{:S(2)}, u32[]{:S(2)}) collective-permute-start(s32[2,4]{1,0:T(2,128)S(1)} %concatenate.3.tab.refs_0_), channel_id=1, source_target_pairs={{0,2},{1,3},{2,4},{3,5},{4,6},{5,7},{6,8},{7,9},{8,10},{9,11},{10,... | collective-permute-start | bytes 104 | tf_op jit(solution)/shard_map/ppermute | solution.py:705
  6.8 2.2 %copy-start = (f32[2,2,128,2048]{3,2,1,0:T(8,128)S(1)}, f32[2,2,128,2048]{3,2,1,0:T(8,128)}, u32[]{:S(2)}) copy-start(f32[2,2,128,2048]{3,2,1,0:T(8,128)} %refs_2_.1) | copy-start | bytes 12582916
  9.0 2.2 %copy-start.1 = (f32[2,2,128,2048]{3,2,1,0:T(8,128)S(1)}, f32[2,2,128,2048]{3,2,1,0:T(8,128)}, u32[]{:S(2)}) copy-start(f32[2,2,128,2048]{3,2,1,0:T(8,128)} %refs_2_.1) | copy-start | bytes 12582916
  9.0 5.1 %copy-start.15 = (bf16[2,256,256]{2,1,0:T(8,128)(2,1)S(1)}, bf16[2,256,256]{2,1,0:T(8,128)(2,1)}, u32[]{:S(2)}) copy-start(bf16[2,256,256]{2,1,0:T(8,128)(2,1)} %param.17) | copy-start | bytes 786436
  10.1 11.3 %copy-start.3 = (f32[2,256,256]{2,1,0:T(8,128)S(1)}, f32[2,256,256]{2,1,0:T(8,128)}, u32[]{:S(2)}) copy-start(f32[2,256,256]{2,1,0:T(8,128)} %probe.1) | copy-start | bytes 1572868
  10.1 11.3 %copy-start.4 = (bf16[512,512]{1,0:T(8,128)(2,1)S(1)}, bf16[512,512]{1,0:T(8,128)(2,1)}, u32[]{:S(2)}) copy-start(bf16[512,512]{1,0:T(8,128)(2,1)} %constant.61.clone.right) | copy-start | bytes 1572868
  10.1 11.3 %copy-start.5 = (bf16[512,512]{1,0:T(8,128)(2,1)S(1)}, bf16[512,512]{1,0:T(8,128)(2,1)}, u32[]{:S(2)}) copy-start(bf16[512,512]{1,0:T(8,128)(2,1)} %constant.60.clone.left) | copy-start | bytes 1572868
  11.2 21.6 %copy-start.2 = (bf16[2,2,1024,1024]{3,2,1,0:T(8,128)(2,1)S(1)}, bf16[2,2,1024,1024]{3,2,1,0:T(8,128)(2,1)}, u32[]{:S(2)}) copy-start(bf16[2,2,1024,1024]{3,2,1,0:T(8,128)(2,1)} %constant.52.clone.refs_7_) | copy-start | bytes 25165828
  12.2 20.6 %copy-start.6 = (f32[8,2048]{1,0:T(8,128)S(1)}, f32[8,2048]{1,0:T(8,128)}, u32[]{:S(2)}) copy-start(f32[8,2048]{1,0:T(8,128)} %constant.56.clone.refs_6_.segs) | copy-start | bytes 196612
  12.2 20.6 %copy-start.7 = (f32[7,2048]{1,0:T(8,128)S(1)}, f32[7,2048]{1,0:T(8,128)}, u32[]{:S(2)}) copy-start(f32[7,2048]{1,0:T(8,128)} %constant.54.clone.refs_5_.scan) | copy-start | bytes 172036
  12.2 7.1 %collective-permute-start.1 = (bf16[624,256]{1,0:T(8,128)(2,1)S(1)}, bf16[624,256]{1,0:T(8,128)(2,1)S(1)}, u32[]{:S(2)}, u32[]{:S(2)}) collective-permute-start(bf16[624,256]{1,0:T(8,128)(2,1)S(1)} %get-tuple-element.12), channel_id=1, source_target_pairs={{0,1},{1,2},{2,3},{3,4},{4,5},{5,6},{6,7},{7,8},{8,9},{9,10},{10,1... | collective-permute-start | bytes 958472 | tf_op jit(solution)/shard_map/ppermute | solution.py:705
  14.1 5.8 %collective-permute-start.2 = (bf16[2,256,256]{2,1,0:T(8,128)(2,1)S(1)}, bf16[2,256,256]{2,1,0:T(8,128)(2,1)S(1)}, u32[]{:S(2)}, u32[]{:S(2)}) collective-permute-start(bf16[2,256,256]{2,1,0:T(8,128)(2,1)S(1)} %copy-done.15), channel_id=1, source_target_pairs={{0,1},{1,2},{2,3},{3,4},{4,5},{5,6},{6,7},{7,8},{8,9},{9,10},{10,1... | collective-permute-start | bytes 786440 | tf_op jit(solution)/shard_map/ppermute | solution.py:705
  18.0 3.4 %collective-permute-start.3 = (bf16[2,2,128,256]{3,2,1,0:T(8,128)(2,1)S(1)}, bf16[2,2,128,256]{3,2,1,0:T(8,128)(2,1)S(1)}, u32[]{:S(2)}, u32[]{:S(2)}) collective-permute-start(bf16[2,2,128,256]{3,2,1,0:T(8,128)(2,1)S(1)} %get-tuple-element.13), channel_id=1, source_target_pairs={{1,0},{2,1},{3,2},{4,3},{5,4},{6,5},{7,6},{8,7},{9,8},{10,9},{11,1... | collective-permute-start | bytes 786440 | tf_op jit(solution)/shard_map/ppermute | solution.py:705
  21.8 11.1 %collective-permute-start.5 = (bf16[2,2,144,256]{3,2,1,0:T(8,128)(2,1)S(1)}, bf16[2,2,144,256]{3,2,1,0:T(8,128)(2,1)S(1)}, u32[]{:S(2)}, u32[]{:S(2)}) collective-permute-start(bf16[2,2,144,256]{3,2,1,0:T(8,128)(2,1)S(1)} %get-tuple-element.16), channel_id=1, source_target_pairs={{0,1},{1,2},{2,3},{3,4},{4,5},{5,6},{6,7},{7,8},{8,9},{9,10},{10,1... | collective-permute-start | bytes 884744 | tf_op jit(solution)/shard_map/ppermute | solution.py:705
  29.4 3.4 %collective-permute-start.4 = (bf16[2,2,128,256]{3,2,1,0:T(8,128)(2,1)S(1)}, bf16[2,2,128,256]{3,2,1,0:T(8,128)(2,1)S(1)}, u32[]{:S(2)}, u32[]{:S(2)}) collective-permute-start(bf16[2,2,128,256]{3,2,1,0:T(8,128)(2,1)S(1)} %get-tuple-element.14), channel_id=1, source_target_pairs={{1,0},{2,1},{3,2},{4,3},{5,4},{6,5},{7,6},{8,7},{9,8},{10,9},{11,1... | collective-permute-start | bytes 786440 | tf_op jit(solution)/shard_map/ppermute | solution.py:705
  32.8 17.4 %copy-start.14 = (f32[2048]{0:T(1024)S(1)}, f32[2048]{0:T(1024)}, u32[]{:S(2)}) copy-start(f32[2048]{0:T(1024)} %constant.70) | copy-start | bytes 24580
  32.9 22.1 %copy-start.13 = (f32[2048]{0:T(1024)S(1)}, f32[2048]{0:T(1024)}, u32[]{:S(2)}) copy-start(f32[2048]{0:T(1024)} %constant.72) | copy-start | bytes 24580
  32.9 26.2 %copy-start.12 = (f32[2048]{0:T(1024)S(1)}, f32[2048]{0:T(1024)}, u32[]{:S(2)}) copy-start(f32[2048]{0:T(1024)} %constant.74) | copy-start | bytes 24580
  32.9 32.6 %copy-start.10 = (f32[2048]{0:T(1024)S(1)}, f32[2048]{0:T(1024)}, u32[]{:S(2)}) copy-start(f32[2048]{0:T(1024)} %constant.78) | copy-start | bytes 24580
  32.9 32.6 %copy-start.11 = (f32[2048]{0:T(1024)S(1)}, f32[2048]{0:T(1024)}, u32[]{:S(2)}) copy-start(f32[2048]{0:T(1024)} %constant.76) | copy-start | bytes 24580
  32.9 32.8 %copy-start.8 = (f32[16,2048]{1,0:T(8,128)S(1)}, f32[16,2048]{1,0:T(8,128)}, u32[]{:S(2)}) copy-start(f32[16,2048]{1,0:T(8,128)} %constant.55.clone.powers) | copy-start | bytes 393220
  32.9 32.8 %copy-start.9 = (f32[8,2048]{1,0:T(8,128)S(1)}, f32[8,2048]{1,0:T(8,128)}, u32[]{:S(2)}) copy-start(f32[8,2048]{1,0:T(8,128)} %constant.57.clone.segs_back) | copy-start | bytes 196612
  44.0 6.3 %collective-permute-start.6 = (f32[2,2,2048]{2,1,0:T(2,128)S(1)}, f32[2,2,2048]{2,1,0:T(2,128)S(1)}, u32[]{:S(2)}, u32[]{:S(2)}) collective-permute-start(f32[2,2,2048]{2,1,0:T(2,128)S(1)} %get-tuple-element.21), channel_id=1, source_target_pairs={{0,1},{1,0},{2,3},{3,2},{4,5},{5,4},{6,7},{7,6},{8,9},{9,8},{10,11... | collective-permute-start | bytes 98312 | tf_op jit(solution)/shard_map/ppermute | solution.py:717
  50.3 4.7 %collective-permute-start.7 = (f32[2,2,2048]{2,1,0:T(2,128)S(1)}, f32[2,2,2048]{2,1,0:T(2,128)S(1)}, u32[]{:S(2)}, u32[]{:S(2)}) collective-permute-start(f32[2,2,2048]{2,1,0:T(2,128)S(1)} %pad_maximum_fusion), channel_id=1, source_target_pairs={{0,2},{1,3},{2,0},{3,1},{4,6},{5,7},{6,4},{7,5},{8,10},{9,11},{10,... | collective-permute-start | bytes 98312 | tf_op jit(solution)/shard_map/ppermute | solution.py:717
  55.0 4.0 %collective-permute-start.8 = (f32[2,2,2048]{2,1,0:T(2,128)S(1)}, f32[2,2,2048]{2,1,0:T(2,128)S(1)}, u32[]{:S(2)}, u32[]{:S(2)}) collective-permute-start(f32[2,2,2048]{2,1,0:T(2,128)S(1)} %pad_maximum_fusion.1), channel_id=1, source_target_pairs={{0,4},{1,5},{2,6},{3,7},{4,0},{5,1},{6,2},{7,3},{8,12},{9,13},{10,... | collective-permute-start | bytes 98312 | tf_op jit(solution)/shard_map/ppermute | solution.py:717
  59.1 6.4 %collective-permute-start.9 = (f32[2,2,2048]{2,1,0:T(2,128)S(1)}, f32[2,2,2048]{2,1,0:T(2,128)S(1)}, u32[]{:S(2)}, u32[]{:S(2)}) collective-permute-start(f32[2,2,2048]{2,1,0:T(2,128)S(1)} %pad_maximum_fusion.2), channel_id=1, source_target_pairs={{0,8},{1,9},{2,10},{3,11},{4,12},{5,13},{6,14},{7,15},{8,0},{9,1},... | collective-permute-start | bytes 98312 | tf_op jit(solution)/shard_map/ppermute | solution.py:717

commit v5 on v4

--- a/solution.py
+++ b/solution.py
@@ -478,7 +478,7 @@
                     source[a, b, rows[i]] = values[i]
             return 0
 
-        lax.fori_loop(0, blocks, columns, 0, unroll=2)
+        lax.fori_loop(0, blocks, columns, 0, unroll=4)
 
     def fold(b, _):
         lanes = pl.ds(pl.multiple_of(b * LANES, LANES), LANES)
@@ -511,7 +511,7 @@
             rows_in[h, count + at : count + at + 2 * PAD, lanes] = low
         return 0
 
-    lax.fori_loop(0, half_blocks, fold, 0, unroll=2)
+    lax.fori_loop(0, half_blocks, fold, 0, unroll=4)
 
     wide = min(2 * LANES, half)
     sub = lax.broadcasted_iota(jnp.int32, (SEG, wide), 0)
@@ -635,7 +635,7 @@
                 )
         return 0
 
-    lax.fori_loop(0, 2 * half_blocks, solve, 0, unroll=2)
+    lax.fori_loop(0, 2 * half_blocks, solve, 0, unroll=4)
 
     def split(b, _):
         lanes = pl.ds(pl.multiple_of(b * LANES, LANES), LANES)

time: 72.6 us -> 71.5 us (0.985)
  no operation moved by 1% of the time
where the time goes in v5:
time: 71.5 us; the launch traced here: 71.3 us
  starting transfers between devices  34.7 us (49%)
  Pallas kernels  20.1 us (28%)
  waiting for transfers between devices  9.22 us (13%)
  local copies, waits for them, and re-layouts  5.25 us (7%)
  between operations  1.77 us (2%)
    ppermute x6, starting transfers between devices, passed_along(): return lax.ppermute(x, 'tile', pairs)  20.8 us
    ppermute x4, starting transfers between devices, entering_values(): lax.ppermute(jnp.stack([head, tail]), 'tile', [(i, i ^ width) for i in ra...  13.9 us
    pallas_call x1, Pallas kernels, run_update(): pl.pallas_call(functools.partial(update_kernel, reach, center), out_shape...  10.4 us
    pallas_call x1, Pallas kernels, run_phase(): pl.pallas_call(phase_kernel, out_shape=jax.ShapeDtypeStruct((angles, stri...  6.72 us
    ppermute x4, waiting for transfers between devices, entering_values(): lax.ppermute(jnp.stack([head, tail]), 'tile', [(i, i ^ width) for i in ra...  5.62 us
    ppermute x6, waiting for transfers between devices, passed_along(): return lax.ppermute(x, 'tile', pairs)  3.6 us
    unnamed x32, local copies, waits for them, and re-layouts  3.34 us
    pallas_call x2, Pallas kernels, extract(): pl.pallas_call(functools.partial(extract_kernel, coded), out_shape=[windo...  1.58 us
  transfers between devices with their start and end apart: 10, of which 6 were waited for; matrix products, arithmetic and copies ran while one was open for 2% of the time, Pallas kernels for 2%

profile of v5, /device:TPU:0, one launch (start us, length us, event | category | flops | bytes accessed | tf_op | source)
XLA Modules:
  0.0 71.3 jit_solution(457666593702947268)
XLA Ops:
  1.3 0.7 concatenate.3.tab.refs_0_
  2.0 4.9 %collective-permute-start = (s32[2,4]{1,0:T(2,128)S(1)}, s32[2,4]{1,0:T(2,128)S(1)}, u32[]{:S(2)}, u32[]{:S(2)}) collective-permute-start(s32[2,4]{1,0:T(2,128)S(1)} %concatenate.3.tab.refs_0_), channel_id=1, source_target_pairs={{0,2},{1,3},{2,4},{3,5},{4,6},{5,7},{6,8},{7,9},{8,10},{9,11},{10,... | collective-permute-start | bytes 104 | tf_op jit(solution)/shard_map/ppermute | solution.py:705
  6.8 0.0 copy-start
  6.8 2.2 %copy-done = f32[2,2,128,2048]{3,2,1,0:T(8,128)S(1)} copy-done((f32[2,2,128,2048]{3,2,1,0:T(8,128)S(1)}, f32[2,2,128,2048]{3,2,1,0:T(8,128)}, u32[]{:S(2)}) %copy-start) | copy-done | bytes 4194328
  9.0 0.0 copy-start.1
  9.0 0.0 copy-start.15
  9.0 1.1 %pack.1.rest_0_ = bf16[624,256]{1,0:T(8,128)(2,1)S(1)} custom-call(s32[2,4]{1,0:T(2,128)S(1)} %concatenate.3.tab.refs_0_, f32[2,2,128,2048]{3,2,1,0:T(8,128)S(1)} %copy-done), custom_call_target="tpu_custom_call" | custom-call | bytes 18000000 | tf_op jit(solution)/shard_map/pack/pallas_call | solution.py:179
  10.1 0.0 copy-start.3
  10.1 0.0 copy-start.4
  10.1 0.0 copy-start.5
  10.1 0.0 collective-permute-done.tab.refs_1_
  10.1 1.1 %copy-done.1 = f32[2,2,128,2048]{3,2,1,0:T(8,128)S(1)} copy-done((f32[2,2,128,2048]{3,2,1,0:T(8,128)S(1)}, f32[2,2,128,2048]{3,2,1,0:T(8,128)}, u32[]{:S(2)}) %copy-start.1) | copy-done | bytes 4194328
  11.2 0.0 copy-start.2
  11.2 1.0 %extract.2 = (bf16[2,2,128,256]{3,2,1,0:T(8,128)(2,1)S(1)}, bf16[624,256]{1,0:T(8,128)(2,1)S(1)}) custom-call(s32[2,4]{1,0:T(2,128)S(1)} %collective-permute-done.tab.refs_1_, f32[2,2,128,2048]{3,2,1,0:T(8,128)S(1)} %copy-done.1, bf16[624,256]{1,0:T(8,128)(2,1)S(1)} %pack.1.rest_0_), custom_call_target="tpu_custom_call", output_to_operand_aliasing={{1}: (2, {})} | custom-call | bytes 6000000 | tf_op jit(solution)/shard_map/extract/pallas_call | solution.py:212
  12.2 0.0 copy-start.6
  12.2 0.0 copy-start.7
  12.2 1.9 %collective-permute-start.1 = (bf16[624,256]{1,0:T(8,128)(2,1)S(1)}, bf16[624,256]{1,0:T(8,128)(2,1)S(1)}, u32[]{:S(2)}, u32[]{:S(2)}) collective-permute-start(bf16[624,256]{1,0:T(8,128)(2,1)S(1)} %get-tuple-element.12), channel_id=1, source_target_pairs={{0,1},{1,2},{2,3},{3,4},{4,5},{5,6},{6,7},{7,8},{8,9},{9,10},{10,1... | collective-permute-start | bytes 958472 | tf_op jit(solution)/shard_map/ppermute | solution.py:705
  14.1 0.0 copy-done.15
  14.1 3.9 %collective-permute-start.2 = (bf16[2,256,256]{2,1,0:T(8,128)(2,1)S(1)}, bf16[2,256,256]{2,1,0:T(8,128)(2,1)S(1)}, u32[]{:S(2)}, u32[]{:S(2)}) collective-permute-start(bf16[2,256,256]{2,1,0:T(8,128)(2,1)S(1)} %copy-done.15), channel_id=1, source_target_pairs={{0,1},{1,2},{2,3},{3,4},{4,5},{5,6},{6,7},{7,8},{8,9},{9,10},{10,1... | collective-permute-start | bytes 786440 | tf_op jit(solution)/shard_map/ppermute | solution.py:705
  18.0 1.3 %collective-permute-start.3 = (bf16[2,2,128,256]{3,2,1,0:T(8,128)(2,1)S(1)}, bf16[2,2,128,256]{3,2,1,0:T(8,128)(2,1)S(1)}, u32[]{:S(2)}, u32[]{:S(2)}) collective-permute-start(bf16[2,2,128,256]{3,2,1,0:T(8,128)(2,1)S(1)} %get-tuple-element.13), channel_id=1, source_target_pairs={{1,0},{2,1},{3,2},{4,3},{5,4},{6,5},{7,6},{8,7},{9,8},{10,9},{11,1... | collective-permute-start | bytes 786440 | tf_op jit(solution)/shard_map/ppermute | solution.py:705
  19.3 0.0 collective-permute-done.1.tab.package.refs_3_
  19.3 0.6 extract.3.rest_0_
  19.9 0.0 collective-permute-done.2.measured
  19.9 1.5 %collective-permute-done.3.rest_1_ = bf16[2,2,128,256]{3,2,1,0:T(8,128)(2,1)S(1)} collective-permute-done((bf16[2,2,128,256]{3,2,1,0:T(8,128)(2,1)S(1)}, bf16[2,2,128,256]{3,2,1,0:T(8,128)(2,1)S(1)}, u32[]{:S(2)}, u32[]{:S(2)}) %collective-permute-start.3) | collective-permute-done | bytes 262176 | tf_op jit(solution)/shard_map/ppermute | solution.py:705
  21.4 0.0 copy-done.3
  21.4 0.0 copy-done.4
  21.4 0.0 copy-done.5
  21.4 0.4 frames.1
  21.8 7.6 %collective-permute-start.5 = (bf16[2,2,144,256]{3,2,1,0:T(8,128)(2,1)S(1)}, bf16[2,2,144,256]{3,2,1,0:T(8,128)(2,1)S(1)}, u32[]{:S(2)}, u32[]{:S(2)}) collective-permute-start(bf16[2,2,144,256]{3,2,1,0:T(8,128)(2,1)S(1)} %get-tuple-element.16), channel_id=1, source_target_pairs={{0,1},{1,2},{2,3},{3,4},{4,5},{5,6},{6,7},{7,8},{8,9},{9,10},{10,1... | collective-permute-start | bytes 884744 | tf_op jit(solution)/shard_map/ppermute | solution.py:705
  29.4 1.3 %collective-permute-start.4 = (bf16[2,2,128,256]{3,2,1,0:T(8,128)(2,1)S(1)}, bf16[2,2,128,256]{3,2,1,0:T(8,128)(2,1)S(1)}, u32[]{:S(2)}, u32[]{:S(2)}) collective-permute-start(bf16[2,2,128,256]{3,2,1,0:T(8,128)(2,1)S(1)} %get-tuple-element.14), channel_id=1, source_target_pairs={{1,0},{2,1},{3,2},{4,3},{5,4},{6,5},{7,6},{8,7},{9,8},{10,9},{11,1... | collective-permute-start | bytes 786440 | tf_op jit(solution)/shard_map/ppermute | solution.py:705
  30.7 2.1 %collective-permute-done.4.refs_8_ = bf16[2,2,128,256]{3,2,1,0:T(8,128)(2,1)S(1)} collective-permute-done((bf16[2,2,128,256]{3,2,1,0:T(8,128)(2,1)S(1)}, bf16[2,2,128,256]{3,2,1,0:T(8,128)(2,1)S(1)}, u32[]{:S(2)}, u32[]{:S(2)}) %collective-permute-start.4) | collective-permute-done | bytes 262176 | tf_op jit(solution)/shard_map/ppermute | solution.py:705
  32.8 0.0 collective-permute-done.5.refs_10_
  32.8 0.0 copy-done.2
  32.8 0.0 copy-done.6
  32.8 0.0 copy-done.7
  32.8 0.0 copy-start.14
  32.9 0.0 copy-start.13
  32.9 0.0 copy-start.12
  32.9 0.0 copy-start.10
  32.9 0.0 copy-start.11
  32.9 0.0 copy-start.8
  32.9 0.0 copy-start.9
  32.9 10.4 %update.1 = (f32[2,2,128,2048]{3,2,1,0:T(8,128)}, f32[2,128,2048]{2,1,0:T(8,128)S(1)}, f32[2,8,2048]{2,1,0:T(8,128)S(1)}, f32[2,8,2048]{2,1,0:T(8,128)S(1)}, f32[2,2,2048]{2,1,0:T(2,128)S(1)}) custom-call(s32[2,4]{1,0:T(2,128)S(1)} %concatenate.3.tab.refs_0_, s32[2,4]{1,0:T(2,128)S(1)} %collective-permute-done.tab.refs_1_, ...), custom_call_target="tpu_custom_call" | custom-call | bytes 42000000 | tf_op jit(solution)/shard_map/update/pallas_call | solution.py:570
  43.3 5.4 %collective-permute-start.6 = (f32[2,2,2048]{2,1,0:T(2,128)S(1)}, f32[2,2,2048]{2,1,0:T(2,128)S(1)}, u32[]{:S(2)}, u32[]{:S(2)}) collective-permute-start(f32[2,2,2048]{2,1,0:T(2,128)S(1)} %get-tuple-element.21), channel_id=1, source_target_pairs={{0,1},{1,0},{2,3},{3,2},{4,5},{5,4},{6,7},{7,6},{8,9},{9,8},{10,11... | collective-permute-start | bytes 98312 | tf_op jit(solution)/shard_map/ppermute | solution.py:717
  48.8 0.9 %collective-permute-done.6 = f32[2,2,2048]{2,1,0:T(2,128)S(1)} collective-permute-done((f32[2,2,2048]{2,1,0:T(2,128)S(1)}, f32[2,2,2048]{2,1,0:T(2,128)S(1)}, u32[]{:S(2)}, u32[]{:S(2)}) %collective-permute-start.6) | collective-permute-done | bytes 32800 | tf_op jit(solution)/shard_map/ppermute | solution.py:717
  49.6 0.0 copy-done.14
  49.7 2.8 %collective-permute-start.7 = (f32[2,2,2048]{2,1,0:T(2,128)S(1)}, f32[2,2,2048]{2,1,0:T(2,128)S(1)}, u32[]{:S(2)}, u32[]{:S(2)}) collective-permute-start(f32[2,2,2048]{2,1,0:T(2,128)S(1)} %pad_maximum_fusion), channel_id=1, source_target_pairs={{0,2},{1,3},{2,0},{3,1},{4,6},{5,7},{6,4},{7,5},{8,10},{9,11},{10,... | collective-permute-start | bytes 98312 | tf_op jit(solution)/shard_map/ppermute | solution.py:717
  52.5 1.9 %collective-permute-done.7 = f32[2,2,2048]{2,1,0:T(2,128)S(1)} collective-permute-done((f32[2,2,2048]{2,1,0:T(2,128)S(1)}, f32[2,2,2048]{2,1,0:T(2,128)S(1)}, u32[]{:S(2)}, u32[]{:S(2)}) %collective-permute-start.7) | collective-permute-done | bytes 32800 | tf_op jit(solution)/shard_map/ppermute | solution.py:717
  54.4 0.0 copy-done.13
  54.4 1.8 %collective-permute-start.8 = (f32[2,2,2048]{2,1,0:T(2,128)S(1)}, f32[2,2,2048]{2,1,0:T(2,128)S(1)}, u32[]{:S(2)}, u32[]{:S(2)}) collective-permute-start(f32[2,2,2048]{2,1,0:T(2,128)S(1)} %pad_maximum_fusion.1), channel_id=1, source_target_pairs={{0,4},{1,5},{2,6},{3,7},{4,0},{5,1},{6,2},{7,3},{8,12},{9,13},{10,... | collective-permute-start | bytes 98312 | tf_op jit(solution)/shard_map/ppermute | solution.py:717
  56.2 2.2 %collective-permute-done.8 = f32[2,2,2048]{2,1,0:T(2,128)S(1)} collective-permute-done((f32[2,2,2048]{2,1,0:T(2,128)S(1)}, f32[2,2,2048]{2,1,0:T(2,128)S(1)}, u32[]{:S(2)}, u32[]{:S(2)}) %collective-permute-start.8) | collective-permute-done | bytes 32800 | tf_op jit(solution)/shard_map/ppermute | solution.py:717
  58.4 0.0 copy-done.12
  58.5 3.9 %collective-permute-start.9 = (f32[2,2,2048]{2,1,0:T(2,128)S(1)}, f32[2,2,2048]{2,1,0:T(2,128)S(1)}, u32[]{:S(2)}, u32[]{:S(2)}) collective-permute-start(f32[2,2,2048]{2,1,0:T(2,128)S(1)} %pad_maximum_fusion.2), channel_id=1, source_target_pairs={{0,8},{1,9},{2,10},{3,11},{4,12},{5,13},{6,14},{7,15},{8,0},{9,1},... | collective-permute-start | bytes 98312 | tf_op jit(solution)/shard_map/ppermute | solution.py:717
  62.3 1.2 %constant_dynamic-slice_fusion.7 = (f32[1,2048]{1,0:T(1,128)S(1)}, f32[1,2048]{1,0:T(1,128)S(1)}, f32[1,2048]{1,0:T(1,128)S(1)}, f32[1,2048]{1,0:T(1,128)S(1)}, ...) fusion(f32[17,2048]{1,0:T(8,128)} %constant.58.clone, ...), kind=kLoop, calls=%fused_computation.21 | loop fusion | bytes 131104 | tf_op jit(solution)/shard_map/dynamic_slice | solution.py:714
  63.5 0.7 collective-permute-done.9
  64.2 0.0 copy-done.10
  64.2 0.0 copy-done.11
  64.2 0.1 multiply_add_fusion
  64.3 0.1 multiply_add_fusion.1
  64.4 0.0 copy-done.8
  64.4 0.0 copy-done.9
  64.4 6.7 %phase.1 = f32[2,128,2048]{2,1,0:T(8,128)} custom-call(f32[2,128,2048]{2,1,0:T(8,128)S(1)} %get-tuple-element.18.inner, f32[2,8,2048]{2,1,0:T(8,128)S(1)} %get-tuple-element.19.carry_y, f32[2,8,2048]{2,1,0:T(8,128)S(1)} %get-tuple-element.20.carry_z, f32[2,2,2048]{2,1,0:T(2,128)S(1)} %pad_maximum_fusion.3.enter, f32[7,2048]{1,0:T(8,128)S(1)} %copy-done.7, ...), custom_call_target="tpu_custom_call" | custom-call | bytes 21000000 | tf_op jit(solution)/shard_map/phase/pallas_call | solution.py:683
  (8 shorter events, 0.2 us)
Async XLA Ops:
  2.0 8.2 %collective-permute-start = (s32[2,4]{1,0:T(2,128)S(1)}, s32[2,4]{1,0:T(2,128)S(1)}, u32[]{:S(2)}, u32[]{:S(2)}) collective-permute-start(s32[2,4]{1,0:T(2,128)S(1)} %concatenate.3.tab.refs_0_), channel_id=1, source_target_pairs={{0,2},{1,3},{2,4},{3,5},{4,6},{5,7},{6,8},{7,9},{8,10},{9,11},{10,... | collective-permute-start | bytes 104 | tf_op jit(solution)/shard_map/ppermute | solution.py:705
  6.8 2.2 %copy-start = (f32[2,2,128,2048]{3,2,1,0:T(8,128)S(1)}, f32[2,2,128,2048]{3,2,1,0:T(8,128)}, u32[]{:S(2)}) copy-start(f32[2,2,128,2048]{3,2,1,0:T(8,128)} %refs_2_.1) | copy-start | bytes 12582916
  9.0 2.2 %copy-start.1 = (f32[2,2,128,2048]{3,2,1,0:T(8,128)S(1)}, f32[2,2,128,2048]{3,2,1,0:T(8,128)}, u32[]{:S(2)}) copy-start(f32[2,2,128,2048]{3,2,1,0:T(8,128)} %refs_2_.1) | copy-start | bytes 12582916
  9.0 5.1 %copy-start.15 = (bf16[2,256,256]{2,1,0:T(8,128)(2,1)S(1)}, bf16[2,256,256]{2,1,0:T(8,128)(2,1)}, u32[]{:S(2)}) copy-start(bf16[2,256,256]{2,1,0:T(8,128)(2,1)} %param.17) | copy-start | bytes 786436
  10.1 11.3 %copy-start.3 = (f32[2,256,256]{2,1,0:T(8,128)S(1)}, f32[2,256,256]{2,1,0:T(8,128)}, u32[]{:S(2)}) copy-start(f32[2,256,256]{2,1,0:T(8,128)} %probe.1) | copy-start | bytes 1572868
  10.1 11.3 %copy-start.4 = (bf16[512,512]{1,0:T(8,128)(2,1)S(1)}, bf16[512,512]{1,0:T(8,128)(2,1)}, u32[]{:S(2)}) copy-start(bf16[512,512]{1,0:T(8,128)(2,1)} %constant.61.clone.right) | copy-start | bytes 1572868
  10.1 11.3 %copy-start.5 = (bf16[512,512]{1,0:T(8,128)(2,1)S(1)}, bf16[512,512]{1,0:T(8,128)(2,1)}, u32[]{:S(2)}) copy-start(bf16[512,512]{1,0:T(8,128)(2,1)} %constant.60.clone.left) | copy-start | bytes 1572868
  11.2 21.6 %copy-start.2 = (bf16[2,2,1024,1024]{3,2,1,0:T(8,128)(2,1)S(1)}, bf16[2,2,1024,1024]{3,2,1,0:T(8,128)(2,1)}, u32[]{:S(2)}) copy-start(bf16[2,2,1024,1024]{3,2,1,0:T(8,128)(2,1)} %constant.52.clone.refs_7_) | copy-start | bytes 25165828
  12.2 20.6 %copy-start.6 = (f32[8,2048]{1,0:T(8,128)S(1)}, f32[8,2048]{1,0:T(8,128)}, u32[]{:S(2)}) copy-start(f32[8,2048]{1,0:T(8,128)} %constant.56.clone.refs_6_.segs) | copy-start | bytes 196612
  12.2 20.6 %copy-start.7 = (f32[7,2048]{1,0:T(8,128)S(1)}, f32[7,2048]{1,0:T(8,128)}, u32[]{:S(2)}) copy-start(f32[7,2048]{1,0:T(8,128)} %constant.54.clone.refs_5_.scan) | copy-start | bytes 172036
  12.2 7.1 %collective-permute-start.1 = (bf16[624,256]{1,0:T(8,128)(2,1)S(1)}, bf16[624,256]{1,0:T(8,128)(2,1)S(1)}, u32[]{:S(2)}, u32[]{:S(2)}) collective-permute-start(bf16[624,256]{1,0:T(8,128)(2,1)S(1)} %get-tuple-element.12), channel_id=1, source_target_pairs={{0,1},{1,2},{2,3},{3,4},{4,5},{5,6},{6,7},{7,8},{8,9},{9,10},{10,1... | collective-permute-start | bytes 958472 | tf_op jit(solution)/shard_map/ppermute | solution.py:705
  14.1 5.8 %collective-permute-start.2 = (bf16[2,256,256]{2,1,0:T(8,128)(2,1)S(1)}, bf16[2,256,256]{2,1,0:T(8,128)(2,1)S(1)}, u32[]{:S(2)}, u32[]{:S(2)}) collective-permute-start(bf16[2,256,256]{2,1,0:T(8,128)(2,1)S(1)} %copy-done.15), channel_id=1, source_target_pairs={{0,1},{1,2},{2,3},{3,4},{4,5},{5,6},{6,7},{7,8},{8,9},{9,10},{10,1... | collective-permute-start | bytes 786440 | tf_op jit(solution)/shard_map/ppermute | solution.py:705
  18.0 3.4 %collective-permute-start.3 = (bf16[2,2,128,256]{3,2,1,0:T(8,128)(2,1)S(1)}, bf16[2,2,128,256]{3,2,1,0:T(8,128)(2,1)S(1)}, u32[]{:S(2)}, u32[]{:S(2)}) collective-permute-start(bf16[2,2,128,256]{3,2,1,0:T(8,128)(2,1)S(1)} %get-tuple-element.13), channel_id=1, source_target_pairs={{1,0},{2,1},{3,2},{4,3},{5,4},{6,5},{7,6},{8,7},{9,8},{10,9},{11,1... | collective-permute-start | bytes 786440 | tf_op jit(solution)/shard_map/ppermute | solution.py:705
  21.8 11.1 %collective-permute-start.5 = (bf16[2,2,144,256]{3,2,1,0:T(8,128)(2,1)S(1)}, bf16[2,2,144,256]{3,2,1,0:T(8,128)(2,1)S(1)}, u32[]{:S(2)}, u32[]{:S(2)}) collective-permute-start(bf16[2,2,144,256]{3,2,1,0:T(8,128)(2,1)S(1)} %get-tuple-element.16), channel_id=1, source_target_pairs={{0,1},{1,2},{2,3},{3,4},{4,5},{5,6},{6,7},{7,8},{8,9},{9,10},{10,1... | collective-permute-start | bytes 884744 | tf_op jit(solution)/shard_map/ppermute | solution.py:705
  29.4 3.4 %collective-permute-start.4 = (bf16[2,2,128,256]{3,2,1,0:T(8,128)(2,1)S(1)}, bf16[2,2,128,256]{3,2,1,0:T(8,128)(2,1)S(1)}, u32[]{:S(2)}, u32[]{:S(2)}) collective-permute-start(bf16[2,2,128,256]{3,2,1,0:T(8,128)(2,1)S(1)} %get-tuple-element.14), channel_id=1, source_target_pairs={{1,0},{2,1},{3,2},{4,3},{5,4},{6,5},{7,6},{8,7},{9,8},{10,9},{11,1... | collective-permute-start | bytes 786440 | tf_op jit(solution)/shard_map/ppermute | solution.py:705
  32.8 16.8 %copy-start.14 = (f32[2048]{0:T(1024)S(1)}, f32[2048]{0:T(1024)}, u32[]{:S(2)}) copy-start(f32[2048]{0:T(1024)} %constant.70) | copy-start | bytes 24580
  32.9 21.5 %copy-start.13 = (f32[2048]{0:T(1024)S(1)}, f32[2048]{0:T(1024)}, u32[]{:S(2)}) copy-start(f32[2048]{0:T(1024)} %constant.72) | copy-start | bytes 24580
  32.9 25.5 %copy-start.12 = (f32[2048]{0:T(1024)S(1)}, f32[2048]{0:T(1024)}, u32[]{:S(2)}) copy-start(f32[2048]{0:T(1024)} %constant.74) | copy-start | bytes 24580
  32.9 31.3 %copy-start.10 = (f32[2048]{0:T(1024)S(1)}, f32[2048]{0:T(1024)}, u32[]{:S(2)}) copy-start(f32[2048]{0:T(1024)} %constant.78) | copy-start | bytes 24580
  32.9 31.3 %copy-start.11 = (f32[2048]{0:T(1024)S(1)}, f32[2048]{0:T(1024)}, u32[]{:S(2)}) copy-start(f32[2048]{0:T(1024)} %constant.76) | copy-start | bytes 24580
  32.9 31.5 %copy-start.8 = (f32[16,2048]{1,0:T(8,128)S(1)}, f32[16,2048]{1,0:T(8,128)}, u32[]{:S(2)}) copy-start(f32[16,2048]{1,0:T(8,128)} %constant.55.clone.powers) | copy-start | bytes 393220
  32.9 31.5 %copy-start.9 = (f32[8,2048]{1,0:T(8,128)S(1)}, f32[8,2048]{1,0:T(8,128)}, u32[]{:S(2)}) copy-start(f32[8,2048]{1,0:T(8,128)} %constant.57.clone.segs_back) | copy-start | bytes 196612
  43.3 6.3 %collective-permute-start.6 = (f32[2,2,2048]{2,1,0:T(2,128)S(1)}, f32[2,2,2048]{2,1,0:T(2,128)S(1)}, u32[]{:S(2)}, u32[]{:S(2)}) collective-permute-start(f32[2,2,2048]{2,1,0:T(2,128)S(1)} %get-tuple-element.21), channel_id=1, source_target_pairs={{0,1},{1,0},{2,3},{3,2},{4,5},{5,4},{6,7},{7,6},{8,9},{9,8},{10,11... | collective-permute-start | bytes 98312 | tf_op jit(solution)/shard_map/ppermute | solution.py:717
  49.7 4.7 %collective-permute-start.7 = (f32[2,2,2048]{2,1,0:T(2,128)S(1)}, f32[2,2,2048]{2,1,0:T(2,128)S(1)}, u32[]{:S(2)}, u32[]{:S(2)}) collective-permute-start(f32[2,2,2048]{2,1,0:T(2,128)S(1)} %pad_maximum_fusion), channel_id=1, source_target_pairs={{0,2},{1,3},{2,0},{3,1},{4,6},{5,7},{6,4},{7,5},{8,10},{9,11},{10,... | collective-permute-start | bytes 98312 | tf_op jit(solution)/shard_map/ppermute | solution.py:717
  54.4 4.0 %collective-permute-start.8 = (f32[2,2,2048]{2,1,0:T(2,128)S(1)}, f32[2,2,2048]{2,1,0:T(2,128)S(1)}, u32[]{:S(2)}, u32[]{:S(2)}) collective-permute-start(f32[2,2,2048]{2,1,0:T(2,128)S(1)} %pad_maximum_fusion.1), channel_id=1, source_target_pairs={{0,4},{1,5},{2,6},{3,7},{4,0},{5,1},{6,2},{7,3},{8,12},{9,13},{10,... | collective-permute-start | bytes 98312 | tf_op jit(solution)/shard_map/ppermute | solution.py:717
  58.5 5.8 %collective-permute-start.9 = (f32[2,2,2048]{2,1,0:T(2,128)S(1)}, f32[2,2,2048]{2,1,0:T(2,128)S(1)}, u32[]{:S(2)}, u32[]{:S(2)}) collective-permute-start(f32[2,2,2048]{2,1,0:T(2,128)S(1)} %pad_maximum_fusion.2), channel_id=1, source_target_pairs={{0,8},{1,9},{2,10},{3,11},{4,12},{5,13},{6,14},{7,15},{8,0},{9,1},... | collective-permute-start | bytes 98312 | tf_op jit(solution)/shard_map/ppermute | solution.py:717
